TPU v7x, 32 devices: a whole 2x2x4 slice. The times are simulated.
32 devices in a mesh: samp: 8 (over y, x, core), var: 4 (over z).
Axes of the slice: x: 2, y: 2, z: 4, core: 2. Of those that a mesh axis runs over, the one named last changes fastest.
Arguments:
- genotypes: int32 [8192, 4096], P('samp', 'var'), may hold values from 0 to 2
- observed: int32 [8192, 4096], P('samp', 'var'), may hold values from 0 to 1, as said below
- proportions: float32 [10, 8192], P(None, 'samp'), may hold values from 0 to 1, as said below
- frequencies: float32 [10, 4096], P(None, ('samp', 'var')), may hold values from 0.02 to 0.98
Outputs:
- mixture: float32 [10, 8192], P(None, 'samp')
- alleles: float32 [10, 4096], P(None, 'var')
Inputs may be any that keep to these rules, and one draw needn't show every extreme that they name: Every sample is observed at 256 or more variants and every variant at 512 or more samples. Each sample's 10 proportions are positive and sum to one.
All inputs are finite; a program needn't handle non-finite values.
Results may differ from a plain program's by a relative error of at most 0.0003.
Values sent between devices are 32-bit elements; how exact they have to be, the bound alone decides.
No kernel may reach another device: no remote copies, remote signals or barrier semaphores. Data moves between devices by JAX's collectives and lax.ppermute only.
A program may use at most 128 MiB of HBM per device.

v0:
```python
import functools

import jax
import jax.numpy as jnp
from jax import lax
from jax.experimental import pallas as pl
from jax.experimental.pallas import tpu as pltpu
from jax.sharding import PartitionSpec as P

STEPS = 2
CLIP_LOW = 1e-05
NORM_EPS = 1e-10
F32 = jnp.float32
BF16 = jnp.bfloat16
SUBLANES = 8
LANES = 128
VMEM_BYTES = 40 * 2**20


def clip_unit(values):
    return jnp.clip(values, CLIP_LOW, 1.0 - CLIP_LOW)


def blocks_of(size, largest):
    width = min(size, largest)
    while size % width:
        width -= 1
    return width


def swap(value, axis, mask):
    size = lax.axis_size(axis)
    return lax.ppermute(value, axis, [(i, i ^ mask) for i in range(size)])


def last_parts(value, axis):
    size, stride = lax.axis_size(axis), 1
    while 2 * stride < size:
        value = value + swap(value, axis, stride)
        stride *= 2
    return value, swap(value, axis, stride)


def gather_frequencies(frequencies):
    samp_count, var_count = lax.axis_size("samp"), lax.axis_size("var")
    group = samp_count // var_count
    samp, var = lax.axis_index("samp"), lax.axis_index("var")
    owner = samp // group
    both = ("samp", "var")
    arrived = [jnp.where(owner == var, frequencies, 0.0)]
    for mask in range(1, var_count):
        pairs = [
            (s * var_count + ((s // group) ^ mask), s * var_count + s // group)
            for s in range(samp_count)
        ]
        arrived.append(lax.ppermute(frequencies, both, pairs))
    stride = 1
    while stride < var_count:
        flip = (var & stride) != 0
        arrived = [jnp.where(flip, arrived[i ^ stride], arrived[i]) for i in range(var_count)]
        stride *= 2
    held = jnp.concatenate(arrived, axis=1)
    stride = 1
    while stride < group:
        other = swap(held, "samp", stride)
        upper = (samp & stride) != 0
        held = jnp.concatenate(
            [jnp.where(upper, other, held), jnp.where(upper, held, other)], axis=1
        )
        stride *= 2
    held = jnp.where(owner == var, held, 0.0)
    total = held
    for mask in range(1, var_count):
        pairs = [
            ((v * group + g) * var_count + v, ((v ^ mask) * group + g) * var_count + v)
            for v in range(var_count)
            for g in range(group)
        ]
        total = total + lax.ppermute(held, both, pairs)
    return total


def dot(left, right, left_dim, right_dim):
    return lax.dot_general(
        left, right, (((left_dim,), (right_dim,)), ((), ())), preferred_element_type=F32
    )


def split(values):
    high = values.astype(BF16)
    rest = values - high.astype(F32)
    middle = rest.astype(BF16)
    return high, middle, (rest - middle.astype(F32)).astype(BF16)


def ratio(counts, denominator):
    inverse = pl.reciprocal(denominator, approx=True)
    high = inverse.astype(BF16)
    low = (inverse - high.astype(F32)).astype(BF16)
    return counts * high, counts * low


def row_mask(values, populations):
    rows = lax.broadcasted_iota(jnp.int32, values.shape, 0)
    return jnp.where(rows < populations, values, 0.0)


def pad_rows(values, rows):
    spare = jnp.zeros((rows - values.shape[0], values.shape[1]), values.dtype)
    return jnp.concatenate([values, spare], axis=0)


def put_packed(ref, first, stride, values):
    count = values.shape[0]
    for block in range(values.shape[1] // LANES):
        top = block * stride + first
        ref[top : top + count, :] = values[:, block * LANES : (block + 1) * LANES]


def sum_packed(parts, first, stride, count):
    one, other = parts
    pieces = []
    for top in range(first, one.shape[0], stride):
        here = slice(top, top + count)
        pieces.append(one[here, :] + other[here, :])
    return jnp.concatenate(pieces, axis=1)


def expectation(populations, mixture, alleles, alt_ref, ref_ref, prop_ref, both_ref, turned, counts=None):
    rows, samples = mixture.shape
    variants = alleles.shape[1]
    tall, wide = blocks_of(samples, 1024), blocks_of(variants, 512)
    mix_high, mix_mid, mix_low = split(mixture)
    all_high, all_mid, all_low = split(alleles)
    away_high, away_mid, _ = split(row_mask(1.0 - alleles, populations))
    turned[...] = jnp.concatenate(
        [mix_high, mix_high, mix_mid, mix_mid, mix_high, mix_low], axis=0
    ).T
    right = jnp.concatenate([all_high, all_mid, all_high, all_mid, all_low, all_high], axis=0)
    toward = jnp.concatenate([all_high, all_mid], axis=0)
    away = jnp.concatenate([away_high, away_mid], axis=0)
    left = jnp.concatenate([mix_high, mix_mid], axis=0)
    column_starts = range(0, variants, wide)
    alt_total = [jnp.zeros((2 * rows, wide), F32) for _ in column_starts]
    ref_total = [jnp.zeros((2 * rows, wide), F32) for _ in column_starts]
    props = []
    for top in range(0, samples, tall):
        here = slice(top, top + tall)
        prop = jnp.zeros((2 * rows, tall), F32)
        for index, start in enumerate(column_starts):
            across = slice(start, start + wide)
            expected = dot(turned[here, :], right[:, across], 1, 0)
            alt_high, alt_low = ratio(alt_ref[here, across], expected)
            ref_high, ref_low = ratio(ref_ref[here, across], 1.0 - expected)
            prop = (
                prop
                + dot(toward[:, across], alt_high, 1, 1)
                + dot(toward[:, across], alt_low, 1, 1)
                + dot(away[:, across], ref_high, 1, 1)
                + dot(away[:, across], ref_low, 1, 1)
            )
            weights = left[:, here]
            alt_total[index] = (
                alt_total[index] + dot(weights, alt_high, 1, 0) + dot(weights, alt_low, 1, 0)
            )
            ref_total[index] = (
                ref_total[index] + dot(weights, ref_high, 1, 0) + dot(weights, ref_low, 1, 0)
            )
        props.append(prop[:populations] + prop[rows : rows + populations])
    stride = prop_ref.shape[0] * LANES // samples
    put_packed(prop_ref, 0, stride, jnp.concatenate(props, axis=1))
    if counts is not None:
        put_packed(prop_ref, populations, stride, counts)
    for place, totals in enumerate((alt_total, ref_total)):
        sums = jnp.concatenate(totals, axis=1)
        sums = sums[:populations] + sums[rows : rows + populations]
        put_packed(both_ref, place * populations, 2 * populations, sums)


def update(populations, mixture, alleles, twice_observed, prop_parts, both_parts):
    rows, samples = mixture.shape
    stride = prop_parts[0].shape[0] * LANES // samples
    prop_sums = sum_packed(prop_parts, 0, stride, populations)
    if twice_observed is None:
        twice_observed = sum_packed(prop_parts, populations, stride, 1)
    alt_sums = sum_packed(both_parts, 0, 2 * populations, populations)
    ref_sums = sum_packed(both_parts, populations, 2 * populations, populations)
    next_mixture = clip_unit(mixture[:populations] * prop_sums / twice_observed)
    current = alleles[:populations]
    weighted = current * alt_sums
    next_alleles = clip_unit(weighted / (weighted + (1.0 - current) * ref_sums))
    return pad_rows(next_mixture, rows), pad_rows(next_alleles, rows), twice_observed


def prepare_kernel(genotypes, observed, alt_out, ref_out, count_out, landed, arrivals):
    samples, variants = genotypes.shape
    tall = blocks_of(samples, 128)
    copies = []
    for index, top in enumerate(range(0, samples, tall)):
        here = pl.ds(top, tall)
        for place, source in enumerate((genotypes, observed)):
            copy = pltpu.make_async_copy(
                source.at[here, :], landed.at[place, here, :], arrivals.at[place, index]
            )
            copy.start()
            copies.append(copy)
    ones = jnp.ones((SUBLANES, variants), BF16)
    for index, top in enumerate(range(0, samples, tall)):
        here = slice(top, top + tall)
        copies[2 * index].wait()
        copies[2 * index + 1].wait()
        seen = landed[1, here, :]
        alt = seen * landed[0, here, :]
        alt_out[here, :] = alt.astype(F32).astype(BF16)
        ref_out[here, :] = (2 * seen - alt).astype(F32).astype(BF16)
        count_out[:, here] = 2.0 * dot(ones, seen.astype(F32).astype(BF16), 1, 1)


def first_kernel(
    mixture, alleles, counts, alt, ref, mixture_out, alleles_out, prop_out, both_out, turned
):
    populations = mixture.shape[0]
    rows = mixture_out.shape[0]
    mix = pad_rows(mixture[...], rows)
    current = pad_rows(alleles[...], rows)
    mixture_out[...] = mix
    alleles_out[...] = current
    expectation(
        populations, mix, current, alt, ref, prop_out, both_out, turned, counts[:1, :]
    )


def step_kernel(populations, with_twice, *refs):
    mixture, alleles = refs[:2]
    twice = refs[2][...] if with_twice else None
    prop_parts, both_parts, (alt, ref), outs = split_refs(refs[2 + with_twice :], 2, 2, 2)
    mix, current, twice = update(
        populations, mixture[...], alleles[...], twice, prop_parts, both_parts
    )
    outs[0][...] = mix
    outs[1][...] = current
    if not with_twice:
        outs[4][...] = twice
    expectation(populations, mix, current, alt, ref, outs[2], outs[3], outs[-1])


def split_refs(refs, *counts):
    groups = []
    for count in counts:
        groups.append(refs[:count])
        refs = refs[count:]
    return (*groups, refs)


def folded(values):
    squares = values * values
    tile = squares.reshape(-1, SUBLANES, squares.shape[1]).sum(axis=0)
    width = tile.shape[1]
    return sum(tile[:, i : i + LANES] for i in range(0, width, LANES))


def square_kernel(populations, *refs):
    mix_zero, all_zero, mix_one, all_one, twice = refs[:5]
    prop_parts, both_parts, (mix_out, all_out, mix_tile, all_tile) = split_refs(refs[5:], 2, 2)
    mix_two, all_two, _ = update(
        populations, mix_one[...], all_one[...], twice[...], prop_parts, both_parts
    )
    mix_out[...] = mix_two
    all_out[...] = all_two
    for zero, one, two, tile in (
        (mix_zero[...], mix_one[...], mix_two, mix_tile),
        (all_zero[...], all_one[...], all_two, all_tile),
    ):
        step = one - zero
        tile[:SUBLANES, :] = folded(step)
        tile[SUBLANES:, :] = folded(two - one - step)


def leap(zero, one, two, tile):
    first = jnp.sum(tile[:SUBLANES], axis=(0, 1), keepdims=True)
    second = jnp.sum(tile[SUBLANES:], axis=(0, 1), keepdims=True)
    alpha = jnp.maximum(1.0, jnp.sqrt(first / (second + NORM_EPS)))
    step = one - zero
    curve = two - one - step
    return zero + 2.0 * alpha * step + alpha * alpha * curve


def leap_kernel(populations, *refs):
    states = [ref[...] for ref in refs[:6]]
    mix_zero, all_zero, mix_one, all_one, mix_two, all_two = states
    mix_parts, all_parts, rest = split_refs(refs[6:], 2, 2)
    alt, ref, mixture_out, alleles_out, prop_out, both_out, turned = rest
    mix_tile = mix_parts[0][...] + mix_parts[1][...]
    all_tile = all_parts[0][...] + all_parts[1][...]
    clipped = row_mask(clip_unit(leap(mix_zero, mix_one, mix_two, mix_tile)), populations)
    mix = clipped / jnp.sum(clipped, axis=0, keepdims=True)
    current = row_mask(clip_unit(leap(all_zero, all_one, all_two, all_tile)), populations)
    mixture_out[...] = mix
    alleles_out[...] = current
    expectation(populations, mix, current, alt, ref, prop_out, both_out, turned)


def final_kernel(populations, mixture, alleles, twice, *refs):
    prop_parts, both_parts, (mixture_out, alleles_out) = split_refs(refs, 2, 2)
    mix, current, _ = update(
        populations, mixture[...], alleles[...], twice[...], prop_parts, both_parts
    )
    mixture_out[...] = mix[:populations]
    alleles_out[...] = current[:populations]


def call(kernel, name, outs, args, scratch=(), space=pltpu.VMEM):
    whole = pl.BlockSpec(memory_space=pltpu.VMEM)
    return pl.pallas_call(
        kernel,
        out_shape=tuple(jax.ShapeDtypeStruct(*out) for out in outs),
        in_specs=[pl.BlockSpec(memory_space=space)] * len(args),
        out_specs=(whole,) * len(outs),
        scratch_shapes=list(scratch),
        compiler_params=pltpu.CompilerParams(vmem_limit_bytes=VMEM_BYTES),
        name=name,
    )(*args)


def local(genotypes, observed, proportions, frequencies):
    populations, samples = proportions.shape
    variants = genotypes.shape[1]
    rows = -(-populations // 16) * 16
    state_out = (((rows, samples), F32), ((rows, variants), F32))
    packed = populations * samples // LANES
    both_out = ((2 * populations * variants // LANES, LANES), F32)
    sums_out = (((packed, LANES), F32), both_out)
    first_sums_out = (((packed + samples // LANES, LANES), F32), both_out)
    tile_out = ((2 * SUBLANES, LANES), F32)
    turned = (pltpu.VMEM((samples, 6 * rows), BF16),)
    table_out = ((samples, variants), BF16)
    chunks = samples // blocks_of(samples, 128)

    alleles = gather_frequencies(frequencies)
    alt, ref, counts = call(
        prepare_kernel,
        "prepare",
        (table_out, table_out, ((SUBLANES, samples), F32)),
        (genotypes, observed),
        (
            pltpu.VMEM((2, samples, variants), jnp.int32),
            pltpu.SemaphoreType.DMA((2, chunks)),
        ),
        pl.ANY,
    )

    def exchanged(prop, both):
        return (*last_parts(prop, "var"), *last_parts(both, "samp"))

    mix_zero, all_zero, prop, both = call(
        first_kernel,
        "first",
        (*state_out, *first_sums_out),
        (proportions, alleles, counts, alt, ref),
        turned,
    )
    twice = None
    for repeat in range(STEPS):
        if repeat:
            mix_zero, all_zero, prop, both = call(
                functools.partial(step_kernel, populations, 1),
                "step",
                (*state_out, *sums_out),
                (mix_zero, all_zero, twice, *exchanged(prop, both), alt, ref),
                turned,
            )
        known = () if twice is None else (twice,)
        extra = () if known else (((1, samples), F32),)
        mix_one, all_one, prop, both, *found = call(
            functools.partial(step_kernel, populations, len(known)),
            "step",
            (*state_out, *sums_out, *extra),
            (mix_zero, all_zero, *known, *exchanged(prop, both), alt, ref),
            turned,
        )
        (twice,) = known or found
        mix_two, all_two, mix_tile, all_tile = call(
            functools.partial(square_kernel, populations),
            "square",
            (*state_out, tile_out, tile_out),
            (mix_zero, all_zero, mix_one, all_one, twice, *exchanged(prop, both)),
        )
        tiles = (*last_parts(mix_tile, "samp"), *last_parts(all_tile, "var"))
        mix_zero, all_zero, prop, both = call(
            functools.partial(leap_kernel, populations),
            "leap",
            (*state_out, *sums_out),
            (mix_zero, all_zero, mix_one, all_one, mix_two, all_two, *tiles, alt, ref),
            turned,
        )
    return call(
        functools.partial(final_kernel, populations),
        "final",
        (((populations, samples), F32), ((populations, variants), F32)),
        (mix_zero, all_zero, twice, *exchanged(prop, both)),
    )


def solution(mesh):
    placed = (P("samp", "var"), P("samp", "var"), P(None, "samp"), P(None, ("samp", "var")))
    return jax.shard_map(
        local,
        mesh=mesh,
        in_specs=placed,
        out_specs=(P(None, "samp"), P(None, "var")),
        check_vma=False,
    )
```

profile of v0, /device:TPU:0, one launch (start us, length us, event | category | flops | bytes accessed | tf_op | source)
XLA Modules:
  0.0 143.0 jit_solution(1879876354919201314)
XLA Ops:
  4.5 3.2 %collective-permute-done.1 = f32[10,128]{1,0:T(8,128)S(1)} collective-permute-done((f32[10,128]{1,0:T(8,128)}, f32[10,128]{1,0:T(8,128)S(1)}, u32[]{:S(2)}, u32[]{:S(2)}) %collective-permute-start.1) | collective-permute-done | bytes 5152 | tf_op jit(solution)/shard_map/ppermute | solution.py:56
  11.5 4.6 %collective-permute-start.6 = (f32[10,1024]{1,0:T(8,128)S(1)}, f32[10,1024]{1,0:T(8,128)S(1)}, u32[]{:S(2)}, u32[]{:S(2)}) collective-permute-start(f32[10,1024]{1,0:T(8,128)S(1)} %maximum_select_fusion), channel_id=1, source_target_pairs={{0,24},{4,28},{9,17},{13,21},{18,10},{22,14},{27,3},{31,7}} | collective-permute-start | bytes 122888 | tf_op jit(solution)/shard_map/ppermute | solution.py:79
  18.8 2.2 %copy-done = s32[1024,1024]{1,0:T(8,128)S(1)} copy-done((s32[1024,1024]{1,0:T(8,128)S(1)}, s32[1024,1024]{1,0:T(8,128)}, u32[]{:S(2)}) %copy-start) | copy-done | bytes 4194328
  21.0 2.2 %copy-done.1 = s32[1024,1024]{1,0:T(8,128)S(1)} copy-done((s32[1024,1024]{1,0:T(8,128)S(1)}, s32[1024,1024]{1,0:T(8,128)}, u32[]{:S(2)}) %copy-start.1) | copy-done | bytes 4194328
  23.1 2.8 %prepare.1 = (bf16[1024,1024]{1,0:T(8,128)(2,1)S(1)}, bf16[1024,1024]{1,0:T(8,128)(2,1)S(1)}, f32[8,1024]{1,0:T(8,128)S(1)}) custom-call(s32[1024,1024]{1,0:T(8,128)S(1)} %copy-done, s32[1024,1024]{1,0:T(8,128)S(1)} %copy-done.1), custom_call_target="tpu_custom_call" | custom-call | tf_op jit(solution)/shard_map/prepare/pallas_call | solution.py:314
  26.0 4.2 %first.1 = (f32[16,1024]{1,0:T(8,128)S(1)}, f32[16,1024]{1,0:T(8,128)S(1)}, f32[88,128]{1,0:T(8,128)S(1)}, f32[160,128]{1,0:T(8,128)S(1)}) custom-call(f32[10,1024]{1,0:T(8,128)S(1)} %copy-done.2, f32[10,1024]{1,0:T(8,128)S(1)} %add_add_fusion.alleles, f32[8,1024]{1,0:T(8,128)S(1)} %get-tuple-element.38.counts, ...), custom_call_target="tpu_custom_call" | custom-call | tf_op jit(solution)/shard_map/first/pallas_call | solution.py:314
  32.2 3.8 %collective-permute-done.10 = f32[160,128]{1,0:T(8,128)S(1)} collective-permute-done((f32[160,128]{1,0:T(8,128)S(1)}, f32[160,128]{1,0:T(8,128)S(1)}, u32[]{:S(2)}, u32[]{:S(2)}) %collective-permute-start.10) | collective-permute-done | bytes 81952 | tf_op jit(solution)/shard_map/ppermute | solution.py:33
  38.0 3.7 %collective-permute-done.8.refs_3_ = f32[88,128]{1,0:T(8,128)S(1)} collective-permute-done((f32[88,128]{1,0:T(8,128)S(1)}, f32[88,128]{1,0:T(8,128)S(1)}, u32[]{:S(2)}, u32[]{:S(2)}) %collective-permute-start.8) | collective-permute-done | bytes 45088 | tf_op jit(solution)/shard_map/ppermute | solution.py:33
  41.7 4.3 %step.3 = (f32[16,1024]{1,0:T(8,128)S(1)}, f32[16,1024]{1,0:T(8,128)S(1)}, f32[80,128]{1,0:T(8,128)S(1)}, f32[160,128]{1,0:T(8,128)S(1)}, f32[1,1024]{1,0:T(1,128)S(1)}) custom-call(f32[16,1024]{1,0:T(8,128)S(1)} %get-tuple-element.41.refs_0_, f32[16,1024]{1,0:T(8,128)S(1)} %get-tuple-element.42.refs_1_, f32[88,128]{1,0:T(8,128)S(1)} %add.85.refs_2_, ...), custom_call_target="tpu_custom_call" | custom-call | tf_op jit(solution)/shard_map/step/pallas_call | solution.py:314
  49.3 2.5 %collective-permute-done.15 = f32[160,128]{1,0:T(8,128)S(1)} collective-permute-done((f32[160,128]{1,0:T(8,128)S(1)}, f32[160,128]{1,0:T(8,128)S(1)}, u32[]{:S(2)}, u32[]{:S(2)}) %collective-permute-start.15) | collective-permute-done | bytes 81952 | tf_op jit(solution)/shard_map/ppermute | solution.py:33
  54.2 4.2 %collective-permute-done.13.refs_6_ = f32[80,128]{1,0:T(8,128)S(1)} collective-permute-done((f32[80,128]{1,0:T(8,128)S(1)}, f32[80,128]{1,0:T(8,128)S(1)}, u32[]{:S(2)}, u32[]{:S(2)}) %collective-permute-start.13) | collective-permute-done | bytes 40992 | tf_op jit(solution)/shard_map/ppermute | solution.py:33
  64.1 2.8 %collective-permute-done.21.refs_9_ = f32[16,128]{1,0:T(8,128)S(1)} collective-permute-done((f32[16,128]{1,0:T(8,128)S(1)}, f32[16,128]{1,0:T(8,128)S(1)}, u32[]{:S(2)}, u32[]{:S(2)}) %collective-permute-start.21) | collective-permute-done | bytes 8224 | tf_op jit(solution)/shard_map/ppermute | solution.py:33
  67.1 4.6 %leap.2 = (f32[16,1024]{1,0:T(8,128)S(1)}, f32[16,1024]{1,0:T(8,128)S(1)}, f32[80,128]{1,0:T(8,128)S(1)}, f32[160,128]{1,0:T(8,128)S(1)}) custom-call(f32[16,1024]{1,0:T(8,128)S(1)} %get-tuple-element.41.refs_0_, f32[16,1024]{1,0:T(8,128)S(1)} %get-tuple-element.42.refs_1_, f32[16,1024]{1,0:T(8,128)S(1)} %get-tuple-element.45.refs_2_, ...), custom_call_target="tpu_custom_call" | custom-call | tf_op jit(solution)/shard_map/leap/pallas_call | solution.py:314
  75.3 2.3 %collective-permute-done.25 = f32[160,128]{1,0:T(8,128)S(1)} collective-permute-done((f32[160,128]{1,0:T(8,128)S(1)}, f32[160,128]{1,0:T(8,128)S(1)}, u32[]{:S(2)}, u32[]{:S(2)}) %collective-permute-start.25) | collective-permute-done | bytes 81952 | tf_op jit(solution)/shard_map/ppermute | solution.py:33
  80.3 3.0 %collective-permute-done.23.refs_4_ = f32[80,128]{1,0:T(8,128)S(1)} collective-permute-done((f32[80,128]{1,0:T(8,128)S(1)}, f32[80,128]{1,0:T(8,128)S(1)}, u32[]{:S(2)}, u32[]{:S(2)}) %collective-permute-start.23) | collective-permute-done | bytes 40992 | tf_op jit(solution)/shard_map/ppermute | solution.py:33
  83.3 4.3 %step.4 = (f32[16,1024]{1,0:T(8,128)S(1)}, f32[16,1024]{1,0:T(8,128)S(1)}, f32[80,128]{1,0:T(8,128)S(1)}, f32[160,128]{1,0:T(8,128)S(1)}) custom-call(f32[16,1024]{1,0:T(8,128)S(1)} %get-tuple-element.54.refs_0_, f32[16,1024]{1,0:T(8,128)S(1)} %get-tuple-element.55.refs_1_, f32[1,1024]{1,0:T(1,128)S(1)} %get-tuple-element.47.refs_4_.refs_2_.twice, ...), custom_call_target="tpu_custom_call" | custom-call | tf_op jit(solution)/shard_map/step/pallas_call | solution.py:314
  96.8 3.1 %collective-permute-done.28.refs_4_ = f32[80,128]{1,0:T(8,128)S(1)} collective-permute-done((f32[80,128]{1,0:T(8,128)S(1)}, f32[80,128]{1,0:T(8,128)S(1)}, u32[]{:S(2)}, u32[]{:S(2)}) %collective-permute-start.28) | collective-permute-done | bytes 40992 | tf_op jit(solution)/shard_map/ppermute | solution.py:33
  99.9 4.3 %step.5 = (f32[16,1024]{1,0:T(8,128)S(1)}, f32[16,1024]{1,0:T(8,128)S(1)}, f32[80,128]{1,0:T(8,128)S(1)}, f32[160,128]{1,0:T(8,128)S(1)}) custom-call(f32[16,1024]{1,0:T(8,128)S(1)} %get-tuple-element.58.refs_0_, f32[16,1024]{1,0:T(8,128)S(1)} %get-tuple-element.59.refs_1_, f32[1,1024]{1,0:T(1,128)S(1)} %get-tuple-element.47.refs_4_.refs_2_.twice, ...), custom_call_target="tpu_custom_call" | custom-call | tf_op jit(solution)/shard_map/step/pallas_call | solution.py:314
  107.7 2.3 %collective-permute-done.35 = f32[160,128]{1,0:T(8,128)S(1)} collective-permute-done((f32[160,128]{1,0:T(8,128)S(1)}, f32[160,128]{1,0:T(8,128)S(1)}, u32[]{:S(2)}, u32[]{:S(2)}) %collective-permute-start.35) | collective-permute-done | bytes 81952 | tf_op jit(solution)/shard_map/ppermute | solution.py:33
  110.8 2.1 %collective-permute-start.33 = (f32[80,128]{1,0:T(8,128)S(1)}, f32[80,128]{1,0:T(8,128)S(1)}, u32[]{:S(2)}, u32[]{:S(2)}) collective-permute-start(f32[80,128]{1,0:T(8,128)S(1)} %add.100.refs_5_), channel_id=1, source_target_pairs={{0,2},{1,3},{2,0},{3,1},{4,6},{5,7},{6,4},{7,5},{8,10},{9,11},{10,... | collective-permute-start | bytes 122888 | tf_op jit(solution)/shard_map/ppermute | solution.py:33
  112.9 2.9 %collective-permute-done.33.refs_6_ = f32[80,128]{1,0:T(8,128)S(1)} collective-permute-done((f32[80,128]{1,0:T(8,128)S(1)}, f32[80,128]{1,0:T(8,128)S(1)}, u32[]{:S(2)}, u32[]{:S(2)}) %collective-permute-start.33) | collective-permute-done | bytes 40992 | tf_op jit(solution)/shard_map/ppermute | solution.py:33
  119.6 2.0 %collective-permute-start.41 = (f32[16,128]{1,0:T(8,128)S(1)}, f32[16,128]{1,0:T(8,128)S(1)}, u32[]{:S(2)}, u32[]{:S(2)}) collective-permute-start(f32[16,128]{1,0:T(8,128)S(1)} %add.105.refs_8_), channel_id=1, source_target_pairs={{0,2},{1,3},{2,0},{3,1},{4,6},{5,7},{6,4},{7,5},{8,10},{9,11},{10,... | collective-permute-start | bytes 24584 | tf_op jit(solution)/shard_map/ppermute | solution.py:33
  125.3 4.4 %leap.3 = (f32[16,1024]{1,0:T(8,128)S(1)}, f32[16,1024]{1,0:T(8,128)S(1)}, f32[80,128]{1,0:T(8,128)S(1)}, f32[160,128]{1,0:T(8,128)S(1)}) custom-call(f32[16,1024]{1,0:T(8,128)S(1)} %get-tuple-element.58.refs_0_, f32[16,1024]{1,0:T(8,128)S(1)} %get-tuple-element.59.refs_1_, f32[16,1024]{1,0:T(8,128)S(1)} %get-tuple-element.62.refs_2_, ...), custom_call_target="tpu_custom_call" | custom-call | tf_op jit(solution)/shard_map/leap/pallas_call | solution.py:314
  138.1 4.2 %collective-permute-done.43.refs_1_ = f32[80,128]{1,0:T(8,128)S(1)} collective-permute-done((f32[80,128]{1,0:T(8,128)S(1)}, f32[80,128]{1,0:T(8,128)S(1)}, u32[]{:S(2)}, u32[]{:S(2)}) %collective-permute-start.43) | collective-permute-done | bytes 40992 | tf_op jit(solution)/shard_map/ppermute | solution.py:33
  (115 shorter events, 61.9 us)
Async XLA Ops:
  0.6 7.2 %collective-permute-start.1 = (f32[10,128]{1,0:T(8,128)}, f32[10,128]{1,0:T(8,128)S(1)}, u32[]{:S(2)}, u32[]{:S(2)}) collective-permute-start(f32[10,128]{1,0:T(8,128)} %param.7), channel_id=1, source_target_pairs={{2,0},{6,4},{11,9},{15,13},{16,18},{20,22},{25,27},{29,31}} | collective-permute-start | bytes 15368 | tf_op jit(solution)/shard_map/ppermute | solution.py:56
  1.9 7.6 %collective-permute-start = (f32[10,128]{1,0:T(8,128)}, f32[10,128]{1,0:T(8,128)S(1)}, u32[]{:S(2)}, u32[]{:S(2)}) collective-permute-start(f32[10,128]{1,0:T(8,128)} %param.7), channel_id=1, source_target_pairs={{3,0},{7,4},{10,9},{14,13},{17,18},{21,22},{24,27},{28,31}} | collective-permute-start | bytes 15368 | tf_op jit(solution)/shard_map/ppermute | solution.py:56
  3.2 6.3 %collective-permute-start.2 = (f32[10,128]{1,0:T(8,128)}, f32[10,128]{1,0:T(8,128)S(1)}, u32[]{:S(2)}, u32[]{:S(2)}) collective-permute-start(f32[10,128]{1,0:T(8,128)} %param.7), channel_id=1, source_target_pairs={{1,0},{5,4},{8,9},{12,13},{19,18},{23,22},{26,27},{30,31}} | collective-permute-start | bytes 15368 | tf_op jit(solution)/shard_map/ppermute | solution.py:56
  11.5 14.4 %collective-permute-start.6 = (f32[10,1024]{1,0:T(8,128)S(1)}, f32[10,1024]{1,0:T(8,128)S(1)}, u32[]{:S(2)}, u32[]{:S(2)}) collective-permute-start(f32[10,1024]{1,0:T(8,128)S(1)} %maximum_select_fusion), channel_id=1, source_target_pairs={{0,24},{4,28},{9,17},{13,21},{18,10},{22,14},{27,3},{31,7}} | collective-permute-start | bytes 122888 | tf_op jit(solution)/shard_map/ppermute | solution.py:79
  16.2 9.8 %collective-permute-start.5 = (f32[10,1024]{1,0:T(8,128)S(1)}, f32[10,1024]{1,0:T(8,128)S(1)}, u32[]{:S(2)}, u32[]{:S(2)}) collective-permute-start(f32[10,1024]{1,0:T(8,128)S(1)} %maximum_select_fusion), channel_id=1, source_target_pairs={{0,16},{4,20},{9,25},{13,29},{18,2},{22,6},{27,11},{31,15}} | collective-permute-start | bytes 122888 | tf_op jit(solution)/shard_map/ppermute | solution.py:79
  17.5 8.5 %collective-permute-start.4 = (f32[10,1024]{1,0:T(8,128)S(1)}, f32[10,1024]{1,0:T(8,128)S(1)}, u32[]{:S(2)}, u32[]{:S(2)}) collective-permute-start(f32[10,1024]{1,0:T(8,128)S(1)} %maximum_select_fusion), channel_id=1, source_target_pairs={{0,8},{4,12},{9,1},{13,5},{18,26},{22,30},{27,19},{31,23}} | collective-permute-start | bytes 122888 | tf_op jit(solution)/shard_map/ppermute | solution.py:79
  31.5 4.6 %collective-permute-start.10 = (f32[160,128]{1,0:T(8,128)S(1)}, f32[160,128]{1,0:T(8,128)S(1)}, u32[]{:S(2)}, u32[]{:S(2)}) collective-permute-start(f32[160,128]{1,0:T(8,128)S(1)} %add.86), channel_id=1, source_target_pairs={{0,8},{4,12},{8,0},{12,4},{16,24},{20,28},{24,16},{28,20},{1,9},{5... | collective-permute-start | bytes 245768 | tf_op jit(solution)/shard_map/ppermute | solution.py:33
  31.6 4.6 %collective-permute-start.7 = (f32[88,128]{1,0:T(8,128)S(1)}, f32[88,128]{1,0:T(8,128)S(1)}, u32[]{:S(2)}, u32[]{:S(2)}) collective-permute-start(f32[88,128]{1,0:T(8,128)S(1)} %get-tuple-element.43), channel_id=1, source_target_pairs={{0,1},{1,0},{2,3},{3,2},{4,5},{5,4},{6,7},{7,6},{8,9},{9,8},{10,11... | collective-permute-start | bytes 135176 | tf_op jit(solution)/shard_map/ppermute | solution.py:33
  36.1 5.6 %collective-permute-start.11 = (f32[160,128]{1,0:T(8,128)S(1)}, f32[160,128]{1,0:T(8,128)S(1)}, u32[]{:S(2)}, u32[]{:S(2)}) collective-permute-start(f32[160,128]{1,0:T(8,128)S(1)} %add.87.refs_4_), channel_id=1, source_target_pairs={{0,16},{4,20},{8,24},{12,28},{16,0},{20,4},{24,8},{28,12},{1,17},{... | collective-permute-start | bytes 245768 | tf_op jit(solution)/shard_map/ppermute | solution.py:33
  36.2 5.5 %collective-permute-start.8 = (f32[88,128]{1,0:T(8,128)S(1)}, f32[88,128]{1,0:T(8,128)S(1)}, u32[]{:S(2)}, u32[]{:S(2)}) collective-permute-start(f32[88,128]{1,0:T(8,128)S(1)} %add.85.refs_2_), channel_id=1, source_target_pairs={{0,2},{1,3},{2,0},{3,1},{4,6},{5,7},{6,4},{7,5},{8,10},{9,11},{10,... | collective-permute-start | bytes 135176 | tf_op jit(solution)/shard_map/ppermute | solution.py:33
  47.3 4.6 %collective-permute-start.15 = (f32[160,128]{1,0:T(8,128)S(1)}, f32[160,128]{1,0:T(8,128)S(1)}, u32[]{:S(2)}, u32[]{:S(2)}) collective-permute-start(f32[160,128]{1,0:T(8,128)S(1)} %add.89), channel_id=1, source_target_pairs={{0,8},{4,12},{8,0},{12,4},{16,24},{20,28},{24,16},{28,20},{1,9},{5... | collective-permute-start | bytes 245768 | tf_op jit(solution)/shard_map/ppermute | solution.py:33
  48.8 4.7 %collective-permute-start.12 = (f32[80,128]{1,0:T(8,128)S(1)}, f32[80,128]{1,0:T(8,128)S(1)}, u32[]{:S(2)}, u32[]{:S(2)}) collective-permute-start(f32[80,128]{1,0:T(8,128)S(1)} %get-tuple-element.48), channel_id=1, source_target_pairs={{0,1},{1,0},{2,3},{3,2},{4,5},{5,4},{6,7},{7,6},{8,9},{9,8},{10,11... | collective-permute-start | bytes 122888 | tf_op jit(solution)/shard_map/ppermute | solution.py:33
  51.9 6.6 %collective-permute-start.16 = (f32[160,128]{1,0:T(8,128)S(1)}, f32[160,128]{1,0:T(8,128)S(1)}, u32[]{:S(2)}, u32[]{:S(2)}) collective-permute-start(f32[160,128]{1,0:T(8,128)S(1)} %add.90.refs_7_), channel_id=1, source_target_pairs={{0,16},{4,20},{8,24},{12,28},{16,0},{20,4},{24,8},{28,12},{1,17},{... | collective-permute-start | bytes 245768 | tf_op jit(solution)/shard_map/ppermute | solution.py:33
  53.5 5.0 %collective-permute-start.13 = (f32[80,128]{1,0:T(8,128)S(1)}, f32[80,128]{1,0:T(8,128)S(1)}, u32[]{:S(2)}, u32[]{:S(2)}) collective-permute-start(f32[80,128]{1,0:T(8,128)S(1)} %add.88.refs_5_), channel_id=1, source_target_pairs={{0,2},{1,3},{2,0},{3,1},{4,6},{5,7},{6,4},{7,5},{8,10},{9,11},{10,... | collective-permute-start | bytes 122888 | tf_op jit(solution)/shard_map/ppermute | solution.py:33
  73.7 4.6 %collective-permute-start.22 = (f32[80,128]{1,0:T(8,128)S(1)}, f32[80,128]{1,0:T(8,128)S(1)}, u32[]{:S(2)}, u32[]{:S(2)}) collective-permute-start(f32[80,128]{1,0:T(8,128)S(1)} %get-tuple-element.56), channel_id=1, source_target_pairs={{0,1},{1,0},{2,3},{3,2},{4,5},{5,4},{6,7},{7,6},{8,9},{9,8},{10,11... | collective-permute-start | bytes 122888 | tf_op jit(solution)/shard_map/ppermute | solution.py:33
  77.6 5.7 %collective-permute-start.26 = (f32[160,128]{1,0:T(8,128)S(1)}, f32[160,128]{1,0:T(8,128)S(1)}, u32[]{:S(2)}, u32[]{:S(2)}) collective-permute-start(f32[160,128]{1,0:T(8,128)S(1)} %add.96.refs_5_), channel_id=1, source_target_pairs={{0,16},{4,20},{8,24},{12,28},{16,0},{20,4},{24,8},{28,12},{1,17},{... | collective-permute-start | bytes 245768 | tf_op jit(solution)/shard_map/ppermute | solution.py:33
  78.3 5.0 %collective-permute-start.23 = (f32[80,128]{1,0:T(8,128)S(1)}, f32[80,128]{1,0:T(8,128)S(1)}, u32[]{:S(2)}, u32[]{:S(2)}) collective-permute-start(f32[80,128]{1,0:T(8,128)S(1)} %add.94.refs_3_), channel_id=1, source_target_pairs={{0,2},{1,3},{2,0},{3,1},{4,6},{5,7},{6,4},{7,5},{8,10},{9,11},{10,... | collective-permute-start | bytes 122888 | tf_op jit(solution)/shard_map/ppermute | solution.py:33
  93.4 6.4 %collective-permute-start.31 = (f32[160,128]{1,0:T(8,128)S(1)}, f32[160,128]{1,0:T(8,128)S(1)}, u32[]{:S(2)}, u32[]{:S(2)}) collective-permute-start(f32[160,128]{1,0:T(8,128)S(1)} %add.99.refs_5_), channel_id=1, source_target_pairs={{0,16},{4,20},{8,24},{12,28},{16,0},{20,4},{24,8},{28,12},{1,17},{... | collective-permute-start | bytes 245768 | tf_op jit(solution)/shard_map/ppermute | solution.py:33
  94.9 5.0 %collective-permute-start.28 = (f32[80,128]{1,0:T(8,128)S(1)}, f32[80,128]{1,0:T(8,128)S(1)}, u32[]{:S(2)}, u32[]{:S(2)}) collective-permute-start(f32[80,128]{1,0:T(8,128)S(1)} %add.97.refs_3_), channel_id=1, source_target_pairs={{0,2},{1,3},{2,0},{3,1},{4,6},{5,7},{6,4},{7,5},{8,10},{9,11},{10,... | collective-permute-start | bytes 122888 | tf_op jit(solution)/shard_map/ppermute | solution.py:33
  106.1 4.6 %collective-permute-start.32 = (f32[80,128]{1,0:T(8,128)S(1)}, f32[80,128]{1,0:T(8,128)S(1)}, u32[]{:S(2)}, u32[]{:S(2)}) collective-permute-start(f32[80,128]{1,0:T(8,128)S(1)} %get-tuple-element.64), channel_id=1, source_target_pairs={{0,1},{1,0},{2,3},{3,2},{4,5},{5,4},{6,7},{7,6},{8,9},{9,8},{10,11... | collective-permute-start | bytes 122888 | tf_op jit(solution)/shard_map/ppermute | solution.py:33
  110.1 5.7 %collective-permute-start.36 = (f32[160,128]{1,0:T(8,128)S(1)}, f32[160,128]{1,0:T(8,128)S(1)}, u32[]{:S(2)}, u32[]{:S(2)}) collective-permute-start(f32[160,128]{1,0:T(8,128)S(1)} %add.102.refs_7_), channel_id=1, source_target_pairs={{0,16},{4,20},{8,24},{12,28},{16,0},{20,4},{24,8},{28,12},{1,17},{... | collective-permute-start | bytes 245768 | tf_op jit(solution)/shard_map/ppermute | solution.py:33
  110.8 5.0 %collective-permute-start.33 = (f32[80,128]{1,0:T(8,128)S(1)}, f32[80,128]{1,0:T(8,128)S(1)}, u32[]{:S(2)}, u32[]{:S(2)}) collective-permute-start(f32[80,128]{1,0:T(8,128)S(1)} %add.100.refs_5_), channel_id=1, source_target_pairs={{0,2},{1,3},{2,0},{3,1},{4,6},{5,7},{6,4},{7,5},{8,10},{9,11},{10,... | collective-permute-start | bytes 122888 | tf_op jit(solution)/shard_map/ppermute | solution.py:33
  135.7 6.7 %collective-permute-start.46 = (f32[160,128]{1,0:T(8,128)S(1)}, f32[160,128]{1,0:T(8,128)S(1)}, u32[]{:S(2)}, u32[]{:S(2)}) collective-permute-start(f32[160,128]{1,0:T(8,128)S(1)} %add.108.refs_2_), channel_id=1, source_target_pairs={{0,16},{4,20},{8,24},{12,28},{16,0},{20,4},{24,8},{28,12},{1,17},{... | collective-permute-start | bytes 245768 | tf_op jit(solution)/shard_map/ppermute | solution.py:33
  136.9 5.4 %collective-permute-start.43 = (f32[80,128]{1,0:T(8,128)S(1)}, f32[80,128]{1,0:T(8,128)S(1)}, u32[]{:S(2)}, u32[]{:S(2)}) collective-permute-start(f32[80,128]{1,0:T(8,128)S(1)} %add.106.refs_0_), channel_id=1, source_target_pairs={{0,2},{1,3},{2,0},{3,1},{4,6},{5,7},{6,4},{7,5},{8,10},{9,11},{10,... | collective-permute-start | bytes 122888 | tf_op jit(solution)/shard_map/ppermute | solution.py:33
  (26 other events, 89.2 us)
where the time goes:
time: 143 us
  waiting for transfers between devices  57.9 us (40%)
  starting transfers between devices  49.1 us (34%)
  Pallas kernels  29.7 us (21%)
  local copies, waits for them, and re-layouts  4.38 us (3%)
    ppermute x41, waiting for transfers between devices, swap(): return lax.ppermute(value, axis, [(i, i ^ mask) for i in range(size)])  53 us
    ppermute x41, starting transfers between devices, swap(): return lax.ppermute(value, axis, [(i, i ^ mask) for i in range(size)])  38 us
    pallas_call x10, Pallas kernels, call(): pl.pallas_call(kernel, out_shape=tuple((jax.ShapeDtypeStruct(*out) for ou...  29.7 us
    ppermute x3, starting transfers between devices, gather_frequencies(): total = total + lax.ppermute(held, both, pairs)  7.22 us
    ppermute x3, waiting for transfers between devices, gather_frequencies(): arrived.append(lax.ppermute(frequencies, both, pairs))  4.93 us
    unnamed x6, local copies, waits for them, and re-layouts  4.38 us
    ppermute x3, starting transfers between devices, gather_frequencies(): arrived.append(lax.ppermute(frequencies, both, pairs))  3.88 us
  transfers between devices with their start and end apart: 47, of which 29 were waited for; matrix products, arithmetic and copies ran while one was open for 0% of the time, Pallas kernels for 2%

commit v1 on v0

--- a/solution.py
+++ b/solution.py
@@ -15,6 +15,7 @@
 SUBLANES = 8
 LANES = 128
 VMEM_BYTES = 40 * 2**20
+MIXTURE_COST = 5 * 10**9
 
 
 def clip_unit(values):
@@ -33,12 +34,25 @@
     return lax.ppermute(value, axis, [(i, i ^ mask) for i in range(size)])
 
 
-def last_parts(value, axis):
-    size, stride = lax.axis_size(axis), 1
-    while 2 * stride < size:
+def strides_of(axis):
+    return [1 << bit for bit in range(lax.axis_size(axis).bit_length() - 1)]
+
+
+def all_parts_of(value, axis):
+    return [value] + [swap(value, axis, mask) for mask in range(1, lax.axis_size(axis))]
+
+
+def pair_sum(parts):
+    while len(parts) > 1:
+        parts = [a + b for a, b in zip(parts[::2], parts[1::2])]
+    return parts[0]
+
+
+def parts_of(value, axis):
+    strides = strides_of(axis)
+    for stride in strides[:-1]:
         value = value + swap(value, axis, stride)
-        stride *= 2
-    return value, swap(value, axis, stride)
+    return value, swap(value, axis, strides[-1])
 
 
 def gather_frequencies(frequencies):
@@ -118,11 +132,10 @@
 
 
 def sum_packed(parts, first, stride, count):
-    one, other = parts
     pieces = []
-    for top in range(first, one.shape[0], stride):
+    for top in range(first, parts[0].shape[0], stride):
         here = slice(top, top + count)
-        pieces.append(one[here, :] + other[here, :])
+        pieces.append(pair_sum([part[here, :] for part in parts]))
     return jnp.concatenate(pieces, axis=1)
 
 
@@ -177,71 +190,53 @@
         put_packed(both_ref, place * populations, 2 * populations, sums)
 
 
-def update(populations, mixture, alleles, twice_observed, prop_parts, both_parts):
+def next_mixture(populations, mixture, twice_observed, prop_parts):
     rows, samples = mixture.shape
     stride = prop_parts[0].shape[0] * LANES // samples
     prop_sums = sum_packed(prop_parts, 0, stride, populations)
     if twice_observed is None:
         twice_observed = sum_packed(prop_parts, populations, stride, 1)
+    moved = clip_unit(mixture[:populations] * prop_sums / twice_observed)
+    return pad_rows(moved, rows), twice_observed
+
+
+def next_alleles(populations, alleles, both_parts):
     alt_sums = sum_packed(both_parts, 0, 2 * populations, populations)
     ref_sums = sum_packed(both_parts, populations, 2 * populations, populations)
-    next_mixture = clip_unit(mixture[:populations] * prop_sums / twice_observed)
     current = alleles[:populations]
     weighted = current * alt_sums
-    next_alleles = clip_unit(weighted / (weighted + (1.0 - current) * ref_sums))
-    return pad_rows(next_mixture, rows), pad_rows(next_alleles, rows), twice_observed
-
-
-def prepare_kernel(genotypes, observed, alt_out, ref_out, count_out, landed, arrivals):
-    samples, variants = genotypes.shape
-    tall = blocks_of(samples, 128)
-    copies = []
-    for index, top in enumerate(range(0, samples, tall)):
-        here = pl.ds(top, tall)
-        for place, source in enumerate((genotypes, observed)):
-            copy = pltpu.make_async_copy(
-                source.at[here, :], landed.at[place, here, :], arrivals.at[place, index]
-            )
-            copy.start()
-            copies.append(copy)
-    ones = jnp.ones((SUBLANES, variants), BF16)
-    for index, top in enumerate(range(0, samples, tall)):
-        here = slice(top, top + tall)
-        copies[2 * index].wait()
-        copies[2 * index + 1].wait()
-        seen = landed[1, here, :]
-        alt = seen * landed[0, here, :]
-        alt_out[here, :] = alt.astype(F32).astype(BF16)
-        ref_out[here, :] = (2 * seen - alt).astype(F32).astype(BF16)
-        count_out[:, here] = 2.0 * dot(ones, seen.astype(F32).astype(BF16), 1, 1)
-
-
-def first_kernel(
-    mixture, alleles, counts, alt, ref, mixture_out, alleles_out, prop_out, both_out, turned
-):
+    moved = clip_unit(weighted / (weighted + (1.0 - current) * ref_sums))
+    return pad_rows(moved, alleles.shape[0])
+
+
+def first_kernel(mixture, alleles, alt, ref, mixture_out, alleles_out, prop_out, both_out, turned):
     populations = mixture.shape[0]
     rows = mixture_out.shape[0]
     mix = pad_rows(mixture[...], rows)
     current = pad_rows(alleles[...], rows)
     mixture_out[...] = mix
     alleles_out[...] = current
+    ones = jnp.ones((SUBLANES, alt.shape[1]), BF16)
+    twice_observed = dot(ones, alt[...], 1, 1) + dot(ones, ref[...], 1, 1)
     expectation(
-        populations, mix, current, alt, ref, prop_out, both_out, turned, counts[:1, :]
-    )
-
-
-def step_kernel(populations, with_twice, *refs):
-    mixture, alleles = refs[:2]
-    twice = refs[2][...] if with_twice else None
-    prop_parts, both_parts, (alt, ref), outs = split_refs(refs[2 + with_twice :], 2, 2, 2)
-    mix, current, twice = update(
-        populations, mixture[...], alleles[...], twice, prop_parts, both_parts
-    )
+        populations, mix, current, alt, ref, prop_out, both_out, turned, twice_observed[:1]
+    )
+
+
+def mixture_kernel(populations, with_twice, mixture, *refs):
+    twice = refs[0][...] if with_twice else None
+    prop_parts, outs = split_refs(refs[with_twice:], len(refs) - 2)
+    mix, twice = next_mixture(populations, mixture[...], twice, prop_parts)
     outs[0][...] = mix
-    outs[1][...] = current
     if not with_twice:
-        outs[4][...] = twice
-    expectation(populations, mix, current, alt, ref, outs[2], outs[3], outs[-1])
+        outs[1][...] = twice
+
+
+def step_kernel(populations, mixture, alleles, *refs):
+    both_parts, (alt, ref, alleles_out, prop_out, both_out, turned) = split_refs(refs, 2)
+    current = next_alleles(populations, alleles[...], both_parts)
+    alleles_out[...] = current
+    expectation(populations, mixture[...], current, alt, ref, prop_out, both_out, turned)
 
 
 def split_refs(refs, *counts):
@@ -259,21 +254,24 @@
     return sum(tile[:, i : i + LANES] for i in range(0, width, LANES))
 
 
-def square_kernel(populations, *refs):
-    mix_zero, all_zero, mix_one, all_one, twice = refs[:5]
-    prop_parts, both_parts, (mix_out, all_out, mix_tile, all_tile) = split_refs(refs[5:], 2, 2)
-    mix_two, all_two, _ = update(
-        populations, mix_one[...], all_one[...], twice[...], prop_parts, both_parts
-    )
-    mix_out[...] = mix_two
-    all_out[...] = all_two
-    for zero, one, two, tile in (
-        (mix_zero[...], mix_one[...], mix_two, mix_tile),
-        (all_zero[...], all_one[...], all_two, all_tile),
-    ):
-        step = one - zero
-        tile[:SUBLANES, :] = folded(step)
-        tile[SUBLANES:, :] = folded(two - one - step)
+def squares(zero, one, two, tile):
+    step = one - zero
+    tile[:SUBLANES, :] = folded(step)
+    tile[SUBLANES:, :] = folded(two - one - step)
+
+
+def mixture_square_kernel(populations, zero, one, twice, *refs):
+    prop_parts, (two_out, tile) = split_refs(refs, len(refs) - 2)
+    two, _ = next_mixture(populations, one[...], twice[...], prop_parts)
+    two_out[...] = two
+    squares(zero[...], one[...], two, tile)
+
+
+def alleles_square_kernel(populations, zero, one, *refs):
+    both_parts, (two_out, tile) = split_refs(refs, 2)
+    two = next_alleles(populations, one[...], both_parts)
+    two_out[...] = two
+    squares(zero[...], one[...], two, tile)
 
 
 def leap(zero, one, two, tile):
@@ -300,24 +298,28 @@
     expectation(populations, mix, current, alt, ref, prop_out, both_out, turned)
 
 
-def final_kernel(populations, mixture, alleles, twice, *refs):
-    prop_parts, both_parts, (mixture_out, alleles_out) = split_refs(refs, 2, 2)
-    mix, current, _ = update(
-        populations, mixture[...], alleles[...], twice[...], prop_parts, both_parts
-    )
-    mixture_out[...] = mix[:populations]
-    alleles_out[...] = current[:populations]
-
-
-def call(kernel, name, outs, args, scratch=(), space=pltpu.VMEM):
+def last_mixture_kernel(populations, mixture, twice, *refs):
+    prop_parts, (out,) = split_refs(refs, len(refs) - 1)
+    mix, _ = next_mixture(populations, mixture[...], twice[...], prop_parts)
+    out[...] = mix[:populations]
+
+
+def last_alleles_kernel(populations, alleles, *refs):
+    both_parts, (out,) = split_refs(refs, 2)
+    out[...] = next_alleles(populations, alleles[...], both_parts)[:populations]
+
+
+def call(kernel, name, outs, args, scratch=(), moved=0):
     whole = pl.BlockSpec(memory_space=pltpu.VMEM)
+    cost = pl.CostEstimate(flops=moved, bytes_accessed=0, transcendentals=0) if moved else None
     return pl.pallas_call(
         kernel,
         out_shape=tuple(jax.ShapeDtypeStruct(*out) for out in outs),
-        in_specs=[pl.BlockSpec(memory_space=space)] * len(args),
+        in_specs=[pl.BlockSpec(memory_space=pltpu.VMEM)] * len(args),
         out_specs=(whole,) * len(outs),
         scratch_shapes=list(scratch),
         compiler_params=pltpu.CompilerParams(vmem_limit_bytes=VMEM_BYTES),
+        cost_estimate=cost,
         name=name,
     )(*args)
 
@@ -333,59 +335,61 @@
     first_sums_out = (((packed + samples // LANES, LANES), F32), both_out)
     tile_out = ((2 * SUBLANES, LANES), F32)
     turned = (pltpu.VMEM((samples, 6 * rows), BF16),)
-    table_out = ((samples, variants), BF16)
-    chunks = samples // blocks_of(samples, 128)
 
     alleles = gather_frequencies(frequencies)
-    alt, ref, counts = call(
-        prepare_kernel,
-        "prepare",
-        (table_out, table_out, ((SUBLANES, samples), F32)),
-        (genotypes, observed),
-        (
-            pltpu.VMEM((2, samples, variants), jnp.int32),
-            pltpu.SemaphoreType.DMA((2, chunks)),
-        ),
-        pl.ANY,
-    )
-
-    def exchanged(prop, both):
-        return (*last_parts(prop, "var"), *last_parts(both, "samp"))
+    alt = (observed * genotypes).astype(BF16)
+    ref = (observed * (2 - genotypes)).astype(BF16)
 
     mix_zero, all_zero, prop, both = call(
         first_kernel,
         "first",
         (*state_out, *first_sums_out),
-        (proportions, alleles, counts, alt, ref),
+        (proportions, alleles, alt, ref),
         turned,
     )
+
+    def moved_mixture(mixture, twice, prop):
+        known = () if twice is None else (twice,)
+        extra = () if known else (((1, samples), F32),)
+        out = call(
+            functools.partial(mixture_kernel, populations, len(known)),
+            "mixture",
+            (state_out[0], *extra),
+            (mixture, *known, *all_parts_of(prop, "var")),
+            moved=MIXTURE_COST,
+        )
+        return out[0], (known or out[1:])[0]
+
+    def step(mixture, alleles, both):
+        return call(
+            functools.partial(step_kernel, populations),
+            "step",
+            (state_out[1], *sums_out),
+            (mixture, alleles, *parts_of(both, "samp"), alt, ref),
+            turned,
+        )
+
     twice = None
     for repeat in range(STEPS):
         if repeat:
-            mix_zero, all_zero, prop, both = call(
-                functools.partial(step_kernel, populations, 1),
-                "step",
-                (*state_out, *sums_out),
-                (mix_zero, all_zero, twice, *exchanged(prop, both), alt, ref),
-                turned,
-            )
-        known = () if twice is None else (twice,)
-        extra = () if known else (((1, samples), F32),)
-        mix_one, all_one, prop, both, *found = call(
-            functools.partial(step_kernel, populations, len(known)),
-            "step",
-            (*state_out, *sums_out, *extra),
-            (mix_zero, all_zero, *known, *exchanged(prop, both), alt, ref),
-            turned,
-        )
-        (twice,) = known or found
-        mix_two, all_two, mix_tile, all_tile = call(
-            functools.partial(square_kernel, populations),
-            "square",
-            (*state_out, tile_out, tile_out),
-            (mix_zero, all_zero, mix_one, all_one, twice, *exchanged(prop, both)),
-        )
-        tiles = (*last_parts(mix_tile, "samp"), *last_parts(all_tile, "var"))
+            mix_zero, twice = moved_mixture(mix_zero, twice, prop)
+            all_zero, prop, both = step(mix_zero, all_zero, both)
+        mix_one, twice = moved_mixture(mix_zero, twice, prop)
+        all_one, prop, both = step(mix_one, all_zero, both)
+        mix_two, mix_tile = call(
+            functools.partial(mixture_square_kernel, populations),
+            "mixture_square",
+            (state_out[0], tile_out),
+            (mix_zero, mix_one, twice, *all_parts_of(prop, "var")),
+            moved=MIXTURE_COST,
+        )
+        all_two, all_tile = call(
+            functools.partial(alleles_square_kernel, populations),
+            "alleles_square",
+            (state_out[1], tile_out),
+            (all_zero, all_one, *parts_of(both, "samp")),
+        )
+        tiles = (*parts_of(mix_tile, "samp"), *parts_of(all_tile, "var"))
         mix_zero, all_zero, prop, both = call(
             functools.partial(leap_kernel, populations),
             "leap",
@@ -393,12 +397,20 @@
             (mix_zero, all_zero, mix_one, all_one, mix_two, all_two, *tiles, alt, ref),
             turned,
         )
-    return call(
-        functools.partial(final_kernel, populations),
-        "final",
-        (((populations, samples), F32), ((populations, variants), F32)),
-        (mix_zero, all_zero, twice, *exchanged(prop, both)),
-    )
+    (mixture,) = call(
+        functools.partial(last_mixture_kernel, populations),
+        "last_mixture",
+        (((populations, samples), F32),),
+        (mix_zero, twice, *all_parts_of(prop, "var")),
+        moved=MIXTURE_COST,
+    )
+    (alleles,) = call(
+        functools.partial(last_alleles_kernel, populations),
+        "last_alleles",
+        (((populations, variants), F32),),
+        (all_zero, *parts_of(both, "samp")),
+    )
+    return mixture, alleles
 
 
 def solution(mesh):

time: 143 us -> 138 us (0.965)
  waiting for transfers between devices: 57.9 us -> 43.1 us
  starting transfers between devices: 49.1 us -> 58.8 us
  other arithmetic: 0.95 us -> 5.65 us
  local copies, waits for them, and re-layouts: 4.38 us -> 0.01 us
    ppermute x41 -> x47, waiting for transfers between devices: 53 us -> 38.2 us  [swap(): return lax.ppermute(value, axis, [(i, i ^ mask) for i in range(size)])]
    ppermute x41 -> x47, starting transfers between devices: 38 us -> 47.5 us  [swap(): return lax.ppermute(value, axis, [(i, i ^ mask) for i in range(size)])]
    convert_element_type x0 -> x1, other arithmetic: none -> 4.75 us  [local(): ref = (observed * (2 - genotypes)).astype(BF16)]
    unnamed x6 -> x2, local copies, waits for them, and re-layouts: 4.38 us -> 0.01 us
    pallas_call x10 -> x15, Pallas kernels: 29.7 us -> 28.8 us  [call(): pl.pallas_call(kernel, out_shape=tuple((jax.ShapeDtypeStruct(*out) for ou...]
  transfers between devices with their start and end apart: 47 -> 53, of which waited for: 29 -> 34; matrix products, arithmetic and copies ran while one was open for 0% -> 4% of each run, Pallas kernels for 2% -> 1%
where the time goes in v1:
time: 138 us; the launch traced here: 137 us
  starting transfers between devices  58.8 us (43%)
  waiting for transfers between devices  43.1 us (31%)
  Pallas kernels  28.8 us (21%)
  other arithmetic  5.65 us (4%)
    ppermute x47, starting transfers between devices, swap(): return lax.ppermute(value, axis, [(i, i ^ mask) for i in range(size)])  47.5 us
    ppermute x47, waiting for transfers between devices, swap(): return lax.ppermute(value, axis, [(i, i ^ mask) for i in range(size)])  38.2 us
    pallas_call x15, Pallas kernels, call(): pl.pallas_call(kernel, out_shape=tuple((jax.ShapeDtypeStruct(*out) for ou...  28.8 us
    ppermute x3, starting transfers between devices, gather_frequencies(): total = total + lax.ppermute(held, both, pairs)  7.35 us
    ppermute x3, waiting for transfers between devices, gather_frequencies(): arrived.append(lax.ppermute(frequencies, both, pairs))  4.93 us
    convert_element_type x1, other arithmetic, local(): ref = (observed * (2 - genotypes)).astype(BF16)  4.75 us
    ppermute x3, starting transfers between devices, gather_frequencies(): arrived.append(lax.ppermute(frequencies, both, pairs))  3.88 us
  transfers between devices with their start and end apart: 53, of which 34 were waited for; matrix products, arithmetic and copies ran while one was open for 4% of the time, Pallas kernels for 1%

profile of v1, /device:TPU:0, one launch (start us, length us, event | category | flops | bytes accessed | tf_op | source)
XLA Modules:
  0.0 137.3 jit_solution(16176990938896794216)
XLA Ops:
  4.5 3.2 %collective-permute-done.1 = f32[10,128]{1,0:T(8,128)S(1)} collective-permute-done((f32[10,128]{1,0:T(8,128)}, f32[10,128]{1,0:T(8,128)S(1)}, u32[]{:S(2)}, u32[]{:S(2)}) %collective-permute-start.1) | collective-permute-done | bytes 5152 | tf_op jit(solution)/shard_map/ppermute | solution.py:70
  11.5 4.8 %collective-permute-start.6 = (f32[10,1024]{1,0:T(8,128)S(1)}, f32[10,1024]{1,0:T(8,128)S(1)}, u32[]{:S(2)}, u32[]{:S(2)}) collective-permute-start(f32[10,1024]{1,0:T(8,128)S(1)} %maximum_select_fusion), channel_id=1, source_target_pairs={{0,24},{4,28},{9,17},{13,21},{18,10},{22,14},{27,3},{31,7}} | collective-permute-start | bytes 122888 | tf_op jit(solution)/shard_map/ppermute | solution.py:93
  18.9 4.7 %multiply_convert_fusion = (bf16[1024,1024]{1,0:T(8,128)(2,1)S(1)}, bf16[1024,1024]{1,0:T(8,128)(2,1)S(1)}) fusion(s32[1024,1024]{1,0:T(8,128)} %param.5, s32[1024,1024]{1,0:T(8,128)} %param.4), kind=kLoop, calls=%fused_computation | loop fusion | flops 5242880 | bytes 12582912 | tf_op jit(solution)/shard_map/convert_element_type | solution.py:341
  23.7 5.2 %first.1 = (f32[16,1024]{1,0:T(8,128)S(1)}, f32[16,1024]{1,0:T(8,128)S(1)}, f32[88,128]{1,0:T(8,128)S(1)}, f32[160,128]{1,0:T(8,128)S(1)}) custom-call(f32[10,1024]{1,0:T(8,128)S(1)} %copy-done, f32[10,1024]{1,0:T(8,128)S(1)} %add_add_fusion.alleles, bf16[1024,1024]{1,0:T(8,128)(2,1)S(1)} %get-tuple-element.65.alt.refs_2_.refs_10_, ...), custom_call_target="tpu_custom_call" | custom-call | tf_op jit(solution)/shard_map/first/pallas_call | solution.py:315
  32.5 2.3 %collective-permute-start.7 = (f32[88,128]{1,0:T(8,128)S(1)}, f32[88,128]{1,0:T(8,128)S(1)}, u32[]{:S(2)}, u32[]{:S(2)}) collective-permute-start(f32[88,128]{1,0:T(8,128)S(1)} %get-tuple-element.35.refs_0_), channel_id=1, source_target_pairs={{0,1},{1,0},{2,3},{3,2},{4,5},{5,4},{6,7},{7,6},{8,9},{9,8},{10,11... | collective-permute-start | bytes 135176 | tf_op jit(solution)/shard_map/ppermute | solution.py:34
  37.4 1.9 %collective-permute-done.12.refs_1_ = f32[160,128]{1,0:T(8,128)S(1)} collective-permute-done((f32[160,128]{1,0:T(8,128)S(1)}, f32[160,128]{1,0:T(8,128)S(1)}, u32[]{:S(2)}, u32[]{:S(2)}) %collective-permute-start.12) | collective-permute-done | bytes 81952 | tf_op jit(solution)/shard_map/ppermute | solution.py:34
  39.4 4.2 %step.3 = (f32[16,1024]{1,0:T(8,128)S(1)}, f32[80,128]{1,0:T(8,128)S(1)}, f32[160,128]{1,0:T(8,128)S(1)}) custom-call(f32[16,1024]{1,0:T(8,128)S(1)} %get-tuple-element.36.mixture.one.refs_2_, f32[16,1024]{1,0:T(8,128)S(1)} %get-tuple-element.34.alleles.zero.refs_1_, f32[160,128]{1,0:T(8,128)S(1)} %add.68.refs_0_, ...), custom_call_target="tpu_custom_call" | custom-call | tf_op jit(solution)/shard_map/step/pallas_call | solution.py:315
  44.9 2.0 %collective-permute-start.17 = (f32[160,128]{1,0:T(8,128)S(1)}, f32[160,128]{1,0:T(8,128)S(1)}, u32[]{:S(2)}, u32[]{:S(2)}) collective-permute-start(f32[160,128]{1,0:T(8,128)S(1)} %add.69), channel_id=1, source_target_pairs={{0,8},{4,12},{8,0},{12,4},{16,24},{20,28},{24,16},{28,20},{1,9},{5... | collective-permute-start | bytes 245768 | tf_op jit(solution)/shard_map/ppermute | solution.py:34
  48.3 2.9 %collective-permute-start.13 = (f32[80,128]{1,0:T(8,128)S(1)}, f32[80,128]{1,0:T(8,128)S(1)}, u32[]{:S(2)}, u32[]{:S(2)}) collective-permute-start(f32[80,128]{1,0:T(8,128)S(1)} %get-tuple-element.40.refs_0_), channel_id=1, source_target_pairs={{0,1},{1,0},{2,3},{3,2},{4,5},{5,4},{6,7},{7,6},{8,9},{9,8},{10,11... | collective-permute-start | bytes 122888 | tf_op jit(solution)/shard_map/ppermute | solution.py:34
  59.6 2.0 %collective-permute-start.23 = (f32[16,128]{1,0:T(8,128)S(1)}, f32[16,128]{1,0:T(8,128)S(1)}, u32[]{:S(2)}, u32[]{:S(2)}) collective-permute-start(f32[16,128]{1,0:T(8,128)S(1)} %add.73.refs_8_), channel_id=1, source_target_pairs={{0,2},{1,3},{2,0},{3,1},{4,6},{5,7},{6,4},{7,5},{8,10},{9,11},{10,... | collective-permute-start | bytes 24584 | tf_op jit(solution)/shard_map/ppermute | solution.py:34
  64.1 4.6 %leap.2 = (f32[16,1024]{1,0:T(8,128)S(1)}, f32[16,1024]{1,0:T(8,128)S(1)}, f32[80,128]{1,0:T(8,128)S(1)}, f32[160,128]{1,0:T(8,128)S(1)}) custom-call(f32[16,1024]{1,0:T(8,128)S(1)} %get-tuple-element.33.mixture.zero.refs_0_, f32[16,1024]{1,0:T(8,128)S(1)} %get-tuple-element.34.alleles.zero.refs_1_, f32[16,1024]{1,0:T(8,128)S(1)} %get-tuple-element.36.mixture.one.refs_2_, ...), custom_call_target="tpu_custom_call" | custom-call | tf_op jit(solution)/shard_map/leap/pallas_call | solution.py:315
  70.1 2.0 %collective-permute-start.28 = (f32[160,128]{1,0:T(8,128)S(1)}, f32[160,128]{1,0:T(8,128)S(1)}, u32[]{:S(2)}, u32[]{:S(2)}) collective-permute-start(f32[160,128]{1,0:T(8,128)S(1)} %add.74), channel_id=1, source_target_pairs={{0,8},{4,12},{8,0},{12,4},{16,24},{20,28},{24,16},{28,20},{1,9},{5... | collective-permute-start | bytes 245768 | tf_op jit(solution)/shard_map/ppermute | solution.py:34
  74.4 2.0 %collective-permute-start.24 = (f32[80,128]{1,0:T(8,128)S(1)}, f32[80,128]{1,0:T(8,128)S(1)}, u32[]{:S(2)}, u32[]{:S(2)}) collective-permute-start(f32[80,128]{1,0:T(8,128)S(1)} %get-tuple-element.47.refs_1_), channel_id=1, source_target_pairs={{0,1},{1,0},{2,3},{3,2},{4,5},{5,4},{6,7},{7,6},{8,9},{9,8},{10,11... | collective-permute-start | bytes 122888 | tf_op jit(solution)/shard_map/ppermute | solution.py:34
  79.0 1.9 %collective-permute-done.29.refs_1_ = f32[160,128]{1,0:T(8,128)S(1)} collective-permute-done((f32[160,128]{1,0:T(8,128)S(1)}, f32[160,128]{1,0:T(8,128)S(1)}, u32[]{:S(2)}, u32[]{:S(2)}) %collective-permute-start.29) | collective-permute-done | bytes 81952 | tf_op jit(solution)/shard_map/ppermute | solution.py:34
  80.9 4.2 %step.4 = (f32[16,1024]{1,0:T(8,128)S(1)}, f32[80,128]{1,0:T(8,128)S(1)}, f32[160,128]{1,0:T(8,128)S(1)}) custom-call(f32[16,1024]{1,0:T(8,128)S(1)} %mixture.6.zero.refs_0_, f32[16,1024]{1,0:T(8,128)S(1)} %get-tuple-element.48.alleles, f32[160,128]{1,0:T(8,128)S(1)} %add.75.refs_0_, f32[160,128]{1,0:T(8,128)S(1)} %collective-permute-done.29.refs_1_, ...), custom_call_target="tpu_custom_call" | custom-call | tf_op jit(solution)/shard_map/step/pallas_call | solution.py:315
  86.7 2.0 %collective-permute-start.32 = (f32[80,128]{1,0:T(8,128)S(1)}, f32[80,128]{1,0:T(8,128)S(1)}, u32[]{:S(2)}, u32[]{:S(2)}) collective-permute-start(f32[80,128]{1,0:T(8,128)S(1)} %get-tuple-element.51.refs_1_), channel_id=1, source_target_pairs={{0,3},{1,2},{2,1},{3,0},{4,7},{5,6},{6,5},{7,4},{8,11},{9,10},{10,... | collective-permute-start | bytes 122888 | tf_op jit(solution)/shard_map/ppermute | solution.py:34
  89.0 2.0 %collective-permute-start.30 = (f32[80,128]{1,0:T(8,128)S(1)}, f32[80,128]{1,0:T(8,128)S(1)}, u32[]{:S(2)}, u32[]{:S(2)}) collective-permute-start(f32[80,128]{1,0:T(8,128)S(1)} %get-tuple-element.51.refs_1_), channel_id=1, source_target_pairs={{0,1},{1,0},{2,3},{3,2},{4,5},{5,4},{6,7},{7,6},{8,9},{9,8},{10,11... | collective-permute-start | bytes 122888 | tf_op jit(solution)/shard_map/ppermute | solution.py:34
  91.1 2.1 %collective-permute-start.35 = (f32[160,128]{1,0:T(8,128)S(1)}, f32[160,128]{1,0:T(8,128)S(1)}, u32[]{:S(2)}, u32[]{:S(2)}) collective-permute-start(f32[160,128]{1,0:T(8,128)S(1)} %add.77.refs_0_), channel_id=1, source_target_pairs={{0,16},{4,20},{8,24},{12,28},{16,0},{20,4},{24,8},{28,12},{1,17},{... | collective-permute-start | bytes 245768 | tf_op jit(solution)/shard_map/ppermute | solution.py:34
  95.6 4.4 %step.5 = (f32[16,1024]{1,0:T(8,128)S(1)}, f32[80,128]{1,0:T(8,128)S(1)}, f32[160,128]{1,0:T(8,128)S(1)}) custom-call(f32[16,1024]{1,0:T(8,128)S(1)} %mixture.7.one.refs_2_, f32[16,1024]{1,0:T(8,128)S(1)} %get-tuple-element.50.alleles.zero.refs_1_, f32[160,128]{1,0:T(8,128)S(1)} %add.77.refs_0_, f32[160,128]{1,0:T(8,128)S(1)} %collective-permute-done.35.refs_1_, ...), custom_call_target="tpu_custom_call" | custom-call | tf_op jit(solution)/shard_map/step/pallas_call | solution.py:315
  101.3 2.0 %collective-permute-start.40 = (f32[160,128]{1,0:T(8,128)S(1)}, f32[160,128]{1,0:T(8,128)S(1)}, u32[]{:S(2)}, u32[]{:S(2)}) collective-permute-start(f32[160,128]{1,0:T(8,128)S(1)} %add.78), channel_id=1, source_target_pairs={{0,8},{4,12},{8,0},{12,4},{16,24},{20,28},{24,16},{28,20},{1,9},{5... | collective-permute-start | bytes 245768 | tf_op jit(solution)/shard_map/ppermute | solution.py:34
  104.8 2.8 %collective-permute-start.36 = (f32[80,128]{1,0:T(8,128)S(1)}, f32[80,128]{1,0:T(8,128)S(1)}, u32[]{:S(2)}, u32[]{:S(2)}) collective-permute-start(f32[80,128]{1,0:T(8,128)S(1)} %get-tuple-element.54.refs_0_), channel_id=1, source_target_pairs={{0,1},{1,0},{2,3},{3,2},{4,5},{5,4},{6,7},{7,6},{8,9},{9,8},{10,11... | collective-permute-start | bytes 122888 | tf_op jit(solution)/shard_map/ppermute | solution.py:34
  113.2 1.9 %collective-permute-done.43 = f32[16,128]{1,0:T(8,128)S(1)} collective-permute-done((f32[16,128]{1,0:T(8,128)S(1)}, f32[16,128]{1,0:T(8,128)S(1)}, u32[]{:S(2)}, u32[]{:S(2)}) %collective-permute-start.43) | collective-permute-done | bytes 8224 | tf_op jit(solution)/shard_map/ppermute | solution.py:34
  116.0 2.0 %collective-permute-start.46 = (f32[16,128]{1,0:T(8,128)S(1)}, f32[16,128]{1,0:T(8,128)S(1)}, u32[]{:S(2)}, u32[]{:S(2)}) collective-permute-start(f32[16,128]{1,0:T(8,128)S(1)} %add.82.refs_8_), channel_id=1, source_target_pairs={{0,2},{1,3},{2,0},{3,1},{4,6},{5,7},{6,4},{7,5},{8,10},{9,11},{10,... | collective-permute-start | bytes 24584 | tf_op jit(solution)/shard_map/ppermute | solution.py:34
  120.5 4.5 %leap.3 = (f32[16,1024]{1,0:T(8,128)S(1)}, f32[16,1024]{1,0:T(8,128)S(1)}, f32[80,128]{1,0:T(8,128)S(1)}, f32[160,128]{1,0:T(8,128)S(1)}) custom-call(f32[16,1024]{1,0:T(8,128)S(1)} %mixture.6.zero.refs_0_, f32[16,1024]{1,0:T(8,128)S(1)} %get-tuple-element.50.alleles.zero.refs_1_, f32[16,1024]{1,0:T(8,128)S(1)} %mixture.7.one.refs_2_, ...), custom_call_target="tpu_custom_call" | custom-call | tf_op jit(solution)/shard_map/leap/pallas_call | solution.py:315
  (123 shorter events, 64.5 us)
Async XLA Ops:
  0.6 7.2 %collective-permute-start.1 = (f32[10,128]{1,0:T(8,128)}, f32[10,128]{1,0:T(8,128)S(1)}, u32[]{:S(2)}, u32[]{:S(2)}) collective-permute-start(f32[10,128]{1,0:T(8,128)} %param.7), channel_id=1, source_target_pairs={{2,0},{6,4},{11,9},{15,13},{16,18},{20,22},{25,27},{29,31}} | collective-permute-start | bytes 15368 | tf_op jit(solution)/shard_map/ppermute | solution.py:70
  1.9 7.6 %collective-permute-start = (f32[10,128]{1,0:T(8,128)}, f32[10,128]{1,0:T(8,128)S(1)}, u32[]{:S(2)}, u32[]{:S(2)}) collective-permute-start(f32[10,128]{1,0:T(8,128)} %param.7), channel_id=1, source_target_pairs={{3,0},{7,4},{10,9},{14,13},{17,18},{21,22},{24,27},{28,31}} | collective-permute-start | bytes 15368 | tf_op jit(solution)/shard_map/ppermute | solution.py:70
  3.2 6.3 %collective-permute-start.2 = (f32[10,128]{1,0:T(8,128)}, f32[10,128]{1,0:T(8,128)S(1)}, u32[]{:S(2)}, u32[]{:S(2)}) collective-permute-start(f32[10,128]{1,0:T(8,128)} %param.7), channel_id=1, source_target_pairs={{1,0},{5,4},{8,9},{12,13},{19,18},{23,22},{26,27},{30,31}} | collective-permute-start | bytes 15368 | tf_op jit(solution)/shard_map/ppermute | solution.py:70
  11.5 12.1 %collective-permute-start.6 = (f32[10,1024]{1,0:T(8,128)S(1)}, f32[10,1024]{1,0:T(8,128)S(1)}, u32[]{:S(2)}, u32[]{:S(2)}) collective-permute-start(f32[10,1024]{1,0:T(8,128)S(1)} %maximum_select_fusion), channel_id=1, source_target_pairs={{0,24},{4,28},{9,17},{13,21},{18,10},{22,14},{27,3},{31,7}} | collective-permute-start | bytes 122888 | tf_op jit(solution)/shard_map/ppermute | solution.py:93
  16.3 7.4 %collective-permute-start.5 = (f32[10,1024]{1,0:T(8,128)S(1)}, f32[10,1024]{1,0:T(8,128)S(1)}, u32[]{:S(2)}, u32[]{:S(2)}) collective-permute-start(f32[10,1024]{1,0:T(8,128)S(1)} %maximum_select_fusion), channel_id=1, source_target_pairs={{0,16},{4,20},{9,25},{13,29},{18,2},{22,6},{27,11},{31,15}} | collective-permute-start | bytes 122888 | tf_op jit(solution)/shard_map/ppermute | solution.py:93
  17.6 6.1 %collective-permute-start.4 = (f32[10,1024]{1,0:T(8,128)S(1)}, f32[10,1024]{1,0:T(8,128)S(1)}, u32[]{:S(2)}, u32[]{:S(2)}) collective-permute-start(f32[10,1024]{1,0:T(8,128)S(1)} %maximum_select_fusion), channel_id=1, source_target_pairs={{0,8},{4,12},{9,1},{13,5},{18,26},{22,30},{27,19},{31,23}} | collective-permute-start | bytes 122888 | tf_op jit(solution)/shard_map/ppermute | solution.py:93
  30.3 6.4 %collective-permute-start.9 = (f32[88,128]{1,0:T(8,128)S(1)}, f32[88,128]{1,0:T(8,128)S(1)}, u32[]{:S(2)}, u32[]{:S(2)}) collective-permute-start(f32[88,128]{1,0:T(8,128)S(1)} %get-tuple-element.35.refs_0_), channel_id=1, source_target_pairs={{0,3},{1,2},{2,1},{3,0},{4,7},{5,6},{6,5},{7,4},{8,11},{9,10},{10,... | collective-permute-start | bytes 135176 | tf_op jit(solution)/shard_map/ppermute | solution.py:34
  31.3 6.0 %collective-permute-start.8 = (f32[88,128]{1,0:T(8,128)S(1)}, f32[88,128]{1,0:T(8,128)S(1)}, u32[]{:S(2)}, u32[]{:S(2)}) collective-permute-start(f32[88,128]{1,0:T(8,128)S(1)} %get-tuple-element.35.refs_0_), channel_id=1, source_target_pairs={{0,2},{1,3},{2,0},{3,1},{4,6},{5,7},{6,4},{7,5},{8,10},{9,11},{10,... | collective-permute-start | bytes 135176 | tf_op jit(solution)/shard_map/ppermute | solution.py:34
  44.9 6.4 %collective-permute-start.17 = (f32[160,128]{1,0:T(8,128)S(1)}, f32[160,128]{1,0:T(8,128)S(1)}, u32[]{:S(2)}, u32[]{:S(2)}) collective-permute-start(f32[160,128]{1,0:T(8,128)S(1)} %add.69), channel_id=1, source_target_pairs={{0,8},{4,12},{8,0},{12,4},{16,24},{20,28},{24,16},{28,20},{1,9},{5... | collective-permute-start | bytes 245768 | tf_op jit(solution)/shard_map/ppermute | solution.py:34
  46.9 6.2 %collective-permute-start.15 = (f32[80,128]{1,0:T(8,128)S(1)}, f32[80,128]{1,0:T(8,128)S(1)}, u32[]{:S(2)}, u32[]{:S(2)}) collective-permute-start(f32[80,128]{1,0:T(8,128)S(1)} %get-tuple-element.40.refs_0_), channel_id=1, source_target_pairs={{0,3},{1,2},{2,1},{3,0},{4,7},{5,6},{6,5},{7,4},{8,11},{9,10},{10,... | collective-permute-start | bytes 122888 | tf_op jit(solution)/shard_map/ppermute | solution.py:34
  47.7 6.0 %collective-permute-start.14 = (f32[80,128]{1,0:T(8,128)S(1)}, f32[80,128]{1,0:T(8,128)S(1)}, u32[]{:S(2)}, u32[]{:S(2)}) collective-permute-start(f32[80,128]{1,0:T(8,128)S(1)} %get-tuple-element.40.refs_0_), channel_id=1, source_target_pairs={{0,2},{1,3},{2,0},{3,1},{4,6},{5,7},{6,4},{7,5},{8,10},{9,11},{10,... | collective-permute-start | bytes 122888 | tf_op jit(solution)/shard_map/ppermute | solution.py:34
  48.3 5.3 %collective-permute-start.13 = (f32[80,128]{1,0:T(8,128)S(1)}, f32[80,128]{1,0:T(8,128)S(1)}, u32[]{:S(2)}, u32[]{:S(2)}) collective-permute-start(f32[80,128]{1,0:T(8,128)S(1)} %get-tuple-element.40.refs_0_), channel_id=1, source_target_pairs={{0,1},{1,0},{2,3},{3,2},{4,5},{5,4},{6,7},{7,6},{8,9},{9,8},{10,11... | collective-permute-start | bytes 122888 | tf_op jit(solution)/shard_map/ppermute | solution.py:34
  70.1 6.3 %collective-permute-start.28 = (f32[160,128]{1,0:T(8,128)S(1)}, f32[160,128]{1,0:T(8,128)S(1)}, u32[]{:S(2)}, u32[]{:S(2)}) collective-permute-start(f32[160,128]{1,0:T(8,128)S(1)} %add.74), channel_id=1, source_target_pairs={{0,8},{4,12},{8,0},{12,4},{16,24},{20,28},{24,16},{28,20},{1,9},{5... | collective-permute-start | bytes 245768 | tf_op jit(solution)/shard_map/ppermute | solution.py:34
  72.0 6.2 %collective-permute-start.26 = (f32[80,128]{1,0:T(8,128)S(1)}, f32[80,128]{1,0:T(8,128)S(1)}, u32[]{:S(2)}, u32[]{:S(2)}) collective-permute-start(f32[80,128]{1,0:T(8,128)S(1)} %get-tuple-element.47.refs_1_), channel_id=1, source_target_pairs={{0,3},{1,2},{2,1},{3,0},{4,7},{5,6},{6,5},{7,4},{8,11},{9,10},{10,... | collective-permute-start | bytes 122888 | tf_op jit(solution)/shard_map/ppermute | solution.py:34
  73.6 5.4 %collective-permute-start.25 = (f32[80,128]{1,0:T(8,128)S(1)}, f32[80,128]{1,0:T(8,128)S(1)}, u32[]{:S(2)}, u32[]{:S(2)}) collective-permute-start(f32[80,128]{1,0:T(8,128)S(1)} %get-tuple-element.47.refs_1_), channel_id=1, source_target_pairs={{0,2},{1,3},{2,0},{3,1},{4,6},{5,7},{6,4},{7,5},{8,10},{9,11},{10,... | collective-permute-start | bytes 122888 | tf_op jit(solution)/shard_map/ppermute | solution.py:34
  86.7 6.5 %collective-permute-start.32 = (f32[80,128]{1,0:T(8,128)S(1)}, f32[80,128]{1,0:T(8,128)S(1)}, u32[]{:S(2)}, u32[]{:S(2)}) collective-permute-start(f32[80,128]{1,0:T(8,128)S(1)} %get-tuple-element.51.refs_1_), channel_id=1, source_target_pairs={{0,3},{1,2},{2,1},{3,0},{4,7},{5,6},{6,5},{7,4},{8,11},{9,10},{10,... | collective-permute-start | bytes 122888 | tf_op jit(solution)/shard_map/ppermute | solution.py:34
  88.7 5.3 %collective-permute-start.31 = (f32[80,128]{1,0:T(8,128)S(1)}, f32[80,128]{1,0:T(8,128)S(1)}, u32[]{:S(2)}, u32[]{:S(2)}) collective-permute-start(f32[80,128]{1,0:T(8,128)S(1)} %get-tuple-element.51.refs_1_), channel_id=1, source_target_pairs={{0,2},{1,3},{2,0},{3,1},{4,6},{5,7},{6,4},{7,5},{8,10},{9,11},{10,... | collective-permute-start | bytes 122888 | tf_op jit(solution)/shard_map/ppermute | solution.py:34
  101.3 6.3 %collective-permute-start.40 = (f32[160,128]{1,0:T(8,128)S(1)}, f32[160,128]{1,0:T(8,128)S(1)}, u32[]{:S(2)}, u32[]{:S(2)}) collective-permute-start(f32[160,128]{1,0:T(8,128)S(1)} %add.78), channel_id=1, source_target_pairs={{0,8},{4,12},{8,0},{12,4},{16,24},{20,28},{24,16},{28,20},{1,9},{5... | collective-permute-start | bytes 245768 | tf_op jit(solution)/shard_map/ppermute | solution.py:34
  103.3 5.8 %collective-permute-start.38 = (f32[80,128]{1,0:T(8,128)S(1)}, f32[80,128]{1,0:T(8,128)S(1)}, u32[]{:S(2)}, u32[]{:S(2)}) collective-permute-start(f32[80,128]{1,0:T(8,128)S(1)} %get-tuple-element.54.refs_0_), channel_id=1, source_target_pairs={{0,3},{1,2},{2,1},{3,0},{4,7},{5,6},{6,5},{7,4},{8,11},{9,10},{10,... | collective-permute-start | bytes 122888 | tf_op jit(solution)/shard_map/ppermute | solution.py:34
  104.8 5.4 %collective-permute-start.37 = (f32[80,128]{1,0:T(8,128)S(1)}, f32[80,128]{1,0:T(8,128)S(1)}, u32[]{:S(2)}, u32[]{:S(2)}) collective-permute-start(f32[80,128]{1,0:T(8,128)S(1)} %get-tuple-element.54.refs_0_), channel_id=1, source_target_pairs={{0,2},{1,3},{2,0},{3,1},{4,6},{5,7},{6,4},{7,5},{8,10},{9,11},{10,... | collective-permute-start | bytes 122888 | tf_op jit(solution)/shard_map/ppermute | solution.py:34
  104.8 5.4 %collective-permute-start.36 = (f32[80,128]{1,0:T(8,128)S(1)}, f32[80,128]{1,0:T(8,128)S(1)}, u32[]{:S(2)}, u32[]{:S(2)}) collective-permute-start(f32[80,128]{1,0:T(8,128)S(1)} %get-tuple-element.54.refs_0_), channel_id=1, source_target_pairs={{0,1},{1,0},{2,3},{3,2},{4,5},{5,4},{6,7},{7,6},{8,9},{9,8},{10,11... | collective-permute-start | bytes 122888 | tf_op jit(solution)/shard_map/ppermute | solution.py:34
  126.3 5.8 %collective-permute-start.51 = (f32[160,128]{1,0:T(8,128)S(1)}, f32[160,128]{1,0:T(8,128)S(1)}, u32[]{:S(2)}, u32[]{:S(2)}) collective-permute-start(f32[160,128]{1,0:T(8,128)S(1)} %add.83), channel_id=1, source_target_pairs={{0,8},{4,12},{8,0},{12,4},{16,24},{20,28},{24,16},{28,20},{1,9},{5... | collective-permute-start | bytes 245768 | tf_op jit(solution)/shard_map/ppermute | solution.py:34
  127.7 5.8 %collective-permute-start.49 = (f32[80,128]{1,0:T(8,128)S(1)}, f32[80,128]{1,0:T(8,128)S(1)}, u32[]{:S(2)}, u32[]{:S(2)}) collective-permute-start(f32[80,128]{1,0:T(8,128)S(1)} %get-tuple-element.61.refs_0_), channel_id=1, source_target_pairs={{0,3},{1,2},{2,1},{3,0},{4,7},{5,6},{6,5},{7,4},{8,11},{9,10},{10,... | collective-permute-start | bytes 122888 | tf_op jit(solution)/shard_map/ppermute | solution.py:34
  129.5 5.6 %collective-permute-start.48 = (f32[80,128]{1,0:T(8,128)S(1)}, f32[80,128]{1,0:T(8,128)S(1)}, u32[]{:S(2)}, u32[]{:S(2)}) collective-permute-start(f32[80,128]{1,0:T(8,128)S(1)} %get-tuple-element.61.refs_0_), channel_id=1, source_target_pairs={{0,2},{1,3},{2,0},{3,1},{4,6},{5,7},{6,4},{7,5},{8,10},{9,11},{10,... | collective-permute-start | bytes 122888 | tf_op jit(solution)/shard_map/ppermute | solution.py:34
  (30 other events, 110.2 us)

commit v2 on v1

--- a/solution.py
+++ b/solution.py
@@ -15,6 +15,7 @@
 SUBLANES = 8
 LANES = 128
 VMEM_BYTES = 40 * 2**20
+TALL, WIDE = 512, 512
 MIXTURE_COST = 5 * 10**9
 
 
@@ -107,11 +108,9 @@
     return high, middle, (rest - middle.astype(F32)).astype(BF16)
 
 
-def ratio(counts, denominator):
-    inverse = pl.reciprocal(denominator, approx=True)
-    high = inverse.astype(BF16)
-    low = (inverse - high.astype(F32)).astype(BF16)
-    return counts * high, counts * low
+def two_terms(values):
+    high = values.astype(BF16)
+    return high, (values - high.astype(F32)).astype(BF16)
 
 
 def row_mask(values, populations):
@@ -139,55 +138,47 @@
     return jnp.concatenate(pieces, axis=1)
 
 
-def expectation(populations, mixture, alleles, alt_ref, ref_ref, prop_ref, both_ref, turned, counts=None):
+def expectation(
+    populations, mixture, alleles, twice_here, alt_ref, ref_ref, prop_ref, both_ref, turned
+):
     rows, samples = mixture.shape
     variants = alleles.shape[1]
-    tall, wide = blocks_of(samples, 1024), blocks_of(variants, 512)
+    tall, wide = blocks_of(samples, TALL), blocks_of(variants, WIDE)
     mix_high, mix_mid, mix_low = split(mixture)
     all_high, all_mid, all_low = split(alleles)
-    away_high, away_mid, _ = split(row_mask(1.0 - alleles, populations))
     turned[...] = jnp.concatenate(
         [mix_high, mix_high, mix_mid, mix_mid, mix_high, mix_low], axis=0
     ).T
     right = jnp.concatenate([all_high, all_mid, all_high, all_mid, all_low, all_high], axis=0)
     toward = jnp.concatenate([all_high, all_mid], axis=0)
-    away = jnp.concatenate([away_high, away_mid], axis=0)
     left = jnp.concatenate([mix_high, mix_mid], axis=0)
-    column_starts = range(0, variants, wide)
-    alt_total = [jnp.zeros((2 * rows, wide), F32) for _ in column_starts]
-    ref_total = [jnp.zeros((2 * rows, wide), F32) for _ in column_starts]
-    props = []
-    for top in range(0, samples, tall):
-        here = slice(top, top + tall)
-        prop = jnp.zeros((2 * rows, tall), F32)
-        for index, start in enumerate(column_starts):
-            across = slice(start, start + wide)
+    props = [jnp.zeros((2 * rows, tall), F32) for _ in range(0, samples, tall)]
+    for start in range(0, variants, wide):
+        across = slice(start, start + wide)
+        excess = jnp.zeros((2 * rows, wide), F32)
+        ref_sum = jnp.zeros((2 * rows, wide), F32)
+        for index, top in enumerate(range(0, samples, tall)):
+            here = slice(top, top + tall)
             expected = dot(turned[here, :], right[:, across], 1, 0)
-            alt_high, alt_low = ratio(alt_ref[here, across], expected)
-            ref_high, ref_low = ratio(ref_ref[here, across], 1.0 - expected)
-            prop = (
-                prop
-                + dot(toward[:, across], alt_high, 1, 1)
-                + dot(toward[:, across], alt_low, 1, 1)
-                + dot(away[:, across], ref_high, 1, 1)
-                + dot(away[:, across], ref_low, 1, 1)
-            )
-            weights = left[:, here]
-            alt_total[index] = (
-                alt_total[index] + dot(weights, alt_high, 1, 0) + dot(weights, alt_low, 1, 0)
-            )
-            ref_total[index] = (
-                ref_total[index] + dot(weights, ref_high, 1, 0) + dot(weights, ref_low, 1, 0)
-            )
-        props.append(prop[:populations] + prop[rows : rows + populations])
+            ref = ref_ref[here, across] * pl.reciprocal(1.0 - expected, approx=True)
+            gap = alt_ref[here, across] * pl.reciprocal(expected, approx=True) - ref
+            for term in two_terms(gap):
+                props[index] = props[index] + dot(toward[:, across], term, 1, 1)
+                excess = excess + dot(left[:, here], term, 1, 0)
+            for term in two_terms(ref):
+                ref_sum = ref_sum + dot(left[:, here], term, 1, 0)
+        excess = excess[:populations] + excess[rows : rows + populations]
+        ref_sum = ref_sum[:populations] + ref_sum[rows : rows + populations]
+        first_block = start // LANES * 2 * populations
+        put_packed(both_ref, first_block, 2 * populations, excess + ref_sum)
+        put_packed(both_ref, first_block + populations, 2 * populations, ref_sum)
+    prop = jnp.concatenate(props, axis=1)
+    prop = prop[:populations] + prop[rows : rows + populations]
+    along = jnp.sum(mixture[:populations] * prop, axis=0, keepdims=True)
     stride = prop_ref.shape[0] * LANES // samples
-    put_packed(prop_ref, 0, stride, jnp.concatenate(props, axis=1))
-    if counts is not None:
-        put_packed(prop_ref, populations, stride, counts)
-    for place, totals in enumerate((alt_total, ref_total)):
-        sums = jnp.concatenate(totals, axis=1)
-        sums = sums[:populations] + sums[rows : rows + populations]
-        put_packed(both_ref, place * populations, 2 * populations, sums)
+    put_packed(prop_ref, 0, stride, prop + (twice_here - along))
+    if stride > populations:
+        put_packed(prop_ref, populations, stride, twice_here)
 
 
 def next_mixture(populations, mixture, twice_observed, prop_parts):
@@ -209,7 +200,9 @@
     return pad_rows(moved, alleles.shape[0])
 
 
-def first_kernel(mixture, alleles, alt, ref, mixture_out, alleles_out, prop_out, both_out, turned):
+def first_kernel(
+    mixture, alleles, alt, ref, mixture_out, alleles_out, twice_out, prop_out, both_out, turned
+):
     populations = mixture.shape[0]
     rows = mixture_out.shape[0]
     mix = pad_rows(mixture[...], rows)
@@ -217,10 +210,9 @@
     mixture_out[...] = mix
     alleles_out[...] = current
     ones = jnp.ones((SUBLANES, alt.shape[1]), BF16)
-    twice_observed = dot(ones, alt[...], 1, 1) + dot(ones, ref[...], 1, 1)
-    expectation(
-        populations, mix, current, alt, ref, prop_out, both_out, turned, twice_observed[:1]
-    )
+    twice = dot(ones, (alt[...] + ref[...]).astype(BF16), 1, 1)[:1]
+    twice_out[...] = twice
+    expectation(populations, mix, current, twice, alt, ref, prop_out, both_out, turned)
 
 
 def mixture_kernel(populations, with_twice, mixture, *refs):
@@ -232,11 +224,13 @@
         outs[1][...] = twice
 
 
-def step_kernel(populations, mixture, alleles, *refs):
+def step_kernel(populations, mixture, alleles, twice_here, *refs):
     both_parts, (alt, ref, alleles_out, prop_out, both_out, turned) = split_refs(refs, 2)
     current = next_alleles(populations, alleles[...], both_parts)
     alleles_out[...] = current
-    expectation(populations, mixture[...], current, alt, ref, prop_out, both_out, turned)
+    expectation(
+        populations, mixture[...], current, twice_here[...], alt, ref, prop_out, both_out, turned
+    )
 
 
 def split_refs(refs, *counts):
@@ -287,7 +281,7 @@
     states = [ref[...] for ref in refs[:6]]
     mix_zero, all_zero, mix_one, all_one, mix_two, all_two = states
     mix_parts, all_parts, rest = split_refs(refs[6:], 2, 2)
-    alt, ref, mixture_out, alleles_out, prop_out, both_out, turned = rest
+    twice_here, alt, ref, mixture_out, alleles_out, prop_out, both_out, turned = rest
     mix_tile = mix_parts[0][...] + mix_parts[1][...]
     all_tile = all_parts[0][...] + all_parts[1][...]
     clipped = row_mask(clip_unit(leap(mix_zero, mix_one, mix_two, mix_tile)), populations)
@@ -295,7 +289,9 @@
     current = row_mask(clip_unit(leap(all_zero, all_one, all_two, all_tile)), populations)
     mixture_out[...] = mix
     alleles_out[...] = current
-    expectation(populations, mix, current, alt, ref, prop_out, both_out, turned)
+    expectation(
+        populations, mix, current, twice_here[...], alt, ref, prop_out, both_out, turned
+    )
 
 
 def last_mixture_kernel(populations, mixture, twice, *refs):
@@ -337,13 +333,13 @@
     turned = (pltpu.VMEM((samples, 6 * rows), BF16),)
 
     alleles = gather_frequencies(frequencies)
-    alt = (observed * genotypes).astype(BF16)
-    ref = (observed * (2 - genotypes)).astype(BF16)
-
-    mix_zero, all_zero, prop, both = call(
+    alt = (observed * genotypes).astype(F32)
+    ref = (observed * (2 - genotypes)).astype(F32)
+
+    mix_zero, all_zero, twice_here, prop, both = call(
         first_kernel,
         "first",
-        (*state_out, *first_sums_out),
+        (*state_out, ((1, samples), F32), *first_sums_out),
         (proportions, alleles, alt, ref),
         turned,
     )
@@ -365,7 +361,7 @@
             functools.partial(step_kernel, populations),
             "step",
             (state_out[1], *sums_out),
-            (mixture, alleles, *parts_of(both, "samp"), alt, ref),
+            (mixture, alleles, twice_here, *parts_of(both, "samp"), alt, ref),
             turned,
         )
 
@@ -394,7 +390,10 @@
             functools.partial(leap_kernel, populations),
             "leap",
             (*state_out, *sums_out),
-            (mix_zero, all_zero, mix_one, all_one, mix_two, all_two, *tiles, alt, ref),
+            (
+                *(mix_zero, all_zero, mix_one, all_one, mix_two, all_two),
+                *(*tiles, twice_here, alt, ref),
+            ),
             turned,
         )
     (mixture,) = call(

time: 138 us -> 134 us (0.971)
  Pallas kernels: 28.8 us -> 25.5 us
    pallas_call x15, Pallas kernels: 28.8 us -> 25.5 us  [call(): pl.pallas_call(kernel, out_shape=tuple((jax.ShapeDtypeStruct(*out) for ou...]
where the time goes in v2:
time: 134 us
  starting transfers between devices  58.8 us (44%)
  waiting for transfers between devices  43 us (32%)
  Pallas kernels  25.5 us (19%)
  other arithmetic  5.86 us (4%)
    ppermute x47, starting transfers between devices, swap(): return lax.ppermute(value, axis, [(i, i ^ mask) for i in range(size)])  47.6 us
    ppermute x47, waiting for transfers between devices, swap(): return lax.ppermute(value, axis, [(i, i ^ mask) for i in range(size)])  38.1 us
    pallas_call x15, Pallas kernels, call(): pl.pallas_call(kernel, out_shape=tuple((jax.ShapeDtypeStruct(*out) for ou...  25.5 us
    ppermute x3, starting transfers between devices, gather_frequencies(): total = total + lax.ppermute(held, both, pairs)  7.35 us
    convert_element_type x1, other arithmetic, local(): ref = (observed * (2 - genotypes)).astype(F32)  4.96 us
    ppermute x3, waiting for transfers between devices, gather_frequencies(): arrived.append(lax.ppermute(frequencies, both, pairs))  4.93 us
    ppermute x3, starting transfers between devices, gather_frequencies(): arrived.append(lax.ppermute(frequencies, both, pairs))  3.88 us
  transfers between devices with their start and end apart: 53, of which 34 were waited for; matrix products, arithmetic and copies ran while one was open for 4% of the time, Pallas kernels for 1%

profile of v2, /device:TPU:0, one launch (start us, length us, event | category | flops | bytes accessed | tf_op | source)
XLA Modules:
  0.0 134.1 jit_solution(12765912037257896988)
XLA Ops:
  4.5 3.2 %collective-permute-done.1 = f32[10,128]{1,0:T(8,128)S(1)} collective-permute-done((f32[10,128]{1,0:T(8,128)}, f32[10,128]{1,0:T(8,128)S(1)}, u32[]{:S(2)}, u32[]{:S(2)}) %collective-permute-start.1) | collective-permute-done | bytes 5152 | tf_op jit(solution)/shard_map/ppermute | solution.py:71
  11.5 4.8 %collective-permute-start.6 = (f32[10,1024]{1,0:T(8,128)S(1)}, f32[10,1024]{1,0:T(8,128)S(1)}, u32[]{:S(2)}, u32[]{:S(2)}) collective-permute-start(f32[10,1024]{1,0:T(8,128)S(1)} %maximum_select_fusion), channel_id=1, source_target_pairs={{0,24},{4,28},{9,17},{13,21},{18,10},{22,14},{27,3},{31,7}} | collective-permute-start | bytes 122888 | tf_op jit(solution)/shard_map/ppermute | solution.py:94
  18.9 5.0 %multiply_convert_fusion = (f32[1024,1024]{1,0:T(8,128)S(1)}, f32[1024,1024]{1,0:T(8,128)S(1)}) fusion(s32[1024,1024]{1,0:T(8,128)} %param.5, s32[1024,1024]{1,0:T(8,128)} %param.4), kind=kLoop, calls=%fused_computation | loop fusion | flops 5242880 | bytes 16777216 | tf_op jit(solution)/shard_map/convert_element_type | solution.py:337
  23.9 4.4 %first.1 = (f32[16,1024]{1,0:T(8,128)S(1)}, f32[16,1024]{1,0:T(8,128)S(1)}, f32[1,1024]{1,0:T(1,128)S(1)}, f32[88,128]{1,0:T(8,128)S(1)}, f32[160,128]{1,0:T(8,128)S(1)}) custom-call(f32[10,1024]{1,0:T(8,128)S(1)} %copy-done, f32[10,1024]{1,0:T(8,128)S(1)} %add_add_fusion.alleles, f32[1024,1024]{1,0:T(8,128)S(1)} %get-tuple-element.67.alt.refs_2_.refs_11_, ...), custom_call_target="tpu_custom_call" | custom-call | tf_op jit(solution)/shard_map/first/pallas_call | solution.py:311
  31.8 2.3 %collective-permute-start.7 = (f32[88,128]{1,0:T(8,128)S(1)}, f32[88,128]{1,0:T(8,128)S(1)}, u32[]{:S(2)}, u32[]{:S(2)}) collective-permute-start(f32[88,128]{1,0:T(8,128)S(1)} %get-tuple-element.36.refs_0_), channel_id=1, source_target_pairs={{0,1},{1,0},{2,3},{3,2},{4,5},{5,4},{6,7},{7,6},{8,9},{9,8},{10,11... | collective-permute-start | bytes 135176 | tf_op jit(solution)/shard_map/ppermute | solution.py:35
  36.8 1.9 %collective-permute-done.12.refs_1_ = f32[160,128]{1,0:T(8,128)S(1)} collective-permute-done((f32[160,128]{1,0:T(8,128)S(1)}, f32[160,128]{1,0:T(8,128)S(1)}, u32[]{:S(2)}, u32[]{:S(2)}) %collective-permute-start.12) | collective-permute-done | bytes 81952 | tf_op jit(solution)/shard_map/ppermute | solution.py:35
  38.7 3.8 %step.3 = (f32[16,1024]{1,0:T(8,128)S(1)}, f32[80,128]{1,0:T(8,128)S(1)}, f32[160,128]{1,0:T(8,128)S(1)}) custom-call(f32[16,1024]{1,0:T(8,128)S(1)} %get-tuple-element.37.mixture.one.refs_2_, f32[16,1024]{1,0:T(8,128)S(1)} %get-tuple-element.35.alleles.zero.refs_1_, f32[1,1024]{1,0:T(1,128)S(1)} %get-tuple-element.38.twice_here.refs_10_, ...), custom_call_target="tpu_custom_call" | custom-call | tf_op jit(solution)/shard_map/step/pallas_call | solution.py:311
  43.8 2.0 %collective-permute-start.17 = (f32[160,128]{1,0:T(8,128)S(1)}, f32[160,128]{1,0:T(8,128)S(1)}, u32[]{:S(2)}, u32[]{:S(2)}) collective-permute-start(f32[160,128]{1,0:T(8,128)S(1)} %add.69), channel_id=1, source_target_pairs={{0,8},{4,12},{8,0},{12,4},{16,24},{20,28},{24,16},{28,20},{1,9},{5... | collective-permute-start | bytes 245768 | tf_op jit(solution)/shard_map/ppermute | solution.py:35
  47.2 2.9 %collective-permute-start.13 = (f32[80,128]{1,0:T(8,128)S(1)}, f32[80,128]{1,0:T(8,128)S(1)}, u32[]{:S(2)}, u32[]{:S(2)}) collective-permute-start(f32[80,128]{1,0:T(8,128)S(1)} %get-tuple-element.42.refs_0_), channel_id=1, source_target_pairs={{0,1},{1,0},{2,3},{3,2},{4,5},{5,4},{6,7},{7,6},{8,9},{9,8},{10,11... | collective-permute-start | bytes 122888 | tf_op jit(solution)/shard_map/ppermute | solution.py:35
  58.4 2.0 %collective-permute-start.23 = (f32[16,128]{1,0:T(8,128)S(1)}, f32[16,128]{1,0:T(8,128)S(1)}, u32[]{:S(2)}, u32[]{:S(2)}) collective-permute-start(f32[16,128]{1,0:T(8,128)S(1)} %add.73.refs_8_), channel_id=1, source_target_pairs={{0,2},{1,3},{2,0},{3,1},{4,6},{5,7},{6,4},{7,5},{8,10},{9,11},{10,... | collective-permute-start | bytes 24584 | tf_op jit(solution)/shard_map/ppermute | solution.py:35
  63.0 4.2 %leap.2 = (f32[16,1024]{1,0:T(8,128)S(1)}, f32[16,1024]{1,0:T(8,128)S(1)}, f32[80,128]{1,0:T(8,128)S(1)}, f32[160,128]{1,0:T(8,128)S(1)}) custom-call(f32[16,1024]{1,0:T(8,128)S(1)} %get-tuple-element.34.mixture.zero.refs_0_, f32[16,1024]{1,0:T(8,128)S(1)} %get-tuple-element.35.alleles.zero.refs_1_, f32[16,1024]{1,0:T(8,128)S(1)} %get-tuple-element.37.mixture.one.refs_2_, ...), custom_call_target="tpu_custom_call" | custom-call | tf_op jit(solution)/shard_map/leap/pallas_call | solution.py:311
  68.5 1.9 %collective-permute-start.28 = (f32[160,128]{1,0:T(8,128)S(1)}, f32[160,128]{1,0:T(8,128)S(1)}, u32[]{:S(2)}, u32[]{:S(2)}) collective-permute-start(f32[160,128]{1,0:T(8,128)S(1)} %add.74), channel_id=1, source_target_pairs={{0,8},{4,12},{8,0},{12,4},{16,24},{20,28},{24,16},{28,20},{1,9},{5... | collective-permute-start | bytes 245768 | tf_op jit(solution)/shard_map/ppermute | solution.py:35
  72.8 2.0 %collective-permute-start.24 = (f32[80,128]{1,0:T(8,128)S(1)}, f32[80,128]{1,0:T(8,128)S(1)}, u32[]{:S(2)}, u32[]{:S(2)}) collective-permute-start(f32[80,128]{1,0:T(8,128)S(1)} %get-tuple-element.49.refs_1_), channel_id=1, source_target_pairs={{0,1},{1,0},{2,3},{3,2},{4,5},{5,4},{6,7},{7,6},{8,9},{9,8},{10,11... | collective-permute-start | bytes 122888 | tf_op jit(solution)/shard_map/ppermute | solution.py:35
  77.5 1.9 %collective-permute-done.29.refs_1_ = f32[160,128]{1,0:T(8,128)S(1)} collective-permute-done((f32[160,128]{1,0:T(8,128)S(1)}, f32[160,128]{1,0:T(8,128)S(1)}, u32[]{:S(2)}, u32[]{:S(2)}) %collective-permute-start.29) | collective-permute-done | bytes 81952 | tf_op jit(solution)/shard_map/ppermute | solution.py:35
  79.4 3.8 %step.4 = (f32[16,1024]{1,0:T(8,128)S(1)}, f32[80,128]{1,0:T(8,128)S(1)}, f32[160,128]{1,0:T(8,128)S(1)}) custom-call(f32[16,1024]{1,0:T(8,128)S(1)} %mixture.6.zero.refs_0_, f32[16,1024]{1,0:T(8,128)S(1)} %get-tuple-element.50.alleles, f32[1,1024]{1,0:T(1,128)S(1)} %get-tuple-element.38.twice_here.refs_10_, f32[160,128]{1,0:T(8,128)S(1)} %add.75.refs_0_, ...), custom_call_target="tpu_custom_call" | custom-call | tf_op jit(solution)/shard_map/step/pallas_call | solution.py:311
  84.7 2.0 %collective-permute-start.32 = (f32[80,128]{1,0:T(8,128)S(1)}, f32[80,128]{1,0:T(8,128)S(1)}, u32[]{:S(2)}, u32[]{:S(2)}) collective-permute-start(f32[80,128]{1,0:T(8,128)S(1)} %get-tuple-element.53.refs_1_), channel_id=1, source_target_pairs={{0,3},{1,2},{2,1},{3,0},{4,7},{5,6},{6,5},{7,4},{8,11},{9,10},{10,... | collective-permute-start | bytes 122888 | tf_op jit(solution)/shard_map/ppermute | solution.py:35
  87.0 2.0 %collective-permute-start.30 = (f32[80,128]{1,0:T(8,128)S(1)}, f32[80,128]{1,0:T(8,128)S(1)}, u32[]{:S(2)}, u32[]{:S(2)}) collective-permute-start(f32[80,128]{1,0:T(8,128)S(1)} %get-tuple-element.53.refs_1_), channel_id=1, source_target_pairs={{0,1},{1,0},{2,3},{3,2},{4,5},{5,4},{6,7},{7,6},{8,9},{9,8},{10,11... | collective-permute-start | bytes 122888 | tf_op jit(solution)/shard_map/ppermute | solution.py:35
  89.1 2.1 %collective-permute-start.35 = (f32[160,128]{1,0:T(8,128)S(1)}, f32[160,128]{1,0:T(8,128)S(1)}, u32[]{:S(2)}, u32[]{:S(2)}) collective-permute-start(f32[160,128]{1,0:T(8,128)S(1)} %add.77.refs_0_), channel_id=1, source_target_pairs={{0,16},{4,20},{8,24},{12,28},{16,0},{20,4},{24,8},{28,12},{1,17},{... | collective-permute-start | bytes 245768 | tf_op jit(solution)/shard_map/ppermute | solution.py:35
  93.6 3.8 %step.5 = (f32[16,1024]{1,0:T(8,128)S(1)}, f32[80,128]{1,0:T(8,128)S(1)}, f32[160,128]{1,0:T(8,128)S(1)}) custom-call(f32[16,1024]{1,0:T(8,128)S(1)} %mixture.7.one.refs_2_, f32[16,1024]{1,0:T(8,128)S(1)} %get-tuple-element.52.alleles.zero.refs_1_, f32[1,1024]{1,0:T(1,128)S(1)} %get-tuple-element.38.twice_here.refs_10_, f32[160,128]{1,0:T(8,128)S(1)} %add.77.refs_0_, ...), custom_call_target="tpu_custom_call" | custom-call | tf_op jit(solution)/shard_map/step/pallas_call | solution.py:311
  98.7 1.9 %collective-permute-start.40 = (f32[160,128]{1,0:T(8,128)S(1)}, f32[160,128]{1,0:T(8,128)S(1)}, u32[]{:S(2)}, u32[]{:S(2)}) collective-permute-start(f32[160,128]{1,0:T(8,128)S(1)} %add.78), channel_id=1, source_target_pairs={{0,8},{4,12},{8,0},{12,4},{16,24},{20,28},{24,16},{28,20},{1,9},{5... | collective-permute-start | bytes 245768 | tf_op jit(solution)/shard_map/ppermute | solution.py:35
  102.2 2.8 %collective-permute-start.36 = (f32[80,128]{1,0:T(8,128)S(1)}, f32[80,128]{1,0:T(8,128)S(1)}, u32[]{:S(2)}, u32[]{:S(2)}) collective-permute-start(f32[80,128]{1,0:T(8,128)S(1)} %get-tuple-element.56.refs_0_), channel_id=1, source_target_pairs={{0,1},{1,0},{2,3},{3,2},{4,5},{5,4},{6,7},{7,6},{8,9},{9,8},{10,11... | collective-permute-start | bytes 122888 | tf_op jit(solution)/shard_map/ppermute | solution.py:35
  110.6 1.9 %collective-permute-done.43 = f32[16,128]{1,0:T(8,128)S(1)} collective-permute-done((f32[16,128]{1,0:T(8,128)S(1)}, f32[16,128]{1,0:T(8,128)S(1)}, u32[]{:S(2)}, u32[]{:S(2)}) %collective-permute-start.43) | collective-permute-done | bytes 8224 | tf_op jit(solution)/shard_map/ppermute | solution.py:35
  113.3 2.0 %collective-permute-start.46 = (f32[16,128]{1,0:T(8,128)S(1)}, f32[16,128]{1,0:T(8,128)S(1)}, u32[]{:S(2)}, u32[]{:S(2)}) collective-permute-start(f32[16,128]{1,0:T(8,128)S(1)} %add.82.refs_8_), channel_id=1, source_target_pairs={{0,2},{1,3},{2,0},{3,1},{4,6},{5,7},{6,4},{7,5},{8,10},{9,11},{10,... | collective-permute-start | bytes 24584 | tf_op jit(solution)/shard_map/ppermute | solution.py:35
  117.8 4.0 %leap.3 = (f32[16,1024]{1,0:T(8,128)S(1)}, f32[16,1024]{1,0:T(8,128)S(1)}, f32[80,128]{1,0:T(8,128)S(1)}, f32[160,128]{1,0:T(8,128)S(1)}) custom-call(f32[16,1024]{1,0:T(8,128)S(1)} %mixture.6.zero.refs_0_, f32[16,1024]{1,0:T(8,128)S(1)} %get-tuple-element.52.alleles.zero.refs_1_, f32[16,1024]{1,0:T(8,128)S(1)} %mixture.7.one.refs_2_, ...), custom_call_target="tpu_custom_call" | custom-call | tf_op jit(solution)/shard_map/leap/pallas_call | solution.py:311
  (123 shorter events, 64.5 us)
Async XLA Ops:
  0.6 7.2 %collective-permute-start.1 = (f32[10,128]{1,0:T(8,128)}, f32[10,128]{1,0:T(8,128)S(1)}, u32[]{:S(2)}, u32[]{:S(2)}) collective-permute-start(f32[10,128]{1,0:T(8,128)} %param.7), channel_id=1, source_target_pairs={{2,0},{6,4},{11,9},{15,13},{16,18},{20,22},{25,27},{29,31}} | collective-permute-start | bytes 15368 | tf_op jit(solution)/shard_map/ppermute | solution.py:71
  1.9 7.6 %collective-permute-start = (f32[10,128]{1,0:T(8,128)}, f32[10,128]{1,0:T(8,128)S(1)}, u32[]{:S(2)}, u32[]{:S(2)}) collective-permute-start(f32[10,128]{1,0:T(8,128)} %param.7), channel_id=1, source_target_pairs={{3,0},{7,4},{10,9},{14,13},{17,18},{21,22},{24,27},{28,31}} | collective-permute-start | bytes 15368 | tf_op jit(solution)/shard_map/ppermute | solution.py:71
  3.2 6.3 %collective-permute-start.2 = (f32[10,128]{1,0:T(8,128)}, f32[10,128]{1,0:T(8,128)S(1)}, u32[]{:S(2)}, u32[]{:S(2)}) collective-permute-start(f32[10,128]{1,0:T(8,128)} %param.7), channel_id=1, source_target_pairs={{1,0},{5,4},{8,9},{12,13},{19,18},{23,22},{26,27},{30,31}} | collective-permute-start | bytes 15368 | tf_op jit(solution)/shard_map/ppermute | solution.py:71
  11.5 12.4 %collective-permute-start.6 = (f32[10,1024]{1,0:T(8,128)S(1)}, f32[10,1024]{1,0:T(8,128)S(1)}, u32[]{:S(2)}, u32[]{:S(2)}) collective-permute-start(f32[10,1024]{1,0:T(8,128)S(1)} %maximum_select_fusion), channel_id=1, source_target_pairs={{0,24},{4,28},{9,17},{13,21},{18,10},{22,14},{27,3},{31,7}} | collective-permute-start | bytes 122888 | tf_op jit(solution)/shard_map/ppermute | solution.py:94
  16.3 7.6 %collective-permute-start.5 = (f32[10,1024]{1,0:T(8,128)S(1)}, f32[10,1024]{1,0:T(8,128)S(1)}, u32[]{:S(2)}, u32[]{:S(2)}) collective-permute-start(f32[10,1024]{1,0:T(8,128)S(1)} %maximum_select_fusion), channel_id=1, source_target_pairs={{0,16},{4,20},{9,25},{13,29},{18,2},{22,6},{27,11},{31,15}} | collective-permute-start | bytes 122888 | tf_op jit(solution)/shard_map/ppermute | solution.py:94
  17.6 6.3 %collective-permute-start.4 = (f32[10,1024]{1,0:T(8,128)S(1)}, f32[10,1024]{1,0:T(8,128)S(1)}, u32[]{:S(2)}, u32[]{:S(2)}) collective-permute-start(f32[10,1024]{1,0:T(8,128)S(1)} %maximum_select_fusion), channel_id=1, source_target_pairs={{0,8},{4,12},{9,1},{13,5},{18,26},{22,30},{27,19},{31,23}} | collective-permute-start | bytes 122888 | tf_op jit(solution)/shard_map/ppermute | solution.py:94
  29.7 6.4 %collective-permute-start.9 = (f32[88,128]{1,0:T(8,128)S(1)}, f32[88,128]{1,0:T(8,128)S(1)}, u32[]{:S(2)}, u32[]{:S(2)}) collective-permute-start(f32[88,128]{1,0:T(8,128)S(1)} %get-tuple-element.36.refs_0_), channel_id=1, source_target_pairs={{0,3},{1,2},{2,1},{3,0},{4,7},{5,6},{6,5},{7,4},{8,11},{9,10},{10,... | collective-permute-start | bytes 135176 | tf_op jit(solution)/shard_map/ppermute | solution.py:35
  30.5 6.3 %collective-permute-start.8 = (f32[88,128]{1,0:T(8,128)S(1)}, f32[88,128]{1,0:T(8,128)S(1)}, u32[]{:S(2)}, u32[]{:S(2)}) collective-permute-start(f32[88,128]{1,0:T(8,128)S(1)} %get-tuple-element.36.refs_0_), channel_id=1, source_target_pairs={{0,2},{1,3},{2,0},{3,1},{4,6},{5,7},{6,4},{7,5},{8,10},{9,11},{10,... | collective-permute-start | bytes 135176 | tf_op jit(solution)/shard_map/ppermute | solution.py:35
  43.8 6.4 %collective-permute-start.17 = (f32[160,128]{1,0:T(8,128)S(1)}, f32[160,128]{1,0:T(8,128)S(1)}, u32[]{:S(2)}, u32[]{:S(2)}) collective-permute-start(f32[160,128]{1,0:T(8,128)S(1)} %add.69), channel_id=1, source_target_pairs={{0,8},{4,12},{8,0},{12,4},{16,24},{20,28},{24,16},{28,20},{1,9},{5... | collective-permute-start | bytes 245768 | tf_op jit(solution)/shard_map/ppermute | solution.py:35
  45.8 6.2 %collective-permute-start.15 = (f32[80,128]{1,0:T(8,128)S(1)}, f32[80,128]{1,0:T(8,128)S(1)}, u32[]{:S(2)}, u32[]{:S(2)}) collective-permute-start(f32[80,128]{1,0:T(8,128)S(1)} %get-tuple-element.42.refs_0_), channel_id=1, source_target_pairs={{0,3},{1,2},{2,1},{3,0},{4,7},{5,6},{6,5},{7,4},{8,11},{9,10},{10,... | collective-permute-start | bytes 122888 | tf_op jit(solution)/shard_map/ppermute | solution.py:35
  46.5 6.0 %collective-permute-start.14 = (f32[80,128]{1,0:T(8,128)S(1)}, f32[80,128]{1,0:T(8,128)S(1)}, u32[]{:S(2)}, u32[]{:S(2)}) collective-permute-start(f32[80,128]{1,0:T(8,128)S(1)} %get-tuple-element.42.refs_0_), channel_id=1, source_target_pairs={{0,2},{1,3},{2,0},{3,1},{4,6},{5,7},{6,4},{7,5},{8,10},{9,11},{10,... | collective-permute-start | bytes 122888 | tf_op jit(solution)/shard_map/ppermute | solution.py:35
  47.2 5.3 %collective-permute-start.13 = (f32[80,128]{1,0:T(8,128)S(1)}, f32[80,128]{1,0:T(8,128)S(1)}, u32[]{:S(2)}, u32[]{:S(2)}) collective-permute-start(f32[80,128]{1,0:T(8,128)S(1)} %get-tuple-element.42.refs_0_), channel_id=1, source_target_pairs={{0,1},{1,0},{2,3},{3,2},{4,5},{5,4},{6,7},{7,6},{8,9},{9,8},{10,11... | collective-permute-start | bytes 122888 | tf_op jit(solution)/shard_map/ppermute | solution.py:35
  68.5 6.3 %collective-permute-start.28 = (f32[160,128]{1,0:T(8,128)S(1)}, f32[160,128]{1,0:T(8,128)S(1)}, u32[]{:S(2)}, u32[]{:S(2)}) collective-permute-start(f32[160,128]{1,0:T(8,128)S(1)} %add.74), channel_id=1, source_target_pairs={{0,8},{4,12},{8,0},{12,4},{16,24},{20,28},{24,16},{28,20},{1,9},{5... | collective-permute-start | bytes 245768 | tf_op jit(solution)/shard_map/ppermute | solution.py:35
  70.4 6.2 %collective-permute-start.26 = (f32[80,128]{1,0:T(8,128)S(1)}, f32[80,128]{1,0:T(8,128)S(1)}, u32[]{:S(2)}, u32[]{:S(2)}) collective-permute-start(f32[80,128]{1,0:T(8,128)S(1)} %get-tuple-element.49.refs_1_), channel_id=1, source_target_pairs={{0,3},{1,2},{2,1},{3,0},{4,7},{5,6},{6,5},{7,4},{8,11},{9,10},{10,... | collective-permute-start | bytes 122888 | tf_op jit(solution)/shard_map/ppermute | solution.py:35
  72.0 5.4 %collective-permute-start.25 = (f32[80,128]{1,0:T(8,128)S(1)}, f32[80,128]{1,0:T(8,128)S(1)}, u32[]{:S(2)}, u32[]{:S(2)}) collective-permute-start(f32[80,128]{1,0:T(8,128)S(1)} %get-tuple-element.49.refs_1_), channel_id=1, source_target_pairs={{0,2},{1,3},{2,0},{3,1},{4,6},{5,7},{6,4},{7,5},{8,10},{9,11},{10,... | collective-permute-start | bytes 122888 | tf_op jit(solution)/shard_map/ppermute | solution.py:35
  84.7 6.5 %collective-permute-start.32 = (f32[80,128]{1,0:T(8,128)S(1)}, f32[80,128]{1,0:T(8,128)S(1)}, u32[]{:S(2)}, u32[]{:S(2)}) collective-permute-start(f32[80,128]{1,0:T(8,128)S(1)} %get-tuple-element.53.refs_1_), channel_id=1, source_target_pairs={{0,3},{1,2},{2,1},{3,0},{4,7},{5,6},{6,5},{7,4},{8,11},{9,10},{10,... | collective-permute-start | bytes 122888 | tf_op jit(solution)/shard_map/ppermute | solution.py:35
  86.6 5.3 %collective-permute-start.31 = (f32[80,128]{1,0:T(8,128)S(1)}, f32[80,128]{1,0:T(8,128)S(1)}, u32[]{:S(2)}, u32[]{:S(2)}) collective-permute-start(f32[80,128]{1,0:T(8,128)S(1)} %get-tuple-element.53.refs_1_), channel_id=1, source_target_pairs={{0,2},{1,3},{2,0},{3,1},{4,6},{5,7},{6,4},{7,5},{8,10},{9,11},{10,... | collective-permute-start | bytes 122888 | tf_op jit(solution)/shard_map/ppermute | solution.py:35
  98.7 6.3 %collective-permute-start.40 = (f32[160,128]{1,0:T(8,128)S(1)}, f32[160,128]{1,0:T(8,128)S(1)}, u32[]{:S(2)}, u32[]{:S(2)}) collective-permute-start(f32[160,128]{1,0:T(8,128)S(1)} %add.78), channel_id=1, source_target_pairs={{0,8},{4,12},{8,0},{12,4},{16,24},{20,28},{24,16},{28,20},{1,9},{5... | collective-permute-start | bytes 245768 | tf_op jit(solution)/shard_map/ppermute | solution.py:35
  100.6 5.8 %collective-permute-start.38 = (f32[80,128]{1,0:T(8,128)S(1)}, f32[80,128]{1,0:T(8,128)S(1)}, u32[]{:S(2)}, u32[]{:S(2)}) collective-permute-start(f32[80,128]{1,0:T(8,128)S(1)} %get-tuple-element.56.refs_0_), channel_id=1, source_target_pairs={{0,3},{1,2},{2,1},{3,0},{4,7},{5,6},{6,5},{7,4},{8,11},{9,10},{10,... | collective-permute-start | bytes 122888 | tf_op jit(solution)/shard_map/ppermute | solution.py:35
  102.2 5.4 %collective-permute-start.37 = (f32[80,128]{1,0:T(8,128)S(1)}, f32[80,128]{1,0:T(8,128)S(1)}, u32[]{:S(2)}, u32[]{:S(2)}) collective-permute-start(f32[80,128]{1,0:T(8,128)S(1)} %get-tuple-element.56.refs_0_), channel_id=1, source_target_pairs={{0,2},{1,3},{2,0},{3,1},{4,6},{5,7},{6,4},{7,5},{8,10},{9,11},{10,... | collective-permute-start | bytes 122888 | tf_op jit(solution)/shard_map/ppermute | solution.py:35
  102.2 5.4 %collective-permute-start.36 = (f32[80,128]{1,0:T(8,128)S(1)}, f32[80,128]{1,0:T(8,128)S(1)}, u32[]{:S(2)}, u32[]{:S(2)}) collective-permute-start(f32[80,128]{1,0:T(8,128)S(1)} %get-tuple-element.56.refs_0_), channel_id=1, source_target_pairs={{0,1},{1,0},{2,3},{3,2},{4,5},{5,4},{6,7},{7,6},{8,9},{9,8},{10,11... | collective-permute-start | bytes 122888 | tf_op jit(solution)/shard_map/ppermute | solution.py:35
  123.2 5.8 %collective-permute-start.51 = (f32[160,128]{1,0:T(8,128)S(1)}, f32[160,128]{1,0:T(8,128)S(1)}, u32[]{:S(2)}, u32[]{:S(2)}) collective-permute-start(f32[160,128]{1,0:T(8,128)S(1)} %add.83), channel_id=1, source_target_pairs={{0,8},{4,12},{8,0},{12,4},{16,24},{20,28},{24,16},{28,20},{1,9},{5... | collective-permute-start | bytes 245768 | tf_op jit(solution)/shard_map/ppermute | solution.py:35
  124.6 5.8 %collective-permute-start.49 = (f32[80,128]{1,0:T(8,128)S(1)}, f32[80,128]{1,0:T(8,128)S(1)}, u32[]{:S(2)}, u32[]{:S(2)}) collective-permute-start(f32[80,128]{1,0:T(8,128)S(1)} %get-tuple-element.63.refs_0_), channel_id=1, source_target_pairs={{0,3},{1,2},{2,1},{3,0},{4,7},{5,6},{6,5},{7,4},{8,11},{9,10},{10,... | collective-permute-start | bytes 122888 | tf_op jit(solution)/shard_map/ppermute | solution.py:35
  126.4 5.6 %collective-permute-start.48 = (f32[80,128]{1,0:T(8,128)S(1)}, f32[80,128]{1,0:T(8,128)S(1)}, u32[]{:S(2)}, u32[]{:S(2)}) collective-permute-start(f32[80,128]{1,0:T(8,128)S(1)} %get-tuple-element.63.refs_0_), channel_id=1, source_target_pairs={{0,2},{1,3},{2,0},{3,1},{4,6},{5,7},{6,4},{7,5},{8,10},{9,11},{10,... | collective-permute-start | bytes 122888 | tf_op jit(solution)/shard_map/ppermute | solution.py:35
  (30 other events, 110.4 us)

commit v3 on v2

--- a/solution.py
+++ b/solution.py
@@ -14,9 +14,10 @@
 BF16 = jnp.bfloat16
 SUBLANES = 8
 LANES = 128
-VMEM_BYTES = 40 * 2**20
+VMEM_BYTES = 32 * 2**20
 TALL, WIDE = 512, 512
 MIXTURE_COST = 5 * 10**9
+ALLELES_COST = 5 * 10**9
 
 
 def clip_unit(values):
@@ -56,34 +57,37 @@
     return value, swap(value, axis, strides[-1])
 
 
-def gather_frequencies(frequencies):
+def gather_flags():
     samp_count, var_count = lax.axis_size("samp"), lax.axis_size("var")
     group = samp_count // var_count
     samp, var = lax.axis_index("samp"), lax.axis_index("var")
-    owner = samp // group
+    var_bits = [(var & stride) != 0 for stride in strides_of("var")]
+    samp_bits = [(samp & stride) != 0 for stride in strides_of("samp") if stride < group]
+    return samp // group == var, var_bits, samp_bits
+
+
+def gather_frequencies(frequencies, flags):
+    owns, var_bits, samp_bits = flags
+    samp_count, var_count = lax.axis_size("samp"), lax.axis_size("var")
+    group = samp_count // var_count
     both = ("samp", "var")
-    arrived = [jnp.where(owner == var, frequencies, 0.0)]
+    arrived = []
     for mask in range(1, var_count):
         pairs = [
             (s * var_count + ((s // group) ^ mask), s * var_count + s // group)
             for s in range(samp_count)
         ]
         arrived.append(lax.ppermute(frequencies, both, pairs))
-    stride = 1
-    while stride < var_count:
-        flip = (var & stride) != 0
-        arrived = [jnp.where(flip, arrived[i ^ stride], arrived[i]) for i in range(var_count)]
-        stride *= 2
+    arrived = [jnp.where(owns, frequencies, 0.0)] + arrived
+    for bit, flip in enumerate(var_bits):
+        arrived = [jnp.where(flip, arrived[i ^ (1 << bit)], arrived[i]) for i in range(var_count)]
     held = jnp.concatenate(arrived, axis=1)
-    stride = 1
-    while stride < group:
-        other = swap(held, "samp", stride)
-        upper = (samp & stride) != 0
+    for bit, upper in enumerate(samp_bits):
+        other = swap(held, "samp", 1 << bit)
         held = jnp.concatenate(
             [jnp.where(upper, other, held), jnp.where(upper, held, other)], axis=1
         )
-        stride *= 2
-    held = jnp.where(owner == var, held, 0.0)
+    held = jnp.where(owns, held, 0.0)
     total = held
     for mask in range(1, var_count):
         pairs = [
@@ -200,8 +204,32 @@
     return pad_rows(moved, alleles.shape[0])
 
 
+def prepare_kernel(genotypes, observed, alt_out, ref_out, twice_out, landed, arrivals):
+    samples, variants = genotypes.shape
+    tall = samples // arrivals.shape[1]
+    copies = []
+    for index, top in enumerate(range(0, samples, tall)):
+        here = pl.ds(top, tall)
+        for place, source in enumerate((genotypes, observed)):
+            copy = pltpu.make_async_copy(
+                source.at[here, :], landed.at[place, here, :], arrivals.at[place, index]
+            )
+            copy.start()
+            copies.append(copy)
+    ones = jnp.ones((SUBLANES, variants), BF16)
+    for index, top in enumerate(range(0, samples, tall)):
+        here = slice(top, top + tall)
+        copies[2 * index].wait()
+        copies[2 * index + 1].wait()
+        seen = landed[1, here, :].astype(F32)
+        alt = seen * landed[0, here, :].astype(F32)
+        alt_out[here, :] = alt
+        ref_out[here, :] = 2.0 * seen - alt
+        twice_out[:, here] = 2.0 * dot(ones, seen.astype(BF16), 1, 1)[:1]
+
+
 def first_kernel(
-    mixture, alleles, alt, ref, mixture_out, alleles_out, twice_out, prop_out, both_out, turned
+    mixture, alleles, twice_here, alt, ref, mixture_out, alleles_out, prop_out, both_out, turned
 ):
     populations = mixture.shape[0]
     rows = mixture_out.shape[0]
@@ -209,10 +237,9 @@
     current = pad_rows(alleles[...], rows)
     mixture_out[...] = mix
     alleles_out[...] = current
-    ones = jnp.ones((SUBLANES, alt.shape[1]), BF16)
-    twice = dot(ones, (alt[...] + ref[...]).astype(BF16), 1, 1)[:1]
-    twice_out[...] = twice
-    expectation(populations, mix, current, twice, alt, ref, prop_out, both_out, turned)
+    expectation(
+        populations, mix, current, twice_here[...], alt, ref, prop_out, both_out, turned
+    )
 
 
 def mixture_kernel(populations, with_twice, mixture, *refs):
@@ -294,20 +321,15 @@
     )
 
 
-def last_mixture_kernel(populations, mixture, twice, *refs):
-    prop_parts, (out,) = split_refs(refs, len(refs) - 1)
-    mix, _ = next_mixture(populations, mixture[...], twice[...], prop_parts)
-    out[...] = mix[:populations]
-
-
-def last_alleles_kernel(populations, alleles, *refs):
-    both_parts, (out,) = split_refs(refs, 2)
-    out[...] = next_alleles(populations, alleles[...], both_parts)[:populations]
-
-
-def call(kernel, name, outs, args, scratch=(), moved=0):
+def last_kernel(populations, mixture, alleles, *refs):
+    both_parts, (mixture_out, alleles_out) = split_refs(refs, 2)
+    mixture_out[...] = mixture[:populations, :]
+    alleles_out[...] = next_alleles(populations, alleles[...], both_parts)[:populations]
+
+
+def call(kernel, name, outs, args, scratch=(), flops=0):
     whole = pl.BlockSpec(memory_space=pltpu.VMEM)
-    cost = pl.CostEstimate(flops=moved, bytes_accessed=0, transcendentals=0) if moved else None
+    cost = pl.CostEstimate(flops=flops, bytes_accessed=0, transcendentals=0) if flops else None
     return pl.pallas_call(
         kernel,
         out_shape=tuple(jax.ShapeDtypeStruct(*out) for out in outs),
@@ -332,15 +354,35 @@
     tile_out = ((2 * SUBLANES, LANES), F32)
     turned = (pltpu.VMEM((samples, 6 * rows), BF16),)
 
-    alleles = gather_frequencies(frequencies)
-    alt = (observed * genotypes).astype(F32)
-    ref = (observed * (2 - genotypes)).astype(F32)
-
-    mix_zero, all_zero, twice_here, prop, both = call(
+    chunks = samples // blocks_of(samples, 128)
+    flags, genotypes, observed = lax.optimization_barrier((gather_flags(), genotypes, observed))
+    in_place = [
+        pltpu.with_memory_space_constraint(array, pltpu.HBM) for array in (genotypes, observed)
+    ]
+    whole = pl.BlockSpec(memory_space=pltpu.VMEM)
+    alt, ref, twice_here = pl.pallas_call(
+        prepare_kernel,
+        out_shape=(
+            pltpu.VMEM((samples, variants), F32),
+            pltpu.VMEM((samples, variants), F32),
+            jax.ShapeDtypeStruct((1, samples), F32),
+        ),
+        in_specs=[pl.BlockSpec(memory_space=pltpu.HBM)] * 2,
+        out_specs=(whole,) * 3,
+        scratch_shapes=[
+            pltpu.VMEM((2, samples, variants), jnp.int32),
+            pltpu.SemaphoreType.DMA((2, chunks)),
+        ],
+        compiler_params=pltpu.CompilerParams(vmem_limit_bytes=VMEM_BYTES),
+        name="prepare",
+    )(*in_place)
+    alleles = gather_frequencies(frequencies, flags)
+
+    mix_zero, all_zero, prop, both = call(
         first_kernel,
         "first",
-        (*state_out, ((1, samples), F32), *first_sums_out),
-        (proportions, alleles, alt, ref),
+        (*state_out, *first_sums_out),
+        (proportions, alleles, twice_here, alt, ref),
         turned,
     )
 
@@ -352,7 +394,7 @@
             "mixture",
             (state_out[0], *extra),
             (mixture, *known, *all_parts_of(prop, "var")),
-            moved=MIXTURE_COST,
+            flops=MIXTURE_COST,
         )
         return out[0], (known or out[1:])[0]
 
@@ -377,13 +419,14 @@
             "mixture_square",
             (state_out[0], tile_out),
             (mix_zero, mix_one, twice, *all_parts_of(prop, "var")),
-            moved=MIXTURE_COST,
+            flops=MIXTURE_COST,
         )
         all_two, all_tile = call(
             functools.partial(alleles_square_kernel, populations),
             "alleles_square",
             (state_out[1], tile_out),
             (all_zero, all_one, *parts_of(both, "samp")),
+            flops=ALLELES_COST,
         )
         tiles = (*parts_of(mix_tile, "samp"), *parts_of(all_tile, "var"))
         mix_zero, all_zero, prop, both = call(
@@ -396,20 +439,13 @@
             ),
             turned,
         )
-    (mixture,) = call(
-        functools.partial(last_mixture_kernel, populations),
-        "last_mixture",
-        (((populations, samples), F32),),
-        (mix_zero, twice, *all_parts_of(prop, "var")),
-        moved=MIXTURE_COST,
-    )
-    (alleles,) = call(
-        functools.partial(last_alleles_kernel, populations),
-        "last_alleles",
-        (((populations, variants), F32),),
-        (all_zero, *parts_of(both, "samp")),
-    )
-    return mixture, alleles
+    mixture, _ = moved_mixture(mix_zero, twice, prop)
+    return call(
+        functools.partial(last_kernel, populations),
+        "last",
+        (((populations, samples), F32), ((populations, variants), F32)),
+        (mixture, all_zero, *parts_of(both, "samp")),
+    )
 
 
 def solution(mesh):

time: 134 us -> 133 us (level)
  other arithmetic: 5.86 us -> 0.9 us
  Pallas kernels: 25.5 us -> 27.9 us
    convert_element_type x1 -> x0, other arithmetic: 4.96 us -> none  [local(): ref = (observed * (2 - genotypes)).astype(F32)]
    pallas_call x0 -> x1, Pallas kernels: none -> 3.79 us  [local(): pl.pallas_call(prepare_kernel, out_shape=(pltpu.VMEM((samples, variants),...]
    pallas_call x15, Pallas kernels: 25.5 us -> 24.1 us  [call(): pl.pallas_call(kernel, out_shape=tuple((jax.ShapeDtypeStruct(*out) for ou...]
  transfers between devices with their start and end apart: 53 -> 53, of which waited for: 34 -> 34; matrix products, arithmetic and copies ran while one was open for 4% -> 0% of each run, Pallas kernels for 1% -> 3%
where the time goes in v3:
time: 133 us; the launch traced here: 132 us
  starting transfers between devices  59.9 us (45%)
  waiting for transfers between devices  42.7 us (32%)
  Pallas kernels  27.9 us (21%)
    ppermute x47, starting transfers between devices, swap(): return lax.ppermute(value, axis, [(i, i ^ mask) for i in range(size)])  48.7 us
    ppermute x47, waiting for transfers between devices, swap(): return lax.ppermute(value, axis, [(i, i ^ mask) for i in range(size)])  37.7 us
    pallas_call x15, Pallas kernels, call(): pl.pallas_call(kernel, out_shape=tuple((jax.ShapeDtypeStruct(*out) for ou...  24.1 us
    ppermute x3, starting transfers between devices, gather_frequencies(): total = total + lax.ppermute(held, both, pairs)  7.35 us
    ppermute x3, waiting for transfers between devices, gather_frequencies(): arrived.append(lax.ppermute(frequencies, both, pairs))  4.93 us
    ppermute x3, starting transfers between devices, gather_frequencies(): arrived.append(lax.ppermute(frequencies, both, pairs))  3.88 us
    pallas_call x1, Pallas kernels, local(): pl.pallas_call(prepare_kernel, out_shape=(pltpu.VMEM((samples, variants),...  3.79 us
  transfers between devices with their start and end apart: 53, of which 34 were waited for; matrix products, arithmetic and copies ran while one was open for 0% of the time, Pallas kernels for 3%

profile of v3, /device:TPU:0, one launch (start us, length us, event | category | flops | bytes accessed | tf_op | source)
XLA Modules:
  0.0 132.3 jit_solution(3984757612878481075)
XLA Ops:
  4.5 3.2 %collective-permute-done.1 = f32[10,128]{1,0:T(8,128)S(1)} collective-permute-done((f32[10,128]{1,0:T(8,128)}, f32[10,128]{1,0:T(8,128)S(1)}, u32[]{:S(2)}, u32[]{:S(2)}) %collective-permute-start.1) | collective-permute-done | bytes 5152 | tf_op jit(solution)/shard_map/ppermute | solution.py:80
  7.8 1.7 %collective-permute-done = f32[10,128]{1,0:T(8,128)S(1)} collective-permute-done((f32[10,128]{1,0:T(8,128)}, f32[10,128]{1,0:T(8,128)S(1)}, u32[]{:S(2)}, u32[]{:S(2)}) %collective-permute-start) | collective-permute-done | bytes 5152 | tf_op jit(solution)/shard_map/ppermute | solution.py:80
  11.5 4.8 %collective-permute-start.6 = (f32[10,1024]{1,0:T(8,128)S(1)}, f32[10,1024]{1,0:T(8,128)S(1)}, u32[]{:S(2)}, u32[]{:S(2)}) collective-permute-start(f32[10,1024]{1,0:T(8,128)S(1)} %maximum_select_fusion), channel_id=1, source_target_pairs={{0,24},{4,28},{9,17},{13,21},{18,10},{22,14},{27,3},{31,7}} | collective-permute-start | bytes 122888 | tf_op jit(solution)/shard_map/ppermute | solution.py:98
  18.9 3.8 %prepare.1 = (f32[1024,1024]{1,0:T(8,128)S(1)}, f32[1024,1024]{1,0:T(8,128)S(1)}, f32[1,1024]{1,0:T(1,128)S(1)}) custom-call(s32[1024,1024]{1,0:T(8,128)} %genotypes, s32[1024,1024]{1,0:T(8,128)} %observed), custom_call_target="tpu_custom_call" | custom-call | tf_op jit(solution)/shard_map/prepare/pallas_call | solution.py:363
  22.8 3.8 %first.1 = (f32[16,1024]{1,0:T(8,128)S(1)}, f32[16,1024]{1,0:T(8,128)S(1)}, f32[88,128]{1,0:T(8,128)S(1)}, f32[160,128]{1,0:T(8,128)S(1)}) custom-call(f32[10,1024]{1,0:T(8,128)S(1)} %copy-done, f32[10,1024]{1,0:T(8,128)S(1)} %add_add_fusion.alleles, f32[1,1024]{1,0:T(1,128)S(1)} %get-tuple-element.48.twice_here.refs_10_, ...), custom_call_target="tpu_custom_call" | custom-call | tf_op jit(solution)/shard_map/first/pallas_call | solution.py:333
  30.0 2.7 %collective-permute-start.7 = (f32[88,128]{1,0:T(8,128)S(1)}, f32[88,128]{1,0:T(8,128)S(1)}, u32[]{:S(2)}, u32[]{:S(2)}) collective-permute-start(f32[88,128]{1,0:T(8,128)S(1)} %get-tuple-element.53.refs_0_), channel_id=1, source_target_pairs={{0,1},{1,0},{2,3},{3,2},{4,5},{5,4},{6,7},{7,6},{8,9},{9,8},{10,11... | collective-permute-start | bytes 135176 | tf_op jit(solution)/shard_map/ppermute | solution.py:36
  35.5 1.7 %collective-permute-done.12.refs_1_ = f32[160,128]{1,0:T(8,128)S(1)} collective-permute-done((f32[160,128]{1,0:T(8,128)S(1)}, f32[160,128]{1,0:T(8,128)S(1)}, u32[]{:S(2)}, u32[]{:S(2)}) %collective-permute-start.12) | collective-permute-done | bytes 81952 | tf_op jit(solution)/shard_map/ppermute | solution.py:36
  37.2 3.8 %step.3 = (f32[16,1024]{1,0:T(8,128)S(1)}, f32[80,128]{1,0:T(8,128)S(1)}, f32[160,128]{1,0:T(8,128)S(1)}) custom-call(f32[16,1024]{1,0:T(8,128)S(1)} %get-tuple-element.54.mixture.one.refs_2_, f32[16,1024]{1,0:T(8,128)S(1)} %get-tuple-element.52.alleles.zero.refs_1_, f32[1,1024]{1,0:T(1,128)S(1)} %get-tuple-element.48.twice_here.refs_10_, ...), custom_call_target="tpu_custom_call" | custom-call | tf_op jit(solution)/shard_map/step/pallas_call | solution.py:333
  42.3 1.7 %collective-permute-start.17 = (f32[160,128]{1,0:T(8,128)S(1)}, f32[160,128]{1,0:T(8,128)S(1)}, u32[]{:S(2)}, u32[]{:S(2)}) collective-permute-start(f32[160,128]{1,0:T(8,128)S(1)} %add.69), channel_id=1, source_target_pairs={{0,8},{4,12},{8,0},{12,4},{16,24},{20,28},{24,16},{28,20},{1,9},{5... | collective-permute-start | bytes 245768 | tf_op jit(solution)/shard_map/ppermute | solution.py:36
  45.4 2.9 %collective-permute-start.13 = (f32[80,128]{1,0:T(8,128)S(1)}, f32[80,128]{1,0:T(8,128)S(1)}, u32[]{:S(2)}, u32[]{:S(2)}) collective-permute-start(f32[80,128]{1,0:T(8,128)S(1)} %get-tuple-element.58.refs_0_), channel_id=1, source_target_pairs={{0,1},{1,0},{2,3},{3,2},{4,5},{5,4},{6,7},{7,6},{8,9},{9,8},{10,11... | collective-permute-start | bytes 122888 | tf_op jit(solution)/shard_map/ppermute | solution.py:36
  57.1 2.0 %collective-permute-start.23 = (f32[16,128]{1,0:T(8,128)S(1)}, f32[16,128]{1,0:T(8,128)S(1)}, u32[]{:S(2)}, u32[]{:S(2)}) collective-permute-start(f32[16,128]{1,0:T(8,128)S(1)} %add.73.refs_8_), channel_id=1, source_target_pairs={{0,2},{1,3},{2,0},{3,1},{4,6},{5,7},{6,4},{7,5},{8,10},{9,11},{10,... | collective-permute-start | bytes 24584 | tf_op jit(solution)/shard_map/ppermute | solution.py:36
  59.5 2.2 %collective-permute-done.23.refs_9_ = f32[16,128]{1,0:T(8,128)S(1)} collective-permute-done((f32[16,128]{1,0:T(8,128)S(1)}, f32[16,128]{1,0:T(8,128)S(1)}, u32[]{:S(2)}, u32[]{:S(2)}) %collective-permute-start.23) | collective-permute-done | bytes 8224 | tf_op jit(solution)/shard_map/ppermute | solution.py:36
  61.7 4.0 %leap.2 = (f32[16,1024]{1,0:T(8,128)S(1)}, f32[16,1024]{1,0:T(8,128)S(1)}, f32[80,128]{1,0:T(8,128)S(1)}, f32[160,128]{1,0:T(8,128)S(1)}) custom-call(f32[16,1024]{1,0:T(8,128)S(1)} %get-tuple-element.51.mixture.zero.refs_0_, f32[16,1024]{1,0:T(8,128)S(1)} %get-tuple-element.52.alleles.zero.refs_1_, f32[16,1024]{1,0:T(8,128)S(1)} %get-tuple-element.54.mixture.one.refs_2_, ...), custom_call_target="tpu_custom_call" | custom-call | tf_op jit(solution)/shard_map/leap/pallas_call | solution.py:333
  71.0 2.0 %collective-permute-start.24 = (f32[80,128]{1,0:T(8,128)S(1)}, f32[80,128]{1,0:T(8,128)S(1)}, u32[]{:S(2)}, u32[]{:S(2)}) collective-permute-start(f32[80,128]{1,0:T(8,128)S(1)} %get-tuple-element.65.refs_1_), channel_id=1, source_target_pairs={{0,1},{1,0},{2,3},{3,2},{4,5},{5,4},{6,7},{7,6},{8,9},{9,8},{10,11... | collective-permute-start | bytes 122888 | tf_op jit(solution)/shard_map/ppermute | solution.py:36
  75.6 1.9 %collective-permute-done.29.refs_1_ = f32[160,128]{1,0:T(8,128)S(1)} collective-permute-done((f32[160,128]{1,0:T(8,128)S(1)}, f32[160,128]{1,0:T(8,128)S(1)}, u32[]{:S(2)}, u32[]{:S(2)}) %collective-permute-start.29) | collective-permute-done | bytes 81952 | tf_op jit(solution)/shard_map/ppermute | solution.py:36
  77.5 3.8 %step.4 = (f32[16,1024]{1,0:T(8,128)S(1)}, f32[80,128]{1,0:T(8,128)S(1)}, f32[160,128]{1,0:T(8,128)S(1)}) custom-call(f32[16,1024]{1,0:T(8,128)S(1)} %mixture.7.zero.refs_0_, f32[16,1024]{1,0:T(8,128)S(1)} %get-tuple-element.66.alleles, f32[1,1024]{1,0:T(1,128)S(1)} %get-tuple-element.48.twice_here.refs_10_, f32[160,128]{1,0:T(8,128)S(1)} %add.75.refs_0_, ...), custom_call_target="tpu_custom_call" | custom-call | tf_op jit(solution)/shard_map/step/pallas_call | solution.py:333
  85.2 2.5 %collective-permute-start.30 = (f32[80,128]{1,0:T(8,128)S(1)}, f32[80,128]{1,0:T(8,128)S(1)}, u32[]{:S(2)}, u32[]{:S(2)}) collective-permute-start(f32[80,128]{1,0:T(8,128)S(1)} %get-tuple-element.69.refs_1_), channel_id=1, source_target_pairs={{0,1},{1,0},{2,3},{3,2},{4,5},{5,4},{6,7},{7,6},{8,9},{9,8},{10,11... | collective-permute-start | bytes 122888 | tf_op jit(solution)/shard_map/ppermute | solution.py:36
  90.2 2.0 %collective-permute-done.35.refs_1_ = f32[160,128]{1,0:T(8,128)S(1)} collective-permute-done((f32[160,128]{1,0:T(8,128)S(1)}, f32[160,128]{1,0:T(8,128)S(1)}, u32[]{:S(2)}, u32[]{:S(2)}) %collective-permute-start.35) | collective-permute-done | bytes 81952 | tf_op jit(solution)/shard_map/ppermute | solution.py:36
  92.2 3.8 %step.5 = (f32[16,1024]{1,0:T(8,128)S(1)}, f32[80,128]{1,0:T(8,128)S(1)}, f32[160,128]{1,0:T(8,128)S(1)}) custom-call(f32[16,1024]{1,0:T(8,128)S(1)} %mixture.8.one.refs_2_, f32[16,1024]{1,0:T(8,128)S(1)} %get-tuple-element.68.alleles.zero.refs_1_, f32[1,1024]{1,0:T(1,128)S(1)} %get-tuple-element.48.twice_here.refs_10_, f32[160,128]{1,0:T(8,128)S(1)} %add.77.refs_0_, ...), custom_call_target="tpu_custom_call" | custom-call | tf_op jit(solution)/shard_map/step/pallas_call | solution.py:333
  100.3 2.8 %collective-permute-start.36 = (f32[80,128]{1,0:T(8,128)S(1)}, f32[80,128]{1,0:T(8,128)S(1)}, u32[]{:S(2)}, u32[]{:S(2)}) collective-permute-start(f32[80,128]{1,0:T(8,128)S(1)} %get-tuple-element.72.refs_0_), channel_id=1, source_target_pairs={{0,1},{1,0},{2,3},{3,2},{4,5},{5,4},{6,7},{7,6},{8,9},{9,8},{10,11... | collective-permute-start | bytes 122888 | tf_op jit(solution)/shard_map/ppermute | solution.py:36
  111.4 2.0 %collective-permute-start.46 = (f32[16,128]{1,0:T(8,128)S(1)}, f32[16,128]{1,0:T(8,128)S(1)}, u32[]{:S(2)}, u32[]{:S(2)}) collective-permute-start(f32[16,128]{1,0:T(8,128)S(1)} %add.82.refs_8_), channel_id=1, source_target_pairs={{0,2},{1,3},{2,0},{3,1},{4,6},{5,7},{6,4},{7,5},{8,10},{9,11},{10,... | collective-permute-start | bytes 24584 | tf_op jit(solution)/shard_map/ppermute | solution.py:36
  114.3 1.7 %collective-permute-done.46.refs_9_ = f32[16,128]{1,0:T(8,128)S(1)} collective-permute-done((f32[16,128]{1,0:T(8,128)S(1)}, f32[16,128]{1,0:T(8,128)S(1)}, u32[]{:S(2)}, u32[]{:S(2)}) %collective-permute-start.46) | collective-permute-done | bytes 8224 | tf_op jit(solution)/shard_map/ppermute | solution.py:36
  116.0 4.0 %leap.3 = (f32[16,1024]{1,0:T(8,128)S(1)}, f32[16,1024]{1,0:T(8,128)S(1)}, f32[80,128]{1,0:T(8,128)S(1)}, f32[160,128]{1,0:T(8,128)S(1)}) custom-call(f32[16,1024]{1,0:T(8,128)S(1)} %mixture.7.zero.refs_0_, f32[16,1024]{1,0:T(8,128)S(1)} %get-tuple-element.68.alleles.zero.refs_1_, f32[16,1024]{1,0:T(8,128)S(1)} %mixture.8.one.refs_2_, ...), custom_call_target="tpu_custom_call" | custom-call | tf_op jit(solution)/shard_map/leap/pallas_call | solution.py:333
  122.7 1.8 %collective-permute-start.49 = (f32[80,128]{1,0:T(8,128)S(1)}, f32[80,128]{1,0:T(8,128)S(1)}, u32[]{:S(2)}, u32[]{:S(2)}) collective-permute-start(f32[80,128]{1,0:T(8,128)S(1)} %get-tuple-element.79.refs_1_), channel_id=1, source_target_pairs={{0,3},{1,2},{2,1},{3,0},{4,7},{5,6},{6,5},{7,4},{8,11},{9,10},{10,... | collective-permute-start | bytes 122888 | tf_op jit(solution)/shard_map/ppermute | solution.py:36
  (123 shorter events, 64.9 us)
Async XLA Ops:
  0.6 7.2 %collective-permute-start.1 = (f32[10,128]{1,0:T(8,128)}, f32[10,128]{1,0:T(8,128)S(1)}, u32[]{:S(2)}, u32[]{:S(2)}) collective-permute-start(f32[10,128]{1,0:T(8,128)} %param.7), channel_id=1, source_target_pairs={{2,0},{6,4},{11,9},{15,13},{16,18},{20,22},{25,27},{29,31}} | collective-permute-start | bytes 15368 | tf_op jit(solution)/shard_map/ppermute | solution.py:80
  1.9 7.6 %collective-permute-start = (f32[10,128]{1,0:T(8,128)}, f32[10,128]{1,0:T(8,128)S(1)}, u32[]{:S(2)}, u32[]{:S(2)}) collective-permute-start(f32[10,128]{1,0:T(8,128)} %param.7), channel_id=1, source_target_pairs={{3,0},{7,4},{10,9},{14,13},{17,18},{21,22},{24,27},{28,31}} | collective-permute-start | bytes 15368 | tf_op jit(solution)/shard_map/ppermute | solution.py:80
  3.2 6.3 %collective-permute-start.2 = (f32[10,128]{1,0:T(8,128)}, f32[10,128]{1,0:T(8,128)S(1)}, u32[]{:S(2)}, u32[]{:S(2)}) collective-permute-start(f32[10,128]{1,0:T(8,128)} %param.7), channel_id=1, source_target_pairs={{1,0},{5,4},{8,9},{12,13},{19,18},{23,22},{26,27},{30,31}} | collective-permute-start | bytes 15368 | tf_op jit(solution)/shard_map/ppermute | solution.py:80
  11.5 11.2 %collective-permute-start.6 = (f32[10,1024]{1,0:T(8,128)S(1)}, f32[10,1024]{1,0:T(8,128)S(1)}, u32[]{:S(2)}, u32[]{:S(2)}) collective-permute-start(f32[10,1024]{1,0:T(8,128)S(1)} %maximum_select_fusion), channel_id=1, source_target_pairs={{0,24},{4,28},{9,17},{13,21},{18,10},{22,14},{27,3},{31,7}} | collective-permute-start | bytes 122888 | tf_op jit(solution)/shard_map/ppermute | solution.py:98
  16.3 6.4 %collective-permute-start.5 = (f32[10,1024]{1,0:T(8,128)S(1)}, f32[10,1024]{1,0:T(8,128)S(1)}, u32[]{:S(2)}, u32[]{:S(2)}) collective-permute-start(f32[10,1024]{1,0:T(8,128)S(1)} %maximum_select_fusion), channel_id=1, source_target_pairs={{0,16},{4,20},{9,25},{13,29},{18,2},{22,6},{27,11},{31,15}} | collective-permute-start | bytes 122888 | tf_op jit(solution)/shard_map/ppermute | solution.py:98
  28.3 5.9 %collective-permute-start.9 = (f32[88,128]{1,0:T(8,128)S(1)}, f32[88,128]{1,0:T(8,128)S(1)}, u32[]{:S(2)}, u32[]{:S(2)}) collective-permute-start(f32[88,128]{1,0:T(8,128)S(1)} %get-tuple-element.53.refs_0_), channel_id=1, source_target_pairs={{0,3},{1,2},{2,1},{3,0},{4,7},{5,6},{6,5},{7,4},{8,11},{9,10},{10,... | collective-permute-start | bytes 135176 | tf_op jit(solution)/shard_map/ppermute | solution.py:36
  29.9 5.6 %collective-permute-start.8 = (f32[88,128]{1,0:T(8,128)S(1)}, f32[88,128]{1,0:T(8,128)S(1)}, u32[]{:S(2)}, u32[]{:S(2)}) collective-permute-start(f32[88,128]{1,0:T(8,128)S(1)} %get-tuple-element.53.refs_0_), channel_id=1, source_target_pairs={{0,2},{1,3},{2,0},{3,1},{4,6},{5,7},{6,4},{7,5},{8,10},{9,11},{10,... | collective-permute-start | bytes 135176 | tf_op jit(solution)/shard_map/ppermute | solution.py:36
  30.0 5.4 %collective-permute-start.7 = (f32[88,128]{1,0:T(8,128)S(1)}, f32[88,128]{1,0:T(8,128)S(1)}, u32[]{:S(2)}, u32[]{:S(2)}) collective-permute-start(f32[88,128]{1,0:T(8,128)S(1)} %get-tuple-element.53.refs_0_), channel_id=1, source_target_pairs={{0,1},{1,0},{2,3},{3,2},{4,5},{5,4},{6,7},{7,6},{8,9},{9,8},{10,11... | collective-permute-start | bytes 135176 | tf_op jit(solution)/shard_map/ppermute | solution.py:36
  42.3 6.1 %collective-permute-start.17 = (f32[160,128]{1,0:T(8,128)S(1)}, f32[160,128]{1,0:T(8,128)S(1)}, u32[]{:S(2)}, u32[]{:S(2)}) collective-permute-start(f32[160,128]{1,0:T(8,128)S(1)} %add.69), channel_id=1, source_target_pairs={{0,8},{4,12},{8,0},{12,4},{16,24},{20,28},{24,16},{28,20},{1,9},{5... | collective-permute-start | bytes 245768 | tf_op jit(solution)/shard_map/ppermute | solution.py:36
  44.0 6.1 %collective-permute-start.15 = (f32[80,128]{1,0:T(8,128)S(1)}, f32[80,128]{1,0:T(8,128)S(1)}, u32[]{:S(2)}, u32[]{:S(2)}) collective-permute-start(f32[80,128]{1,0:T(8,128)S(1)} %get-tuple-element.58.refs_0_), channel_id=1, source_target_pairs={{0,3},{1,2},{2,1},{3,0},{4,7},{5,6},{6,5},{7,4},{8,11},{9,10},{10,... | collective-permute-start | bytes 122888 | tf_op jit(solution)/shard_map/ppermute | solution.py:36
  45.2 5.7 %collective-permute-start.14 = (f32[80,128]{1,0:T(8,128)S(1)}, f32[80,128]{1,0:T(8,128)S(1)}, u32[]{:S(2)}, u32[]{:S(2)}) collective-permute-start(f32[80,128]{1,0:T(8,128)S(1)} %get-tuple-element.58.refs_0_), channel_id=1, source_target_pairs={{0,2},{1,3},{2,0},{3,1},{4,6},{5,7},{6,4},{7,5},{8,10},{9,11},{10,... | collective-permute-start | bytes 122888 | tf_op jit(solution)/shard_map/ppermute | solution.py:36
  45.4 5.4 %collective-permute-start.13 = (f32[80,128]{1,0:T(8,128)S(1)}, f32[80,128]{1,0:T(8,128)S(1)}, u32[]{:S(2)}, u32[]{:S(2)}) collective-permute-start(f32[80,128]{1,0:T(8,128)S(1)} %get-tuple-element.58.refs_0_), channel_id=1, source_target_pairs={{0,1},{1,0},{2,3},{3,2},{4,5},{5,4},{6,7},{7,6},{8,9},{9,8},{10,11... | collective-permute-start | bytes 122888 | tf_op jit(solution)/shard_map/ppermute | solution.py:36
  67.1 5.9 %collective-permute-start.28 = (f32[160,128]{1,0:T(8,128)S(1)}, f32[160,128]{1,0:T(8,128)S(1)}, u32[]{:S(2)}, u32[]{:S(2)}) collective-permute-start(f32[160,128]{1,0:T(8,128)S(1)} %add.74), channel_id=1, source_target_pairs={{0,8},{4,12},{8,0},{12,4},{16,24},{20,28},{24,16},{28,20},{1,9},{5... | collective-permute-start | bytes 245768 | tf_op jit(solution)/shard_map/ppermute | solution.py:36
  68.6 6.2 %collective-permute-start.26 = (f32[80,128]{1,0:T(8,128)S(1)}, f32[80,128]{1,0:T(8,128)S(1)}, u32[]{:S(2)}, u32[]{:S(2)}) collective-permute-start(f32[80,128]{1,0:T(8,128)S(1)} %get-tuple-element.65.refs_1_), channel_id=1, source_target_pairs={{0,3},{1,2},{2,1},{3,0},{4,7},{5,6},{6,5},{7,4},{8,11},{9,10},{10,... | collective-permute-start | bytes 122888 | tf_op jit(solution)/shard_map/ppermute | solution.py:36
  70.2 5.4 %collective-permute-start.25 = (f32[80,128]{1,0:T(8,128)S(1)}, f32[80,128]{1,0:T(8,128)S(1)}, u32[]{:S(2)}, u32[]{:S(2)}) collective-permute-start(f32[80,128]{1,0:T(8,128)S(1)} %get-tuple-element.65.refs_1_), channel_id=1, source_target_pairs={{0,2},{1,3},{2,0},{3,1},{4,6},{5,7},{6,4},{7,5},{8,10},{9,11},{10,... | collective-permute-start | bytes 122888 | tf_op jit(solution)/shard_map/ppermute | solution.py:36
  83.2 6.0 %collective-permute-start.32 = (f32[80,128]{1,0:T(8,128)S(1)}, f32[80,128]{1,0:T(8,128)S(1)}, u32[]{:S(2)}, u32[]{:S(2)}) collective-permute-start(f32[80,128]{1,0:T(8,128)S(1)} %get-tuple-element.69.refs_1_), channel_id=1, source_target_pairs={{0,3},{1,2},{2,1},{3,0},{4,7},{5,6},{6,5},{7,4},{8,11},{9,10},{10,... | collective-permute-start | bytes 122888 | tf_op jit(solution)/shard_map/ppermute | solution.py:36
  84.8 5.3 %collective-permute-start.31 = (f32[80,128]{1,0:T(8,128)S(1)}, f32[80,128]{1,0:T(8,128)S(1)}, u32[]{:S(2)}, u32[]{:S(2)}) collective-permute-start(f32[80,128]{1,0:T(8,128)S(1)} %get-tuple-element.69.refs_1_), channel_id=1, source_target_pairs={{0,2},{1,3},{2,0},{3,1},{4,6},{5,7},{6,4},{7,5},{8,10},{9,11},{10,... | collective-permute-start | bytes 122888 | tf_op jit(solution)/shard_map/ppermute | solution.py:36
  97.2 5.9 %collective-permute-start.40 = (f32[160,128]{1,0:T(8,128)S(1)}, f32[160,128]{1,0:T(8,128)S(1)}, u32[]{:S(2)}, u32[]{:S(2)}) collective-permute-start(f32[160,128]{1,0:T(8,128)S(1)} %add.78), channel_id=1, source_target_pairs={{0,8},{4,12},{8,0},{12,4},{16,24},{20,28},{24,16},{28,20},{1,9},{5... | collective-permute-start | bytes 245768 | tf_op jit(solution)/shard_map/ppermute | solution.py:36
  98.8 5.8 %collective-permute-start.38 = (f32[80,128]{1,0:T(8,128)S(1)}, f32[80,128]{1,0:T(8,128)S(1)}, u32[]{:S(2)}, u32[]{:S(2)}) collective-permute-start(f32[80,128]{1,0:T(8,128)S(1)} %get-tuple-element.72.refs_0_), channel_id=1, source_target_pairs={{0,3},{1,2},{2,1},{3,0},{4,7},{5,6},{6,5},{7,4},{8,11},{9,10},{10,... | collective-permute-start | bytes 122888 | tf_op jit(solution)/shard_map/ppermute | solution.py:36
  100.3 5.4 %collective-permute-start.37 = (f32[80,128]{1,0:T(8,128)S(1)}, f32[80,128]{1,0:T(8,128)S(1)}, u32[]{:S(2)}, u32[]{:S(2)}) collective-permute-start(f32[80,128]{1,0:T(8,128)S(1)} %get-tuple-element.72.refs_0_), channel_id=1, source_target_pairs={{0,2},{1,3},{2,0},{3,1},{4,6},{5,7},{6,4},{7,5},{8,10},{9,11},{10,... | collective-permute-start | bytes 122888 | tf_op jit(solution)/shard_map/ppermute | solution.py:36
  100.3 5.4 %collective-permute-start.36 = (f32[80,128]{1,0:T(8,128)S(1)}, f32[80,128]{1,0:T(8,128)S(1)}, u32[]{:S(2)}, u32[]{:S(2)}) collective-permute-start(f32[80,128]{1,0:T(8,128)S(1)} %get-tuple-element.72.refs_0_), channel_id=1, source_target_pairs={{0,1},{1,0},{2,3},{3,2},{4,5},{5,4},{6,7},{7,6},{8,9},{9,8},{10,11... | collective-permute-start | bytes 122888 | tf_op jit(solution)/shard_map/ppermute | solution.py:36
  121.3 5.8 %collective-permute-start.51 = (f32[160,128]{1,0:T(8,128)S(1)}, f32[160,128]{1,0:T(8,128)S(1)}, u32[]{:S(2)}, u32[]{:S(2)}) collective-permute-start(f32[160,128]{1,0:T(8,128)S(1)} %add.83), channel_id=1, source_target_pairs={{0,8},{4,12},{8,0},{12,4},{16,24},{20,28},{24,16},{28,20},{1,9},{5... | collective-permute-start | bytes 245768 | tf_op jit(solution)/shard_map/ppermute | solution.py:36
  122.7 5.8 %collective-permute-start.49 = (f32[80,128]{1,0:T(8,128)S(1)}, f32[80,128]{1,0:T(8,128)S(1)}, u32[]{:S(2)}, u32[]{:S(2)}) collective-permute-start(f32[80,128]{1,0:T(8,128)S(1)} %get-tuple-element.79.refs_1_), channel_id=1, source_target_pairs={{0,3},{1,2},{2,1},{3,0},{4,7},{5,6},{6,5},{7,4},{8,11},{9,10},{10,... | collective-permute-start | bytes 122888 | tf_op jit(solution)/shard_map/ppermute | solution.py:36
  124.5 5.6 %collective-permute-start.48 = (f32[80,128]{1,0:T(8,128)S(1)}, f32[80,128]{1,0:T(8,128)S(1)}, u32[]{:S(2)}, u32[]{:S(2)}) collective-permute-start(f32[80,128]{1,0:T(8,128)S(1)} %get-tuple-element.79.refs_1_), channel_id=1, source_target_pairs={{0,2},{1,3},{2,0},{3,1},{4,6},{5,7},{6,4},{7,5},{8,10},{9,11},{10,... | collective-permute-start | bytes 122888 | tf_op jit(solution)/shard_map/ppermute | solution.py:36
  (30 other events, 110.7 us)

commit v4 on v3

--- a/solution.py
+++ b/solution.py
@@ -50,8 +50,8 @@
     return parts[0]
 
 
-def parts_of(value, axis):
-    strides = strides_of(axis)
+def parts_of(value, axis, done=0):
+    strides = strides_of(axis)[done:]
     for stride in strides[:-1]:
         value = value + swap(value, axis, stride)
     return value, swap(value, axis, strides[-1])
@@ -142,8 +142,8 @@
     return jnp.concatenate(pieces, axis=1)
 
 
-def expectation(
-    populations, mixture, alleles, twice_here, alt_ref, ref_ref, prop_ref, both_ref, turned
+def variant_sums(
+    populations, mixture, alleles, alt_ref, ref_ref, both_ref, gap_high, gap_low, turned
 ):
     rows, samples = mixture.shape
     variants = alleles.shape[1]
@@ -154,20 +154,18 @@
         [mix_high, mix_high, mix_mid, mix_mid, mix_high, mix_low], axis=0
     ).T
     right = jnp.concatenate([all_high, all_mid, all_high, all_mid, all_low, all_high], axis=0)
-    toward = jnp.concatenate([all_high, all_mid], axis=0)
     left = jnp.concatenate([mix_high, mix_mid], axis=0)
-    props = [jnp.zeros((2 * rows, tall), F32) for _ in range(0, samples, tall)]
     for start in range(0, variants, wide):
         across = slice(start, start + wide)
         excess = jnp.zeros((2 * rows, wide), F32)
         ref_sum = jnp.zeros((2 * rows, wide), F32)
-        for index, top in enumerate(range(0, samples, tall)):
+        for top in range(0, samples, tall):
             here = slice(top, top + tall)
             expected = dot(turned[here, :], right[:, across], 1, 0)
             ref = ref_ref[here, across] * pl.reciprocal(1.0 - expected, approx=True)
             gap = alt_ref[here, across] * pl.reciprocal(expected, approx=True) - ref
-            for term in two_terms(gap):
-                props[index] = props[index] + dot(toward[:, across], term, 1, 1)
+            for table, term in zip((gap_high, gap_low), two_terms(gap)):
+                table[here, across] = term
                 excess = excess + dot(left[:, here], term, 1, 0)
             for term in two_terms(ref):
                 ref_sum = ref_sum + dot(left[:, here], term, 1, 0)
@@ -176,13 +174,20 @@
         first_block = start // LANES * 2 * populations
         put_packed(both_ref, first_block, 2 * populations, excess + ref_sum)
         put_packed(both_ref, first_block + populations, 2 * populations, ref_sum)
-    prop = jnp.concatenate(props, axis=1)
+
+
+def sample_sums_kernel(populations, mixture, alleles, twice_here, gap_high, gap_low, prop_ref):
+    samples = mixture.shape[1]
+    rows = alleles.shape[0]
+    all_high, all_mid, _ = split(alleles[...])
+    toward = jnp.concatenate([all_high, all_mid], axis=0)
+    prop = dot(toward, gap_high[...], 1, 1) + dot(toward, gap_low[...], 1, 1)
     prop = prop[:populations] + prop[rows : rows + populations]
-    along = jnp.sum(mixture[:populations] * prop, axis=0, keepdims=True)
+    along = jnp.sum(mixture[:populations, :] * prop, axis=0, keepdims=True)
     stride = prop_ref.shape[0] * LANES // samples
-    put_packed(prop_ref, 0, stride, prop + (twice_here - along))
+    put_packed(prop_ref, 0, stride, prop + (twice_here[...] - along))
     if stride > populations:
-        put_packed(prop_ref, populations, stride, twice_here)
+        put_packed(prop_ref, populations, stride, twice_here[...])
 
 
 def next_mixture(populations, mixture, twice_observed, prop_parts):
@@ -228,18 +233,14 @@
         twice_out[:, here] = 2.0 * dot(ones, seen.astype(BF16), 1, 1)[:1]
 
 
-def first_kernel(
-    mixture, alleles, twice_here, alt, ref, mixture_out, alleles_out, prop_out, both_out, turned
-):
+def first_kernel(mixture, alleles, alt, ref, mixture_out, alleles_out, both_out, *refs):
     populations = mixture.shape[0]
     rows = mixture_out.shape[0]
     mix = pad_rows(mixture[...], rows)
     current = pad_rows(alleles[...], rows)
     mixture_out[...] = mix
     alleles_out[...] = current
-    expectation(
-        populations, mix, current, twice_here[...], alt, ref, prop_out, both_out, turned
-    )
+    variant_sums(populations, mix, current, alt, ref, both_out, *refs)
 
 
 def mixture_kernel(populations, with_twice, mixture, *refs):
@@ -251,13 +252,11 @@
         outs[1][...] = twice
 
 
-def step_kernel(populations, mixture, alleles, twice_here, *refs):
-    both_parts, (alt, ref, alleles_out, prop_out, both_out, turned) = split_refs(refs, 2)
+def step_kernel(populations, mixture, alleles, *refs):
+    both_parts, (alt, ref, alleles_out, both_out), refs = split_refs(refs, 2, 4)
     current = next_alleles(populations, alleles[...], both_parts)
     alleles_out[...] = current
-    expectation(
-        populations, mixture[...], current, twice_here[...], alt, ref, prop_out, both_out, turned
-    )
+    variant_sums(populations, mixture[...], current, alt, ref, both_out, *refs)
 
 
 def split_refs(refs, *counts):
@@ -308,7 +307,7 @@
     states = [ref[...] for ref in refs[:6]]
     mix_zero, all_zero, mix_one, all_one, mix_two, all_two = states
     mix_parts, all_parts, rest = split_refs(refs[6:], 2, 2)
-    twice_here, alt, ref, mixture_out, alleles_out, prop_out, both_out, turned = rest
+    alt, ref, mixture_out, alleles_out, both_out, *refs = rest
     mix_tile = mix_parts[0][...] + mix_parts[1][...]
     all_tile = all_parts[0][...] + all_parts[1][...]
     clipped = row_mask(clip_unit(leap(mix_zero, mix_one, mix_two, mix_tile)), populations)
@@ -316,9 +315,7 @@
     current = row_mask(clip_unit(leap(all_zero, all_one, all_two, all_tile)), populations)
     mixture_out[...] = mix
     alleles_out[...] = current
-    expectation(
-        populations, mix, current, twice_here[...], alt, ref, prop_out, both_out, turned
-    )
+    variant_sums(populations, mix, current, alt, ref, both_out, *refs)
 
 
 def last_kernel(populations, mixture, alleles, *refs):
@@ -349,8 +346,7 @@
     state_out = (((rows, samples), F32), ((rows, variants), F32))
     packed = populations * samples // LANES
     both_out = ((2 * populations * variants // LANES, LANES), F32)
-    sums_out = (((packed, LANES), F32), both_out)
-    first_sums_out = (((packed + samples // LANES, LANES), F32), both_out)
+    sums_out = (both_out, ((samples, variants), BF16), ((samples, variants), BF16))
     tile_out = ((2 * SUBLANES, LANES), F32)
     turned = (pltpu.VMEM((samples, 6 * rows), BF16),)
 
@@ -378,13 +374,24 @@
     )(*in_place)
     alleles = gather_frequencies(frequencies, flags)
 
-    mix_zero, all_zero, prop, both = call(
+    def sums(mixture, alleles, both, gaps, extra=0):
+        (prop,) = call(
+            functools.partial(sample_sums_kernel, populations),
+            "sample_sums",
+            (((packed + extra, LANES), F32),),
+            (mixture, alleles, twice_here, *gaps),
+        )
+        both = both + swap(both, "samp", 1)
+        return lax.optimization_barrier((prop, both))
+
+    mix_zero, all_zero, both, *gaps = call(
         first_kernel,
         "first",
-        (*state_out, *first_sums_out),
-        (proportions, alleles, twice_here, alt, ref),
+        (*state_out, *sums_out),
+        (proportions, alleles, alt, ref),
         turned,
     )
+    prop, both = sums(mix_zero, all_zero, both, gaps, samples // LANES)
 
     def moved_mixture(mixture, twice, prop):
         known = () if twice is None else (twice,)
@@ -399,13 +406,14 @@
         return out[0], (known or out[1:])[0]
 
     def step(mixture, alleles, both):
-        return call(
+        moved, both, *gaps = call(
             functools.partial(step_kernel, populations),
             "step",
             (state_out[1], *sums_out),
-            (mixture, alleles, twice_here, *parts_of(both, "samp"), alt, ref),
+            (mixture, alleles, *parts_of(both, "samp", 1), alt, ref),
             turned,
         )
+        return moved, *sums(mixture, moved, both, gaps)
 
     twice = None
     for repeat in range(STEPS):
@@ -425,26 +433,26 @@
             functools.partial(alleles_square_kernel, populations),
             "alleles_square",
             (state_out[1], tile_out),
-            (all_zero, all_one, *parts_of(both, "samp")),
+            (all_zero, all_one, *parts_of(both, "samp", 1)),
             flops=ALLELES_COST,
         )
-        tiles = (*parts_of(mix_tile, "samp"), *parts_of(all_tile, "var"))
-        mix_zero, all_zero, prop, both = call(
+        mix_tile = mix_tile + swap(mix_tile, "samp", 1)
+        mix_tile, all_tile = lax.optimization_barrier((mix_tile, all_tile))
+        tiles = (*parts_of(mix_tile, "samp", 1), *parts_of(all_tile, "var"))
+        mix_zero, all_zero, both, *gaps = call(
             functools.partial(leap_kernel, populations),
             "leap",
             (*state_out, *sums_out),
-            (
-                *(mix_zero, all_zero, mix_one, all_one, mix_two, all_two),
-                *(*tiles, twice_here, alt, ref),
-            ),
+            (mix_zero, all_zero, mix_one, all_one, mix_two, all_two, *tiles, alt, ref),
             turned,
         )
+        prop, both = sums(mix_zero, all_zero, both, gaps)
     mixture, _ = moved_mixture(mix_zero, twice, prop)
     return call(
         functools.partial(last_kernel, populations),
         "last",
         (((populations, samples), F32), ((populations, variants), F32)),
-        (mixture, all_zero, *parts_of(both, "samp")),
+        (mixture, all_zero, *parts_of(both, "samp", 1)),
     )
 
 

time: 133 us -> 130 us (0.977)
  Pallas kernels: 27.9 us -> 32.4 us
  waiting for transfers between devices: 42.7 us -> 38.8 us
  starting transfers between devices: 59.9 us -> 56.9 us
    pallas_call x15 -> x21, Pallas kernels: 24.1 us -> 28.7 us  [call(): pl.pallas_call(kernel, out_shape=tuple((jax.ShapeDtypeStruct(*out) for ou...]
    ppermute x47, waiting for transfers between devices: 37.7 us -> 33.9 us  [swap(): return lax.ppermute(value, axis, [(i, i ^ mask) for i in range(size)])]
    ppermute x47, starting transfers between devices: 48.7 us -> 45.6 us  [swap(): return lax.ppermute(value, axis, [(i, i ^ mask) for i in range(size)])]
  transfers between devices with their start and end apart: 53 -> 53, of which waited for: 34 -> 28; matrix products, arithmetic and copies ran while one was open for 0% -> 0% of each run, Pallas kernels for 3% -> 9%
where the time goes in v4:
time: 130 us
  starting transfers between devices  56.9 us (44%)
  waiting for transfers between devices  38.8 us (30%)
  Pallas kernels  32.4 us (25%)
    ppermute x47, starting transfers between devices, swap(): return lax.ppermute(value, axis, [(i, i ^ mask) for i in range(size)])  45.6 us
    ppermute x47, waiting for transfers between devices, swap(): return lax.ppermute(value, axis, [(i, i ^ mask) for i in range(size)])  33.9 us
    pallas_call x21, Pallas kernels, call(): pl.pallas_call(kernel, out_shape=tuple((jax.ShapeDtypeStruct(*out) for ou...  28.7 us
    ppermute x3, starting transfers between devices, gather_frequencies(): total = total + lax.ppermute(held, both, pairs)  7.35 us
    ppermute x3, waiting for transfers between devices, gather_frequencies(): arrived.append(lax.ppermute(frequencies, both, pairs))  4.93 us
    ppermute x3, starting transfers between devices, gather_frequencies(): arrived.append(lax.ppermute(frequencies, both, pairs))  3.88 us
    pallas_call x1, Pallas kernels, local(): pl.pallas_call(prepare_kernel, out_shape=(pltpu.VMEM((samples, variants),...  3.77 us
  transfers between devices with their start and end apart: 53, of which 28 were waited for; matrix products, arithmetic and copies ran while one was open for 0% of the time, Pallas kernels for 9%

profile of v4, /device:TPU:0, one launch (start us, length us, event | category | flops | bytes accessed | tf_op | source)
XLA Modules:
  0.0 130.1 jit_solution(13566300624324727288)
XLA Ops:
  4.5 3.2 %collective-permute-done.1 = f32[10,128]{1,0:T(8,128)S(1)} collective-permute-done((f32[10,128]{1,0:T(8,128)}, f32[10,128]{1,0:T(8,128)S(1)}, u32[]{:S(2)}, u32[]{:S(2)}) %collective-permute-start.1) | collective-permute-done | bytes 5152 | tf_op jit(solution)/shard_map/ppermute | solution.py:80
  7.8 1.7 %collective-permute-done = f32[10,128]{1,0:T(8,128)S(1)} collective-permute-done((f32[10,128]{1,0:T(8,128)}, f32[10,128]{1,0:T(8,128)S(1)}, u32[]{:S(2)}, u32[]{:S(2)}) %collective-permute-start) | collective-permute-done | bytes 5152 | tf_op jit(solution)/shard_map/ppermute | solution.py:80
  11.5 4.8 %collective-permute-start.6 = (f32[10,1024]{1,0:T(8,128)S(1)}, f32[10,1024]{1,0:T(8,128)S(1)}, u32[]{:S(2)}, u32[]{:S(2)}) collective-permute-start(f32[10,1024]{1,0:T(8,128)S(1)} %maximum_select_fusion), channel_id=1, source_target_pairs={{0,24},{4,28},{9,17},{13,21},{18,10},{22,14},{27,3},{31,7}} | collective-permute-start | bytes 122888 | tf_op jit(solution)/shard_map/ppermute | solution.py:98
  18.9 3.8 %prepare.1 = (f32[1024,1024]{1,0:T(8,128)S(1)}, f32[1024,1024]{1,0:T(8,128)S(1)}, f32[1,1024]{1,0:T(1,128)S(1)}) custom-call(s32[1024,1024]{1,0:T(8,128)} %genotypes, s32[1024,1024]{1,0:T(8,128)} %observed), custom_call_target="tpu_custom_call" | custom-call | tf_op jit(solution)/shard_map/prepare/pallas_call | solution.py:359
  22.7 3.2 %first.1 = (f32[16,1024]{1,0:T(8,128)S(1)}, f32[16,1024]{1,0:T(8,128)S(1)}, f32[160,128]{1,0:T(8,128)S(1)}, bf16[1024,1024]{1,0:T(8,128)(2,1)S(1)}, bf16[1024,1024]{1,0:T(8,128)(2,1)S(1)}) custom-call(f32[10,1024]{1,0:T(8,128)S(1)} %copy-done, f32[10,1024]{1,0:T(8,128)S(1)} %add_add_fusion.alleles, f32[1024,1024]{1,0:T(8,128)S(1)} %get-tuple-element.70.alt.refs_2_.refs_10_, ...), custom_call_target="tpu_custom_call" | custom-call | tf_op jit(solution)/shard_map/first/pallas_call | solution.py:330
  29.6 2.5 %collective-permute-start.8 = (f32[88,128]{1,0:T(8,128)S(1)}, f32[88,128]{1,0:T(8,128)S(1)}, u32[]{:S(2)}, u32[]{:S(2)}) collective-permute-start(f32[88,128]{1,0:T(8,128)S(1)} %sample_sums.6.refs_0_), channel_id=1, source_target_pairs={{0,1},{1,0},{2,3},{3,2},{4,5},{5,4},{6,7},{7,6},{8,9},{9,8},{10,11... | collective-permute-start | bytes 135176 | tf_op jit(solution)/shard_map/ppermute | solution.py:36
  36.7 3.2 %step.3 = (f32[16,1024]{1,0:T(8,128)S(1)}, f32[160,128]{1,0:T(8,128)S(1)}, bf16[1024,1024]{1,0:T(8,128)(2,1)S(1)}, bf16[1024,1024]{1,0:T(8,128)(2,1)S(1)}) custom-call(f32[16,1024]{1,0:T(8,128)S(1)} %get-tuple-element.79.mixture.one.refs_2_, f32[16,1024]{1,0:T(8,128)S(1)} %get-tuple-element.73.alleles.zero.refs_1_, f32[160,128]{1,0:T(8,128)S(1)} %add.68.refs_0_, ...), custom_call_target="tpu_custom_call" | custom-call | tf_op jit(solution)/shard_map/step/pallas_call | solution.py:330
  44.3 2.9 %collective-permute-start.14 = (f32[80,128]{1,0:T(8,128)S(1)}, f32[80,128]{1,0:T(8,128)S(1)}, u32[]{:S(2)}, u32[]{:S(2)}) collective-permute-start(f32[80,128]{1,0:T(8,128)S(1)} %sample_sums.7.refs_0_), channel_id=1, source_target_pairs={{0,1},{1,0},{2,3},{3,2},{4,5},{5,4},{6,7},{7,6},{8,9},{9,8},{10,11... | collective-permute-start | bytes 122888 | tf_op jit(solution)/shard_map/ppermute | solution.py:36
  53.1 2.4 %collective-permute-done.20 = f32[16,128]{1,0:T(8,128)S(1)} collective-permute-done((f32[16,128]{1,0:T(8,128)S(1)}, f32[16,128]{1,0:T(8,128)S(1)}, u32[]{:S(2)}, u32[]{:S(2)}) %collective-permute-start.20) | collective-permute-done | bytes 8224 | tf_op jit(solution)/shard_map/ppermute | solution.py:36
  56.1 2.0 %collective-permute-start.23 = (f32[16,128]{1,0:T(8,128)S(1)}, f32[16,128]{1,0:T(8,128)S(1)}, u32[]{:S(2)}, u32[]{:S(2)}) collective-permute-start(f32[16,128]{1,0:T(8,128)S(1)} %add.73.refs_8_), channel_id=1, source_target_pairs={{0,2},{1,3},{2,0},{3,1},{4,6},{5,7},{6,4},{7,5},{8,10},{9,11},{10,... | collective-permute-start | bytes 24584 | tf_op jit(solution)/shard_map/ppermute | solution.py:36
  60.7 3.6 %leap.2 = (f32[16,1024]{1,0:T(8,128)S(1)}, f32[16,1024]{1,0:T(8,128)S(1)}, f32[160,128]{1,0:T(8,128)S(1)}, bf16[1024,1024]{1,0:T(8,128)(2,1)S(1)}, bf16[1024,1024]{1,0:T(8,128)(2,1)S(1)}) custom-call(f32[16,1024]{1,0:T(8,128)S(1)} %get-tuple-element.72.mixture.zero.refs_0_, f32[16,1024]{1,0:T(8,128)S(1)} %get-tuple-element.73.alleles.zero.refs_1_, ...), custom_call_target="tpu_custom_call" | custom-call | tf_op jit(solution)/shard_map/leap/pallas_call | solution.py:330
  67.3 2.7 %collective-permute-start.27 = (f32[80,128]{1,0:T(8,128)S(1)}, f32[80,128]{1,0:T(8,128)S(1)}, u32[]{:S(2)}, u32[]{:S(2)}) collective-permute-start(f32[80,128]{1,0:T(8,128)S(1)} %sample_sums.8.refs_1_), channel_id=1, source_target_pairs={{0,3},{1,2},{2,1},{3,0},{4,7},{5,6},{6,5},{7,4},{8,11},{9,10},{10,... | collective-permute-start | bytes 122888 | tf_op jit(solution)/shard_map/ppermute | solution.py:36
  70.0 1.7 %collective-permute-start.25 = (f32[80,128]{1,0:T(8,128)S(1)}, f32[80,128]{1,0:T(8,128)S(1)}, u32[]{:S(2)}, u32[]{:S(2)}) collective-permute-start(f32[80,128]{1,0:T(8,128)S(1)} %sample_sums.8.refs_1_), channel_id=1, source_target_pairs={{0,1},{1,0},{2,3},{3,2},{4,5},{5,4},{6,7},{7,6},{8,9},{9,8},{10,11... | collective-permute-start | bytes 122888 | tf_op jit(solution)/shard_map/ppermute | solution.py:36
  76.2 3.2 %step.4 = (f32[16,1024]{1,0:T(8,128)S(1)}, f32[160,128]{1,0:T(8,128)S(1)}, bf16[1024,1024]{1,0:T(8,128)(2,1)S(1)}, bf16[1024,1024]{1,0:T(8,128)(2,1)S(1)}) custom-call(f32[16,1024]{1,0:T(8,128)S(1)} %mixture.7.zero.refs_0_, f32[16,1024]{1,0:T(8,128)S(1)} %get-tuple-element.95.alleles, f32[160,128]{1,0:T(8,128)S(1)} %add.75.refs_0_, ...), custom_call_target="tpu_custom_call" | custom-call | tf_op jit(solution)/shard_map/step/pallas_call | solution.py:330
  81.3 2.7 %collective-permute-start.33 = (f32[80,128]{1,0:T(8,128)S(1)}, f32[80,128]{1,0:T(8,128)S(1)}, u32[]{:S(2)}, u32[]{:S(2)}) collective-permute-start(f32[80,128]{1,0:T(8,128)S(1)} %sample_sums.9.refs_1_), channel_id=1, source_target_pairs={{0,3},{1,2},{2,1},{3,0},{4,7},{5,6},{6,5},{7,4},{8,11},{9,10},{10,... | collective-permute-start | bytes 122888 | tf_op jit(solution)/shard_map/ppermute | solution.py:36
  84.0 1.7 %collective-permute-start.31 = (f32[80,128]{1,0:T(8,128)S(1)}, f32[80,128]{1,0:T(8,128)S(1)}, u32[]{:S(2)}, u32[]{:S(2)}) collective-permute-start(f32[80,128]{1,0:T(8,128)S(1)} %sample_sums.9.refs_1_), channel_id=1, source_target_pairs={{0,1},{1,0},{2,3},{3,2},{4,5},{5,4},{6,7},{7,6},{8,9},{9,8},{10,11... | collective-permute-start | bytes 122888 | tf_op jit(solution)/shard_map/ppermute | solution.py:36
  90.2 3.2 %step.5 = (f32[16,1024]{1,0:T(8,128)S(1)}, f32[160,128]{1,0:T(8,128)S(1)}, bf16[1024,1024]{1,0:T(8,128)(2,1)S(1)}, bf16[1024,1024]{1,0:T(8,128)(2,1)S(1)}) custom-call(f32[16,1024]{1,0:T(8,128)S(1)} %mixture.8.one.refs_2_, f32[16,1024]{1,0:T(8,128)S(1)} %get-tuple-element.101.alleles.zero.refs_1_, f32[160,128]{1,0:T(8,128)S(1)} %add.77.refs_0_, ...), custom_call_target="tpu_custom_call" | custom-call | tf_op jit(solution)/shard_map/step/pallas_call | solution.py:330
  96.4 2.7 %collective-permute-start.39 = (f32[80,128]{1,0:T(8,128)S(1)}, f32[80,128]{1,0:T(8,128)S(1)}, u32[]{:S(2)}, u32[]{:S(2)}) collective-permute-start(f32[80,128]{1,0:T(8,128)S(1)} %sample_sums.10.refs_0_), channel_id=1, source_target_pairs={{0,3},{1,2},{2,1},{3,0},{4,7},{5,6},{6,5},{7,4},{8,11},{9,10},{10,... | collective-permute-start | bytes 122888 | tf_op jit(solution)/shard_map/ppermute | solution.py:36
  99.1 1.7 %collective-permute-start.37 = (f32[80,128]{1,0:T(8,128)S(1)}, f32[80,128]{1,0:T(8,128)S(1)}, u32[]{:S(2)}, u32[]{:S(2)}) collective-permute-start(f32[80,128]{1,0:T(8,128)S(1)} %sample_sums.10.refs_0_), channel_id=1, source_target_pairs={{0,1},{1,0},{2,3},{3,2},{4,5},{5,4},{6,7},{7,6},{8,9},{9,8},{10,11... | collective-permute-start | bytes 122888 | tf_op jit(solution)/shard_map/ppermute | solution.py:36
  106.6 2.4 %collective-permute-done.43 = f32[16,128]{1,0:T(8,128)S(1)} collective-permute-done((f32[16,128]{1,0:T(8,128)S(1)}, f32[16,128]{1,0:T(8,128)S(1)}, u32[]{:S(2)}, u32[]{:S(2)}) %collective-permute-start.43) | collective-permute-done | bytes 8224 | tf_op jit(solution)/shard_map/ppermute | solution.py:36
  109.5 2.0 %collective-permute-start.46 = (f32[16,128]{1,0:T(8,128)S(1)}, f32[16,128]{1,0:T(8,128)S(1)}, u32[]{:S(2)}, u32[]{:S(2)}) collective-permute-start(f32[16,128]{1,0:T(8,128)S(1)} %add.82.refs_8_), channel_id=1, source_target_pairs={{0,2},{1,3},{2,0},{3,1},{4,6},{5,7},{6,4},{7,5},{8,10},{9,11},{10,... | collective-permute-start | bytes 24584 | tf_op jit(solution)/shard_map/ppermute | solution.py:36
  114.1 3.4 %leap.3 = (f32[16,1024]{1,0:T(8,128)S(1)}, f32[16,1024]{1,0:T(8,128)S(1)}, f32[160,128]{1,0:T(8,128)S(1)}, bf16[1024,1024]{1,0:T(8,128)(2,1)S(1)}, bf16[1024,1024]{1,0:T(8,128)(2,1)S(1)}) custom-call(f32[16,1024]{1,0:T(8,128)S(1)} %mixture.7.zero.refs_0_, f32[16,1024]{1,0:T(8,128)S(1)} %get-tuple-element.101.alleles.zero.refs_1_, ...), custom_call_target="tpu_custom_call" | custom-call | tf_op jit(solution)/shard_map/leap/pallas_call | solution.py:330
  120.5 2.7 %collective-permute-start.50 = (f32[80,128]{1,0:T(8,128)S(1)}, f32[80,128]{1,0:T(8,128)S(1)}, u32[]{:S(2)}, u32[]{:S(2)}) collective-permute-start(f32[80,128]{1,0:T(8,128)S(1)} %sample_sums.11.refs_1_), channel_id=1, source_target_pairs={{0,3},{1,2},{2,1},{3,0},{4,7},{5,6},{6,5},{7,4},{8,11},{9,10},{10,... | collective-permute-start | bytes 122888 | tf_op jit(solution)/shard_map/ppermute | solution.py:36
  123.2 1.7 %collective-permute-start.48 = (f32[80,128]{1,0:T(8,128)S(1)}, f32[80,128]{1,0:T(8,128)S(1)}, u32[]{:S(2)}, u32[]{:S(2)}) collective-permute-start(f32[80,128]{1,0:T(8,128)S(1)} %sample_sums.11.refs_1_), channel_id=1, source_target_pairs={{0,1},{1,0},{2,3},{3,2},{4,5},{5,4},{6,7},{7,6},{8,9},{9,8},{10,11... | collective-permute-start | bytes 122888 | tf_op jit(solution)/shard_map/ppermute | solution.py:36
  (129 shorter events, 64.0 us)
Async XLA Ops:
  0.6 7.2 %collective-permute-start.1 = (f32[10,128]{1,0:T(8,128)}, f32[10,128]{1,0:T(8,128)S(1)}, u32[]{:S(2)}, u32[]{:S(2)}) collective-permute-start(f32[10,128]{1,0:T(8,128)} %param.7), channel_id=1, source_target_pairs={{2,0},{6,4},{11,9},{15,13},{16,18},{20,22},{25,27},{29,31}} | collective-permute-start | bytes 15368 | tf_op jit(solution)/shard_map/ppermute | solution.py:80
  1.9 7.6 %collective-permute-start = (f32[10,128]{1,0:T(8,128)}, f32[10,128]{1,0:T(8,128)S(1)}, u32[]{:S(2)}, u32[]{:S(2)}) collective-permute-start(f32[10,128]{1,0:T(8,128)} %param.7), channel_id=1, source_target_pairs={{3,0},{7,4},{10,9},{14,13},{17,18},{21,22},{24,27},{28,31}} | collective-permute-start | bytes 15368 | tf_op jit(solution)/shard_map/ppermute | solution.py:80
  3.2 6.3 %collective-permute-start.2 = (f32[10,128]{1,0:T(8,128)}, f32[10,128]{1,0:T(8,128)S(1)}, u32[]{:S(2)}, u32[]{:S(2)}) collective-permute-start(f32[10,128]{1,0:T(8,128)} %param.7), channel_id=1, source_target_pairs={{1,0},{5,4},{8,9},{12,13},{19,18},{23,22},{26,27},{30,31}} | collective-permute-start | bytes 15368 | tf_op jit(solution)/shard_map/ppermute | solution.py:80
  11.5 11.2 %collective-permute-start.6 = (f32[10,1024]{1,0:T(8,128)S(1)}, f32[10,1024]{1,0:T(8,128)S(1)}, u32[]{:S(2)}, u32[]{:S(2)}) collective-permute-start(f32[10,1024]{1,0:T(8,128)S(1)} %maximum_select_fusion), channel_id=1, source_target_pairs={{0,24},{4,28},{9,17},{13,21},{18,10},{22,14},{27,3},{31,7}} | collective-permute-start | bytes 122888 | tf_op jit(solution)/shard_map/ppermute | solution.py:98
  16.3 6.4 %collective-permute-start.5 = (f32[10,1024]{1,0:T(8,128)S(1)}, f32[10,1024]{1,0:T(8,128)S(1)}, u32[]{:S(2)}, u32[]{:S(2)}) collective-permute-start(f32[10,1024]{1,0:T(8,128)S(1)} %maximum_select_fusion), channel_id=1, source_target_pairs={{0,16},{4,20},{9,25},{13,29},{18,2},{22,6},{27,11},{31,15}} | collective-permute-start | bytes 122888 | tf_op jit(solution)/shard_map/ppermute | solution.py:98
  17.6 5.1 %collective-permute-start.4 = (f32[10,1024]{1,0:T(8,128)S(1)}, f32[10,1024]{1,0:T(8,128)S(1)}, u32[]{:S(2)}, u32[]{:S(2)}) collective-permute-start(f32[10,1024]{1,0:T(8,128)S(1)} %maximum_select_fusion), channel_id=1, source_target_pairs={{0,8},{4,12},{9,1},{13,5},{18,26},{22,30},{27,19},{31,23}} | collective-permute-start | bytes 122888 | tf_op jit(solution)/shard_map/ppermute | solution.py:98
  27.3 4.9 %collective-permute-start.11 = (f32[160,128]{1,0:T(8,128)S(1)}, f32[160,128]{1,0:T(8,128)S(1)}, u32[]{:S(2)}, u32[]{:S(2)}) collective-permute-start(f32[160,128]{1,0:T(8,128)S(1)} %add.67), channel_id=1, source_target_pairs={{0,8},{4,12},{8,0},{12,4},{16,24},{20,28},{24,16},{28,20},{1,9},{5... | collective-permute-start | bytes 245768 | tf_op jit(solution)/shard_map/ppermute | solution.py:36
  27.8 6.2 %collective-permute-start.10 = (f32[88,128]{1,0:T(8,128)S(1)}, f32[88,128]{1,0:T(8,128)S(1)}, u32[]{:S(2)}, u32[]{:S(2)}) collective-permute-start(f32[88,128]{1,0:T(8,128)S(1)} %sample_sums.6.refs_0_), channel_id=1, source_target_pairs={{0,3},{1,2},{2,1},{3,0},{4,7},{5,6},{6,5},{7,4},{8,11},{9,10},{10,... | collective-permute-start | bytes 135176 | tf_op jit(solution)/shard_map/ppermute | solution.py:36
  29.3 5.9 %collective-permute-start.9 = (f32[88,128]{1,0:T(8,128)S(1)}, f32[88,128]{1,0:T(8,128)S(1)}, u32[]{:S(2)}, u32[]{:S(2)}) collective-permute-start(f32[88,128]{1,0:T(8,128)S(1)} %sample_sums.6.refs_0_), channel_id=1, source_target_pairs={{0,2},{1,3},{2,0},{3,1},{4,6},{5,7},{6,4},{7,5},{8,10},{9,11},{10,... | collective-permute-start | bytes 135176 | tf_op jit(solution)/shard_map/ppermute | solution.py:36
  29.6 5.6 %collective-permute-start.8 = (f32[88,128]{1,0:T(8,128)S(1)}, f32[88,128]{1,0:T(8,128)S(1)}, u32[]{:S(2)}, u32[]{:S(2)}) collective-permute-start(f32[88,128]{1,0:T(8,128)S(1)} %sample_sums.6.refs_0_), channel_id=1, source_target_pairs={{0,1},{1,0},{2,3},{3,2},{4,5},{5,4},{6,7},{7,6},{8,9},{9,8},{10,11... | collective-permute-start | bytes 135176 | tf_op jit(solution)/shard_map/ppermute | solution.py:36
  41.3 6.0 %collective-permute-start.17 = (f32[160,128]{1,0:T(8,128)S(1)}, f32[160,128]{1,0:T(8,128)S(1)}, u32[]{:S(2)}, u32[]{:S(2)}) collective-permute-start(f32[160,128]{1,0:T(8,128)S(1)} %add.69), channel_id=1, source_target_pairs={{0,8},{4,12},{8,0},{12,4},{16,24},{20,28},{24,16},{28,20},{1,9},{5... | collective-permute-start | bytes 245768 | tf_op jit(solution)/shard_map/ppermute | solution.py:36
  42.9 6.0 %collective-permute-start.16 = (f32[80,128]{1,0:T(8,128)S(1)}, f32[80,128]{1,0:T(8,128)S(1)}, u32[]{:S(2)}, u32[]{:S(2)}) collective-permute-start(f32[80,128]{1,0:T(8,128)S(1)} %sample_sums.7.refs_0_), channel_id=1, source_target_pairs={{0,3},{1,2},{2,1},{3,0},{4,7},{5,6},{6,5},{7,4},{8,11},{9,10},{10,... | collective-permute-start | bytes 122888 | tf_op jit(solution)/shard_map/ppermute | solution.py:36
  44.2 6.0 %collective-permute-start.15 = (f32[80,128]{1,0:T(8,128)S(1)}, f32[80,128]{1,0:T(8,128)S(1)}, u32[]{:S(2)}, u32[]{:S(2)}) collective-permute-start(f32[80,128]{1,0:T(8,128)S(1)} %sample_sums.7.refs_0_), channel_id=1, source_target_pairs={{0,2},{1,3},{2,0},{3,1},{4,6},{5,7},{6,4},{7,5},{8,10},{9,11},{10,... | collective-permute-start | bytes 122888 | tf_op jit(solution)/shard_map/ppermute | solution.py:36
  44.3 5.8 %collective-permute-start.14 = (f32[80,128]{1,0:T(8,128)S(1)}, f32[80,128]{1,0:T(8,128)S(1)}, u32[]{:S(2)}, u32[]{:S(2)}) collective-permute-start(f32[80,128]{1,0:T(8,128)S(1)} %sample_sums.7.refs_0_), channel_id=1, source_target_pairs={{0,1},{1,0},{2,3},{3,2},{4,5},{5,4},{6,7},{7,6},{8,9},{9,8},{10,11... | collective-permute-start | bytes 122888 | tf_op jit(solution)/shard_map/ppermute | solution.py:36
  65.6 6.0 %collective-permute-start.28 = (f32[160,128]{1,0:T(8,128)S(1)}, f32[160,128]{1,0:T(8,128)S(1)}, u32[]{:S(2)}, u32[]{:S(2)}) collective-permute-start(f32[160,128]{1,0:T(8,128)S(1)} %add.74), channel_id=1, source_target_pairs={{0,8},{4,12},{8,0},{12,4},{16,24},{20,28},{24,16},{28,20},{1,9},{5... | collective-permute-start | bytes 245768 | tf_op jit(solution)/shard_map/ppermute | solution.py:36
  67.3 6.2 %collective-permute-start.27 = (f32[80,128]{1,0:T(8,128)S(1)}, f32[80,128]{1,0:T(8,128)S(1)}, u32[]{:S(2)}, u32[]{:S(2)}) collective-permute-start(f32[80,128]{1,0:T(8,128)S(1)} %sample_sums.8.refs_1_), channel_id=1, source_target_pairs={{0,3},{1,2},{2,1},{3,0},{4,7},{5,6},{6,5},{7,4},{8,11},{9,10},{10,... | collective-permute-start | bytes 122888 | tf_op jit(solution)/shard_map/ppermute | solution.py:36
  70.0 4.9 %collective-permute-start.26 = (f32[80,128]{1,0:T(8,128)S(1)}, f32[80,128]{1,0:T(8,128)S(1)}, u32[]{:S(2)}, u32[]{:S(2)}) collective-permute-start(f32[80,128]{1,0:T(8,128)S(1)} %sample_sums.8.refs_1_), channel_id=1, source_target_pairs={{0,2},{1,3},{2,0},{3,1},{4,6},{5,7},{6,4},{7,5},{8,10},{9,11},{10,... | collective-permute-start | bytes 122888 | tf_op jit(solution)/shard_map/ppermute | solution.py:36
  70.0 4.9 %collective-permute-start.25 = (f32[80,128]{1,0:T(8,128)S(1)}, f32[80,128]{1,0:T(8,128)S(1)}, u32[]{:S(2)}, u32[]{:S(2)}) collective-permute-start(f32[80,128]{1,0:T(8,128)S(1)} %sample_sums.8.refs_1_), channel_id=1, source_target_pairs={{0,1},{1,0},{2,3},{3,2},{4,5},{5,4},{6,7},{7,6},{8,9},{9,8},{10,11... | collective-permute-start | bytes 122888 | tf_op jit(solution)/shard_map/ppermute | solution.py:36
  80.8 4.9 %collective-permute-start.34 = (f32[160,128]{1,0:T(8,128)S(1)}, f32[160,128]{1,0:T(8,128)S(1)}, u32[]{:S(2)}, u32[]{:S(2)}) collective-permute-start(f32[160,128]{1,0:T(8,128)S(1)} %add.76), channel_id=1, source_target_pairs={{0,8},{4,12},{8,0},{12,4},{16,24},{20,28},{24,16},{28,20},{1,9},{5... | collective-permute-start | bytes 245768 | tf_op jit(solution)/shard_map/ppermute | solution.py:36
  81.3 6.2 %collective-permute-start.33 = (f32[80,128]{1,0:T(8,128)S(1)}, f32[80,128]{1,0:T(8,128)S(1)}, u32[]{:S(2)}, u32[]{:S(2)}) collective-permute-start(f32[80,128]{1,0:T(8,128)S(1)} %sample_sums.9.refs_1_), channel_id=1, source_target_pairs={{0,3},{1,2},{2,1},{3,0},{4,7},{5,6},{6,5},{7,4},{8,11},{9,10},{10,... | collective-permute-start | bytes 122888 | tf_op jit(solution)/shard_map/ppermute | solution.py:36
  94.7 6.0 %collective-permute-start.40 = (f32[160,128]{1,0:T(8,128)S(1)}, f32[160,128]{1,0:T(8,128)S(1)}, u32[]{:S(2)}, u32[]{:S(2)}) collective-permute-start(f32[160,128]{1,0:T(8,128)S(1)} %add.78), channel_id=1, source_target_pairs={{0,8},{4,12},{8,0},{12,4},{16,24},{20,28},{24,16},{28,20},{1,9},{5... | collective-permute-start | bytes 245768 | tf_op jit(solution)/shard_map/ppermute | solution.py:36
  96.4 6.0 %collective-permute-start.39 = (f32[80,128]{1,0:T(8,128)S(1)}, f32[80,128]{1,0:T(8,128)S(1)}, u32[]{:S(2)}, u32[]{:S(2)}) collective-permute-start(f32[80,128]{1,0:T(8,128)S(1)} %sample_sums.10.refs_0_), channel_id=1, source_target_pairs={{0,3},{1,2},{2,1},{3,0},{4,7},{5,6},{6,5},{7,4},{8,11},{9,10},{10,... | collective-permute-start | bytes 122888 | tf_op jit(solution)/shard_map/ppermute | solution.py:36
  118.9 6.0 %collective-permute-start.51 = (f32[160,128]{1,0:T(8,128)S(1)}, f32[160,128]{1,0:T(8,128)S(1)}, u32[]{:S(2)}, u32[]{:S(2)}) collective-permute-start(f32[160,128]{1,0:T(8,128)S(1)} %add.83), channel_id=1, source_target_pairs={{0,8},{4,12},{8,0},{12,4},{16,24},{20,28},{24,16},{28,20},{1,9},{5... | collective-permute-start | bytes 245768 | tf_op jit(solution)/shard_map/ppermute | solution.py:36
  120.5 6.2 %collective-permute-start.50 = (f32[80,128]{1,0:T(8,128)S(1)}, f32[80,128]{1,0:T(8,128)S(1)}, u32[]{:S(2)}, u32[]{:S(2)}) collective-permute-start(f32[80,128]{1,0:T(8,128)S(1)} %sample_sums.11.refs_1_), channel_id=1, source_target_pairs={{0,3},{1,2},{2,1},{3,0},{4,7},{5,6},{6,5},{7,4},{8,11},{9,10},{10,... | collective-permute-start | bytes 122888 | tf_op jit(solution)/shard_map/ppermute | solution.py:36
  (30 other events, 110.7 us)

commit v5 on v4

--- a/solution.py
+++ b/solution.py
@@ -15,7 +15,7 @@
 SUBLANES = 8
 LANES = 128
 VMEM_BYTES = 32 * 2**20
-TALL, WIDE = 512, 512
+TALL, WIDE = 512, 1024
 MIXTURE_COST = 5 * 10**9
 ALLELES_COST = 5 * 10**9
 
@@ -41,7 +41,7 @@
 
 
 def all_parts_of(value, axis):
-    return [value] + [swap(value, axis, mask) for mask in range(1, lax.axis_size(axis))]
+    return [value] + [swap(value, axis, i ^ (i >> 1)) for i in range(1, lax.axis_size(axis))]
 
 
 def pair_sum(parts):
@@ -437,7 +437,6 @@
             flops=ALLELES_COST,
         )
         mix_tile = mix_tile + swap(mix_tile, "samp", 1)
-        mix_tile, all_tile = lax.optimization_barrier((mix_tile, all_tile))
         tiles = (*parts_of(mix_tile, "samp", 1), *parts_of(all_tile, "var"))
         mix_zero, all_zero, both, *gaps = call(
             functools.partial(leap_kernel, populations),

time: 130 us -> 127 us (0.977)
  starting transfers between devices: 56.9 us -> 54.2 us
    ppermute x47, starting transfers between devices: 45.6 us -> 43 us  [swap(): return lax.ppermute(value, axis, [(i, i ^ mask) for i in range(size)])]
  transfers between devices with their start and end apart: 53 -> 53, of which waited for: 28 -> 36; matrix products, arithmetic and copies ran while one was open for 0% -> 0% of each run, Pallas kernels for 9% -> 9%
where the time goes in v5:
time: 127 us
  starting transfers between devices  54.2 us (43%)
  waiting for transfers between devices  39.5 us (31%)
  Pallas kernels  31.4 us (25%)
    ppermute x47, starting transfers between devices, swap(): return lax.ppermute(value, axis, [(i, i ^ mask) for i in range(size)])  43 us
    ppermute x47, waiting for transfers between devices, swap(): return lax.ppermute(value, axis, [(i, i ^ mask) for i in range(size)])  34.5 us
    pallas_call x21, Pallas kernels, call(): pl.pallas_call(kernel, out_shape=tuple((jax.ShapeDtypeStruct(*out) for ou...  27.6 us
    ppermute x3, starting transfers between devices, gather_frequencies(): total = total + lax.ppermute(held, both, pairs)  7.35 us
    ppermute x3, waiting for transfers between devices, gather_frequencies(): arrived.append(lax.ppermute(frequencies, both, pairs))  4.93 us
    ppermute x3, starting transfers between devices, gather_frequencies(): arrived.append(lax.ppermute(frequencies, both, pairs))  3.88 us
    pallas_call x1, Pallas kernels, local(): pl.pallas_call(prepare_kernel, out_shape=(pltpu.VMEM((samples, variants),...  3.77 us
  transfers between devices with their start and end apart: 53, of which 36 were waited for; matrix products, arithmetic and copies ran while one was open for 0% of the time, Pallas kernels for 9%

profile of v5, /device:TPU:0, one launch (start us, length us, event | category | flops | bytes accessed | tf_op | source)
XLA Modules:
  0.0 127.0 jit_solution(5088221736061163944)
XLA Ops:
  4.5 3.2 %collective-permute-done.1 = f32[10,128]{1,0:T(8,128)S(1)} collective-permute-done((f32[10,128]{1,0:T(8,128)}, f32[10,128]{1,0:T(8,128)S(1)}, u32[]{:S(2)}, u32[]{:S(2)}) %collective-permute-start.1) | collective-permute-done | bytes 5152 | tf_op jit(solution)/shard_map/ppermute | solution.py:80
  7.8 1.7 %collective-permute-done = f32[10,128]{1,0:T(8,128)S(1)} collective-permute-done((f32[10,128]{1,0:T(8,128)}, f32[10,128]{1,0:T(8,128)S(1)}, u32[]{:S(2)}, u32[]{:S(2)}) %collective-permute-start) | collective-permute-done | bytes 5152 | tf_op jit(solution)/shard_map/ppermute | solution.py:80
  11.5 4.8 %collective-permute-start.6 = (f32[10,1024]{1,0:T(8,128)S(1)}, f32[10,1024]{1,0:T(8,128)S(1)}, u32[]{:S(2)}, u32[]{:S(2)}) collective-permute-start(f32[10,1024]{1,0:T(8,128)S(1)} %maximum_select_fusion), channel_id=1, source_target_pairs={{0,24},{4,28},{9,17},{13,21},{18,10},{22,14},{27,3},{31,7}} | collective-permute-start | bytes 122888 | tf_op jit(solution)/shard_map/ppermute | solution.py:98
  18.9 3.8 %prepare.1 = (f32[1024,1024]{1,0:T(8,128)S(1)}, f32[1024,1024]{1,0:T(8,128)S(1)}, f32[1,1024]{1,0:T(1,128)S(1)}) custom-call(s32[1024,1024]{1,0:T(8,128)} %genotypes, s32[1024,1024]{1,0:T(8,128)} %observed), custom_call_target="tpu_custom_call" | custom-call | tf_op jit(solution)/shard_map/prepare/pallas_call | solution.py:359
  22.7 3.0 %first.1 = (f32[16,1024]{1,0:T(8,128)S(1)}, f32[16,1024]{1,0:T(8,128)S(1)}, f32[160,128]{1,0:T(8,128)S(1)}, bf16[1024,1024]{1,0:T(8,128)(2,1)S(1)}, bf16[1024,1024]{1,0:T(8,128)(2,1)S(1)}) custom-call(f32[10,1024]{1,0:T(8,128)S(1)} %copy-done, f32[10,1024]{1,0:T(8,128)S(1)} %add_add_fusion.alleles, f32[1024,1024]{1,0:T(8,128)S(1)} %get-tuple-element.66.alt.refs_2_.refs_10_, ...), custom_call_target="tpu_custom_call" | custom-call | tf_op jit(solution)/shard_map/first/pallas_call | solution.py:330
  27.6 2.8 %collective-permute-start.9 = (f32[88,128]{1,0:T(8,128)S(1)}, f32[88,128]{1,0:T(8,128)S(1)}, u32[]{:S(2)}, u32[]{:S(2)}) collective-permute-start(f32[88,128]{1,0:T(8,128)S(1)} %sample_sums.6.refs_0_), channel_id=1, source_target_pairs={{0,3},{1,2},{2,1},{3,0},{4,7},{5,6},{6,5},{7,4},{8,11},{9,10},{10,... | collective-permute-start | bytes 135176 | tf_op jit(solution)/shard_map/ppermute | solution.py:36
  34.9 1.7 %collective-permute-done.12.refs_1_ = f32[160,128]{1,0:T(8,128)S(1)} collective-permute-done((f32[160,128]{1,0:T(8,128)S(1)}, f32[160,128]{1,0:T(8,128)S(1)}, u32[]{:S(2)}, u32[]{:S(2)}) %collective-permute-start.12) | collective-permute-done | bytes 81952 | tf_op jit(solution)/shard_map/ppermute | solution.py:36
  36.6 3.0 %step.3 = (f32[16,1024]{1,0:T(8,128)S(1)}, f32[160,128]{1,0:T(8,128)S(1)}, bf16[1024,1024]{1,0:T(8,128)(2,1)S(1)}, bf16[1024,1024]{1,0:T(8,128)(2,1)S(1)}) custom-call(f32[16,1024]{1,0:T(8,128)S(1)} %get-tuple-element.75.mixture.one.refs_2_, f32[16,1024]{1,0:T(8,128)S(1)} %get-tuple-element.69.alleles.zero.refs_1_, f32[160,128]{1,0:T(8,128)S(1)} %add.68.refs_0_, ...), custom_call_target="tpu_custom_call" | custom-call | tf_op jit(solution)/shard_map/step/pallas_call | solution.py:330
  53.6 1.7 %collective-permute-start.21 = (f32[16,128]{1,0:T(8,128)S(1)}, f32[16,128]{1,0:T(8,128)S(1)}, u32[]{:S(2)}, u32[]{:S(2)}) collective-permute-start(f32[16,128]{1,0:T(8,128)S(1)} %add.72.refs_6_), channel_id=1, source_target_pairs={{0,16},{4,20},{8,24},{12,28},{16,0},{20,4},{24,8},{28,12},{1,17},{... | collective-permute-start | bytes 24584 | tf_op jit(solution)/shard_map/ppermute | solution.py:36
  57.2 2.6 %collective-permute-done.23.refs_9_ = f32[16,128]{1,0:T(8,128)S(1)} collective-permute-done((f32[16,128]{1,0:T(8,128)S(1)}, f32[16,128]{1,0:T(8,128)S(1)}, u32[]{:S(2)}, u32[]{:S(2)}) %collective-permute-start.23) | collective-permute-done | bytes 8224 | tf_op jit(solution)/shard_map/ppermute | solution.py:36
  59.9 3.4 %leap.2 = (f32[16,1024]{1,0:T(8,128)S(1)}, f32[16,1024]{1,0:T(8,128)S(1)}, f32[160,128]{1,0:T(8,128)S(1)}, bf16[1024,1024]{1,0:T(8,128)(2,1)S(1)}, bf16[1024,1024]{1,0:T(8,128)(2,1)S(1)}) custom-call(f32[16,1024]{1,0:T(8,128)S(1)} %get-tuple-element.68.mixture.zero.refs_0_, f32[16,1024]{1,0:T(8,128)S(1)} %get-tuple-element.69.alleles.zero.refs_1_, ...), custom_call_target="tpu_custom_call" | custom-call | tf_op jit(solution)/shard_map/leap/pallas_call | solution.py:330
  66.9 1.7 %collective-permute-start.26 = (f32[80,128]{1,0:T(8,128)S(1)}, f32[80,128]{1,0:T(8,128)S(1)}, u32[]{:S(2)}, u32[]{:S(2)}) collective-permute-start(f32[80,128]{1,0:T(8,128)S(1)} %sample_sums.8.refs_1_), channel_id=1, source_target_pairs={{0,3},{1,2},{2,1},{3,0},{4,7},{5,6},{6,5},{7,4},{8,11},{9,10},{10,... | collective-permute-start | bytes 122888 | tf_op jit(solution)/shard_map/ppermute | solution.py:36
  74.0 3.0 %step.4 = (f32[16,1024]{1,0:T(8,128)S(1)}, f32[160,128]{1,0:T(8,128)S(1)}, bf16[1024,1024]{1,0:T(8,128)(2,1)S(1)}, bf16[1024,1024]{1,0:T(8,128)(2,1)S(1)}) custom-call(f32[16,1024]{1,0:T(8,128)S(1)} %mixture.7.zero.refs_0_, f32[16,1024]{1,0:T(8,128)S(1)} %get-tuple-element.89.alleles, f32[160,128]{1,0:T(8,128)S(1)} %add.75.refs_0_, ...), custom_call_target="tpu_custom_call" | custom-call | tf_op jit(solution)/shard_map/step/pallas_call | solution.py:330
  79.8 1.7 %collective-permute-start.33 = (f32[80,128]{1,0:T(8,128)S(1)}, f32[80,128]{1,0:T(8,128)S(1)}, u32[]{:S(2)}, u32[]{:S(2)}) collective-permute-start(f32[80,128]{1,0:T(8,128)S(1)} %sample_sums.9.refs_1_), channel_id=1, source_target_pairs={{0,2},{1,3},{2,0},{3,1},{4,6},{5,7},{6,4},{7,5},{8,10},{9,11},{10,... | collective-permute-start | bytes 122888 | tf_op jit(solution)/shard_map/ppermute | solution.py:36
  85.6 1.7 %collective-permute-done.32.refs_3_ = f32[80,128]{1,0:T(8,128)S(1)} collective-permute-done((f32[80,128]{1,0:T(8,128)S(1)}, f32[80,128]{1,0:T(8,128)S(1)}, u32[]{:S(2)}, u32[]{:S(2)}) %collective-permute-start.32) | collective-permute-done | bytes 40992 | tf_op jit(solution)/shard_map/ppermute | solution.py:36
  87.9 3.0 %step.5 = (f32[16,1024]{1,0:T(8,128)S(1)}, f32[160,128]{1,0:T(8,128)S(1)}, bf16[1024,1024]{1,0:T(8,128)(2,1)S(1)}, bf16[1024,1024]{1,0:T(8,128)(2,1)S(1)}) custom-call(f32[16,1024]{1,0:T(8,128)S(1)} %mixture.8.one.refs_2_, f32[16,1024]{1,0:T(8,128)S(1)} %get-tuple-element.95.alleles.zero.refs_1_, f32[160,128]{1,0:T(8,128)S(1)} %add.77.refs_0_, ...), custom_call_target="tpu_custom_call" | custom-call | tf_op jit(solution)/shard_map/step/pallas_call | solution.py:330
  93.6 2.1 %collective-permute-start.39 = (f32[80,128]{1,0:T(8,128)S(1)}, f32[80,128]{1,0:T(8,128)S(1)}, u32[]{:S(2)}, u32[]{:S(2)}) collective-permute-start(f32[80,128]{1,0:T(8,128)S(1)} %sample_sums.10.refs_0_), channel_id=1, source_target_pairs={{0,2},{1,3},{2,0},{3,1},{4,6},{5,7},{6,4},{7,5},{8,10},{9,11},{10,... | collective-permute-start | bytes 122888 | tf_op jit(solution)/shard_map/ppermute | solution.py:36
  95.7 1.7 %collective-permute-start.38 = (f32[80,128]{1,0:T(8,128)S(1)}, f32[80,128]{1,0:T(8,128)S(1)}, u32[]{:S(2)}, u32[]{:S(2)}) collective-permute-start(f32[80,128]{1,0:T(8,128)S(1)} %sample_sums.10.refs_0_), channel_id=1, source_target_pairs={{0,3},{1,2},{2,1},{3,0},{4,7},{5,6},{6,5},{7,4},{8,11},{9,10},{10,... | collective-permute-start | bytes 122888 | tf_op jit(solution)/shard_map/ppermute | solution.py:36
  99.7 1.9 %collective-permute-done.38.refs_2_ = f32[80,128]{1,0:T(8,128)S(1)} collective-permute-done((f32[80,128]{1,0:T(8,128)S(1)}, f32[80,128]{1,0:T(8,128)S(1)}, u32[]{:S(2)}, u32[]{:S(2)}) %collective-permute-start.38) | collective-permute-done | bytes 40992 | tf_op jit(solution)/shard_map/ppermute | solution.py:36
  104.1 2.6 %collective-permute-done.43 = f32[16,128]{1,0:T(8,128)S(1)} collective-permute-done((f32[16,128]{1,0:T(8,128)S(1)}, f32[16,128]{1,0:T(8,128)S(1)}, u32[]{:S(2)}, u32[]{:S(2)}) %collective-permute-start.43) | collective-permute-done | bytes 8224 | tf_op jit(solution)/shard_map/ppermute | solution.py:36
  108.8 1.6 %collective-permute-done.44.refs_7_ = f32[16,128]{1,0:T(8,128)S(1)} collective-permute-done((f32[16,128]{1,0:T(8,128)S(1)}, f32[16,128]{1,0:T(8,128)S(1)}, u32[]{:S(2)}, u32[]{:S(2)}) %collective-permute-start.44) | collective-permute-done | bytes 8224 | tf_op jit(solution)/shard_map/ppermute | solution.py:36
  110.4 1.9 %collective-permute-done.46.refs_9_ = f32[16,128]{1,0:T(8,128)S(1)} collective-permute-done((f32[16,128]{1,0:T(8,128)S(1)}, f32[16,128]{1,0:T(8,128)S(1)}, u32[]{:S(2)}, u32[]{:S(2)}) %collective-permute-start.46) | collective-permute-done | bytes 8224 | tf_op jit(solution)/shard_map/ppermute | solution.py:36
  112.3 3.2 %leap.3 = (f32[16,1024]{1,0:T(8,128)S(1)}, f32[16,1024]{1,0:T(8,128)S(1)}, f32[160,128]{1,0:T(8,128)S(1)}, bf16[1024,1024]{1,0:T(8,128)(2,1)S(1)}, bf16[1024,1024]{1,0:T(8,128)(2,1)S(1)}) custom-call(f32[16,1024]{1,0:T(8,128)S(1)} %mixture.7.zero.refs_0_, f32[16,1024]{1,0:T(8,128)S(1)} %get-tuple-element.95.alleles.zero.refs_1_, ...), custom_call_target="tpu_custom_call" | custom-call | tf_op jit(solution)/shard_map/leap/pallas_call | solution.py:330
  118.8 1.7 %collective-permute-start.49 = (f32[80,128]{1,0:T(8,128)S(1)}, f32[80,128]{1,0:T(8,128)S(1)}, u32[]{:S(2)}, u32[]{:S(2)}) collective-permute-start(f32[80,128]{1,0:T(8,128)S(1)} %sample_sums.11.refs_1_), channel_id=1, source_target_pairs={{0,3},{1,2},{2,1},{3,0},{4,7},{5,6},{6,5},{7,4},{8,11},{9,10},{10,... | collective-permute-start | bytes 122888 | tf_op jit(solution)/shard_map/ppermute | solution.py:36
  (129 shorter events, 66.4 us)
Async XLA Ops:
  0.6 7.2 %collective-permute-start.1 = (f32[10,128]{1,0:T(8,128)}, f32[10,128]{1,0:T(8,128)S(1)}, u32[]{:S(2)}, u32[]{:S(2)}) collective-permute-start(f32[10,128]{1,0:T(8,128)} %param.7), channel_id=1, source_target_pairs={{2,0},{6,4},{11,9},{15,13},{16,18},{20,22},{25,27},{29,31}} | collective-permute-start | bytes 15368 | tf_op jit(solution)/shard_map/ppermute | solution.py:80
  1.9 7.6 %collective-permute-start = (f32[10,128]{1,0:T(8,128)}, f32[10,128]{1,0:T(8,128)S(1)}, u32[]{:S(2)}, u32[]{:S(2)}) collective-permute-start(f32[10,128]{1,0:T(8,128)} %param.7), channel_id=1, source_target_pairs={{3,0},{7,4},{10,9},{14,13},{17,18},{21,22},{24,27},{28,31}} | collective-permute-start | bytes 15368 | tf_op jit(solution)/shard_map/ppermute | solution.py:80
  3.2 6.3 %collective-permute-start.2 = (f32[10,128]{1,0:T(8,128)}, f32[10,128]{1,0:T(8,128)S(1)}, u32[]{:S(2)}, u32[]{:S(2)}) collective-permute-start(f32[10,128]{1,0:T(8,128)} %param.7), channel_id=1, source_target_pairs={{1,0},{5,4},{8,9},{12,13},{19,18},{23,22},{26,27},{30,31}} | collective-permute-start | bytes 15368 | tf_op jit(solution)/shard_map/ppermute | solution.py:80
  11.5 11.2 %collective-permute-start.6 = (f32[10,1024]{1,0:T(8,128)S(1)}, f32[10,1024]{1,0:T(8,128)S(1)}, u32[]{:S(2)}, u32[]{:S(2)}) collective-permute-start(f32[10,1024]{1,0:T(8,128)S(1)} %maximum_select_fusion), channel_id=1, source_target_pairs={{0,24},{4,28},{9,17},{13,21},{18,10},{22,14},{27,3},{31,7}} | collective-permute-start | bytes 122888 | tf_op jit(solution)/shard_map/ppermute | solution.py:98
  16.3 6.4 %collective-permute-start.5 = (f32[10,1024]{1,0:T(8,128)S(1)}, f32[10,1024]{1,0:T(8,128)S(1)}, u32[]{:S(2)}, u32[]{:S(2)}) collective-permute-start(f32[10,1024]{1,0:T(8,128)S(1)} %maximum_select_fusion), channel_id=1, source_target_pairs={{0,16},{4,20},{9,25},{13,29},{18,2},{22,6},{27,11},{31,15}} | collective-permute-start | bytes 122888 | tf_op jit(solution)/shard_map/ppermute | solution.py:98
  17.6 5.1 %collective-permute-start.4 = (f32[10,1024]{1,0:T(8,128)S(1)}, f32[10,1024]{1,0:T(8,128)S(1)}, u32[]{:S(2)}, u32[]{:S(2)}) collective-permute-start(f32[10,1024]{1,0:T(8,128)S(1)} %maximum_select_fusion), channel_id=1, source_target_pairs={{0,8},{4,12},{9,1},{13,5},{18,26},{22,30},{27,19},{31,23}} | collective-permute-start | bytes 122888 | tf_op jit(solution)/shard_map/ppermute | solution.py:98
  27.6 6.7 %collective-permute-start.10 = (f32[88,128]{1,0:T(8,128)S(1)}, f32[88,128]{1,0:T(8,128)S(1)}, u32[]{:S(2)}, u32[]{:S(2)}) collective-permute-start(f32[88,128]{1,0:T(8,128)S(1)} %sample_sums.6.refs_0_), channel_id=1, source_target_pairs={{0,2},{1,3},{2,0},{3,1},{4,6},{5,7},{6,4},{7,5},{8,10},{9,11},{10,... | collective-permute-start | bytes 135176 | tf_op jit(solution)/shard_map/ppermute | solution.py:36
  27.6 6.7 %collective-permute-start.9 = (f32[88,128]{1,0:T(8,128)S(1)}, f32[88,128]{1,0:T(8,128)S(1)}, u32[]{:S(2)}, u32[]{:S(2)}) collective-permute-start(f32[88,128]{1,0:T(8,128)S(1)} %sample_sums.6.refs_0_), channel_id=1, source_target_pairs={{0,3},{1,2},{2,1},{3,0},{4,7},{5,6},{6,5},{7,4},{8,11},{9,10},{10,... | collective-permute-start | bytes 135176 | tf_op jit(solution)/shard_map/ppermute | solution.py:36
  41.0 4.9 %collective-permute-start.17 = (f32[160,128]{1,0:T(8,128)S(1)}, f32[160,128]{1,0:T(8,128)S(1)}, u32[]{:S(2)}, u32[]{:S(2)}) collective-permute-start(f32[160,128]{1,0:T(8,128)S(1)} %add.69), channel_id=1, source_target_pairs={{0,8},{4,12},{8,0},{12,4},{16,24},{20,28},{24,16},{28,20},{1,9},{5... | collective-permute-start | bytes 245768 | tf_op jit(solution)/shard_map/ppermute | solution.py:36
  41.7 5.8 %collective-permute-start.16 = (f32[80,128]{1,0:T(8,128)S(1)}, f32[80,128]{1,0:T(8,128)S(1)}, u32[]{:S(2)}, u32[]{:S(2)}) collective-permute-start(f32[80,128]{1,0:T(8,128)S(1)} %sample_sums.7.refs_0_), channel_id=1, source_target_pairs={{0,2},{1,3},{2,0},{3,1},{4,6},{5,7},{6,4},{7,5},{8,10},{9,11},{10,... | collective-permute-start | bytes 122888 | tf_op jit(solution)/shard_map/ppermute | solution.py:36
  42.6 5.9 %collective-permute-start.15 = (f32[80,128]{1,0:T(8,128)S(1)}, f32[80,128]{1,0:T(8,128)S(1)}, u32[]{:S(2)}, u32[]{:S(2)}) collective-permute-start(f32[80,128]{1,0:T(8,128)S(1)} %sample_sums.7.refs_0_), channel_id=1, source_target_pairs={{0,3},{1,2},{2,1},{3,0},{4,7},{5,6},{6,5},{7,4},{8,11},{9,10},{10,... | collective-permute-start | bytes 122888 | tf_op jit(solution)/shard_map/ppermute | solution.py:36
  45.9 5.5 %collective-permute-start.18 = (f32[160,128]{1,0:T(8,128)S(1)}, f32[160,128]{1,0:T(8,128)S(1)}, u32[]{:S(2)}, u32[]{:S(2)}) collective-permute-start(f32[160,128]{1,0:T(8,128)S(1)} %add.70.refs_0_), channel_id=1, source_target_pairs={{0,16},{4,20},{8,24},{12,28},{16,0},{20,4},{24,8},{28,12},{1,17},{... | collective-permute-start | bytes 245768 | tf_op jit(solution)/shard_map/ppermute | solution.py:36
  66.0 5.9 %collective-permute-start.27 = (f32[80,128]{1,0:T(8,128)S(1)}, f32[80,128]{1,0:T(8,128)S(1)}, u32[]{:S(2)}, u32[]{:S(2)}) collective-permute-start(f32[80,128]{1,0:T(8,128)S(1)} %sample_sums.8.refs_1_), channel_id=1, source_target_pairs={{0,2},{1,3},{2,0},{3,1},{4,6},{5,7},{6,4},{7,5},{8,10},{9,11},{10,... | collective-permute-start | bytes 122888 | tf_op jit(solution)/shard_map/ppermute | solution.py:36
  66.9 5.9 %collective-permute-start.26 = (f32[80,128]{1,0:T(8,128)S(1)}, f32[80,128]{1,0:T(8,128)S(1)}, u32[]{:S(2)}, u32[]{:S(2)}) collective-permute-start(f32[80,128]{1,0:T(8,128)S(1)} %sample_sums.8.refs_1_), channel_id=1, source_target_pairs={{0,3},{1,2},{2,1},{3,0},{4,7},{5,6},{6,5},{7,4},{8,11},{9,10},{10,... | collective-permute-start | bytes 122888 | tf_op jit(solution)/shard_map/ppermute | solution.py:36
  78.4 4.9 %collective-permute-start.34 = (f32[160,128]{1,0:T(8,128)S(1)}, f32[160,128]{1,0:T(8,128)S(1)}, u32[]{:S(2)}, u32[]{:S(2)}) collective-permute-start(f32[160,128]{1,0:T(8,128)S(1)} %add.76), channel_id=1, source_target_pairs={{0,8},{4,12},{8,0},{12,4},{16,24},{20,28},{24,16},{28,20},{1,9},{5... | collective-permute-start | bytes 245768 | tf_op jit(solution)/shard_map/ppermute | solution.py:36
  79.8 5.8 %collective-permute-start.33 = (f32[80,128]{1,0:T(8,128)S(1)}, f32[80,128]{1,0:T(8,128)S(1)}, u32[]{:S(2)}, u32[]{:S(2)}) collective-permute-start(f32[80,128]{1,0:T(8,128)S(1)} %sample_sums.9.refs_1_), channel_id=1, source_target_pairs={{0,2},{1,3},{2,0},{3,1},{4,6},{5,7},{6,4},{7,5},{8,10},{9,11},{10,... | collective-permute-start | bytes 122888 | tf_op jit(solution)/shard_map/ppermute | solution.py:36
  81.5 5.8 %collective-permute-start.32 = (f32[80,128]{1,0:T(8,128)S(1)}, f32[80,128]{1,0:T(8,128)S(1)}, u32[]{:S(2)}, u32[]{:S(2)}) collective-permute-start(f32[80,128]{1,0:T(8,128)S(1)} %sample_sums.9.refs_1_), channel_id=1, source_target_pairs={{0,3},{1,2},{2,1},{3,0},{4,7},{5,6},{6,5},{7,4},{8,11},{9,10},{10,... | collective-permute-start | bytes 122888 | tf_op jit(solution)/shard_map/ppermute | solution.py:36
  92.3 5.1 %collective-permute-start.40 = (f32[160,128]{1,0:T(8,128)S(1)}, f32[160,128]{1,0:T(8,128)S(1)}, u32[]{:S(2)}, u32[]{:S(2)}) collective-permute-start(f32[160,128]{1,0:T(8,128)S(1)} %add.78), channel_id=1, source_target_pairs={{0,8},{4,12},{8,0},{12,4},{16,24},{20,28},{24,16},{28,20},{1,9},{5... | collective-permute-start | bytes 245768 | tf_op jit(solution)/shard_map/ppermute | solution.py:36
  93.6 6.0 %collective-permute-start.39 = (f32[80,128]{1,0:T(8,128)S(1)}, f32[80,128]{1,0:T(8,128)S(1)}, u32[]{:S(2)}, u32[]{:S(2)}) collective-permute-start(f32[80,128]{1,0:T(8,128)S(1)} %sample_sums.10.refs_0_), channel_id=1, source_target_pairs={{0,2},{1,3},{2,0},{3,1},{4,6},{5,7},{6,4},{7,5},{8,10},{9,11},{10,... | collective-permute-start | bytes 122888 | tf_op jit(solution)/shard_map/ppermute | solution.py:36
  95.7 5.9 %collective-permute-start.38 = (f32[80,128]{1,0:T(8,128)S(1)}, f32[80,128]{1,0:T(8,128)S(1)}, u32[]{:S(2)}, u32[]{:S(2)}) collective-permute-start(f32[80,128]{1,0:T(8,128)S(1)} %sample_sums.10.refs_0_), channel_id=1, source_target_pairs={{0,3},{1,2},{2,1},{3,0},{4,7},{5,6},{6,5},{7,4},{8,11},{9,10},{10,... | collective-permute-start | bytes 122888 | tf_op jit(solution)/shard_map/ppermute | solution.py:36
  97.4 6.6 %collective-permute-start.41 = (f32[160,128]{1,0:T(8,128)S(1)}, f32[160,128]{1,0:T(8,128)S(1)}, u32[]{:S(2)}, u32[]{:S(2)}) collective-permute-start(f32[160,128]{1,0:T(8,128)S(1)} %add.79.refs_0_), channel_id=1, source_target_pairs={{0,16},{4,20},{8,24},{12,28},{16,0},{20,4},{24,8},{28,12},{1,17},{... | collective-permute-start | bytes 245768 | tf_op jit(solution)/shard_map/ppermute | solution.py:36
  116.9 4.9 %collective-permute-start.51 = (f32[160,128]{1,0:T(8,128)S(1)}, f32[160,128]{1,0:T(8,128)S(1)}, u32[]{:S(2)}, u32[]{:S(2)}) collective-permute-start(f32[160,128]{1,0:T(8,128)S(1)} %add.83), channel_id=1, source_target_pairs={{0,8},{4,12},{8,0},{12,4},{16,24},{20,28},{24,16},{28,20},{1,9},{5... | collective-permute-start | bytes 245768 | tf_op jit(solution)/shard_map/ppermute | solution.py:36
  118.1 5.8 %collective-permute-start.50 = (f32[80,128]{1,0:T(8,128)S(1)}, f32[80,128]{1,0:T(8,128)S(1)}, u32[]{:S(2)}, u32[]{:S(2)}) collective-permute-start(f32[80,128]{1,0:T(8,128)S(1)} %sample_sums.11.refs_1_), channel_id=1, source_target_pairs={{0,2},{1,3},{2,0},{3,1},{4,6},{5,7},{6,4},{7,5},{8,10},{9,11},{10,... | collective-permute-start | bytes 122888 | tf_op jit(solution)/shard_map/ppermute | solution.py:36
  118.8 6.0 %collective-permute-start.49 = (f32[80,128]{1,0:T(8,128)S(1)}, f32[80,128]{1,0:T(8,128)S(1)}, u32[]{:S(2)}, u32[]{:S(2)}) collective-permute-start(f32[80,128]{1,0:T(8,128)S(1)} %sample_sums.11.refs_1_), channel_id=1, source_target_pairs={{0,3},{1,2},{2,1},{3,0},{4,7},{5,6},{6,5},{7,4},{8,11},{9,10},{10,... | collective-permute-start | bytes 122888 | tf_op jit(solution)/shard_map/ppermute | solution.py:36
  (30 other events, 108.8 us)

commit v6 on v5

--- a/solution.py
+++ b/solution.py
@@ -303,13 +303,13 @@
     return zero + 2.0 * alpha * step + alpha * alpha * curve
 
 
-def leap_kernel(populations, *refs):
+def leap_kernel(populations, n_all, *refs):
     states = [ref[...] for ref in refs[:6]]
     mix_zero, all_zero, mix_one, all_one, mix_two, all_two = states
-    mix_parts, all_parts, rest = split_refs(refs[6:], 2, 2)
+    mix_parts, all_parts, rest = split_refs(refs[6:], 2, n_all)
     alt, ref, mixture_out, alleles_out, both_out, *refs = rest
     mix_tile = mix_parts[0][...] + mix_parts[1][...]
-    all_tile = all_parts[0][...] + all_parts[1][...]
+    all_tile = pair_sum([part[...] for part in all_parts])
     clipped = row_mask(clip_unit(leap(mix_zero, mix_one, mix_two, mix_tile)), populations)
     mix = clipped / jnp.sum(clipped, axis=0, keepdims=True)
     current = row_mask(clip_unit(leap(all_zero, all_one, all_two, all_tile)), populations)
@@ -437,9 +437,10 @@
             flops=ALLELES_COST,
         )
         mix_tile = mix_tile + swap(mix_tile, "samp", 1)
-        tiles = (*parts_of(mix_tile, "samp", 1), *parts_of(all_tile, "var"))
+        mix_tile, all_tile = lax.optimization_barrier((mix_tile, all_tile))
+        tiles = (*parts_of(mix_tile, "samp", 1), *all_parts_of(all_tile, "var"))
         mix_zero, all_zero, both, *gaps = call(
-            functools.partial(leap_kernel, populations),
+            functools.partial(leap_kernel, populations, len(tiles) - 2),
             "leap",
             (*state_out, *sums_out),
             (mix_zero, all_zero, mix_one, all_one, mix_two, all_two, *tiles, alt, ref),

time: 127 us -> 126 us (level)
  waiting for transfers between devices: 39.5 us -> 31.7 us
  starting transfers between devices: 54.2 us -> 60.9 us
    ppermute x47 -> x49, waiting for transfers between devices: 34.5 us -> 26.8 us  [swap(): return lax.ppermute(value, axis, [(i, i ^ mask) for i in range(size)])]
    ppermute x47 -> x49, starting transfers between devices: 43 us -> 49.6 us  [swap(): return lax.ppermute(value, axis, [(i, i ^ mask) for i in range(size)])]
  transfers between devices with their start and end apart: 53 -> 55, of which waited for: 36 -> 35; matrix products, arithmetic and copies ran while one was open for 0% -> 0% of each run, Pallas kernels for 9% -> 9%
where the time goes in v6:
time: 126 us
  starting transfers between devices  60.9 us (48%)
  waiting for transfers between devices  31.7 us (25%)
  Pallas kernels  31.4 us (25%)
    ppermute x49, starting transfers between devices, swap(): return lax.ppermute(value, axis, [(i, i ^ mask) for i in range(size)])  49.6 us
    pallas_call x21, Pallas kernels, call(): pl.pallas_call(kernel, out_shape=tuple((jax.ShapeDtypeStruct(*out) for ou...  27.6 us
    ppermute x49, waiting for transfers between devices, swap(): return lax.ppermute(value, axis, [(i, i ^ mask) for i in range(size)])  26.8 us
    ppermute x3, starting transfers between devices, gather_frequencies(): total = total + lax.ppermute(held, both, pairs)  7.35 us
    ppermute x3, waiting for transfers between devices, gather_frequencies(): arrived.append(lax.ppermute(frequencies, both, pairs))  4.93 us
    ppermute x3, starting transfers between devices, gather_frequencies(): arrived.append(lax.ppermute(frequencies, both, pairs))  3.88 us
    pallas_call x1, Pallas kernels, local(): pl.pallas_call(prepare_kernel, out_shape=(pltpu.VMEM((samples, variants),...  3.79 us
  transfers between devices with their start and end apart: 55, of which 35 were waited for; matrix products, arithmetic and copies ran while one was open for 0% of the time, Pallas kernels for 9%

profile of v6, /device:TPU:0, one launch (start us, length us, event | category | flops | bytes accessed | tf_op | source)
XLA Modules:
  0.0 125.9 jit_solution(1782404192743377241)
XLA Ops:
  4.5 3.2 %collective-permute-done.1 = f32[10,128]{1,0:T(8,128)S(1)} collective-permute-done((f32[10,128]{1,0:T(8,128)}, f32[10,128]{1,0:T(8,128)S(1)}, u32[]{:S(2)}, u32[]{:S(2)}) %collective-permute-start.1) | collective-permute-done | bytes 5152 | tf_op jit(solution)/shard_map/ppermute | solution.py:80
  7.8 1.7 %collective-permute-done = f32[10,128]{1,0:T(8,128)S(1)} collective-permute-done((f32[10,128]{1,0:T(8,128)}, f32[10,128]{1,0:T(8,128)S(1)}, u32[]{:S(2)}, u32[]{:S(2)}) %collective-permute-start) | collective-permute-done | bytes 5152 | tf_op jit(solution)/shard_map/ppermute | solution.py:80
  11.5 4.8 %collective-permute-start.6 = (f32[10,1024]{1,0:T(8,128)S(1)}, f32[10,1024]{1,0:T(8,128)S(1)}, u32[]{:S(2)}, u32[]{:S(2)}) collective-permute-start(f32[10,1024]{1,0:T(8,128)S(1)} %maximum_select_fusion), channel_id=1, source_target_pairs={{0,24},{4,28},{9,17},{13,21},{18,10},{22,14},{27,3},{31,7}} | collective-permute-start | bytes 122888 | tf_op jit(solution)/shard_map/ppermute | solution.py:98
  18.9 3.8 %prepare.1 = (f32[1024,1024]{1,0:T(8,128)S(1)}, f32[1024,1024]{1,0:T(8,128)S(1)}, f32[1,1024]{1,0:T(1,128)S(1)}) custom-call(s32[1024,1024]{1,0:T(8,128)} %genotypes, s32[1024,1024]{1,0:T(8,128)} %observed), custom_call_target="tpu_custom_call" | custom-call | tf_op jit(solution)/shard_map/prepare/pallas_call | solution.py:359
  22.8 3.0 %first.1 = (f32[16,1024]{1,0:T(8,128)S(1)}, f32[16,1024]{1,0:T(8,128)S(1)}, f32[160,128]{1,0:T(8,128)S(1)}, bf16[1024,1024]{1,0:T(8,128)(2,1)S(1)}, bf16[1024,1024]{1,0:T(8,128)(2,1)S(1)}) custom-call(f32[10,1024]{1,0:T(8,128)S(1)} %copy-done, f32[10,1024]{1,0:T(8,128)S(1)} %add_add_fusion.alleles, f32[1024,1024]{1,0:T(8,128)S(1)} %get-tuple-element.70.alt.refs_2_.refs_12_, ...), custom_call_target="tpu_custom_call" | custom-call | tf_op jit(solution)/shard_map/first/pallas_call | solution.py:330
  27.6 2.8 %collective-permute-start.9 = (f32[88,128]{1,0:T(8,128)S(1)}, f32[88,128]{1,0:T(8,128)S(1)}, u32[]{:S(2)}, u32[]{:S(2)}) collective-permute-start(f32[88,128]{1,0:T(8,128)S(1)} %sample_sums.6.refs_0_), channel_id=1, source_target_pairs={{0,3},{1,2},{2,1},{3,0},{4,7},{5,6},{6,5},{7,4},{8,11},{9,10},{10,... | collective-permute-start | bytes 135176 | tf_op jit(solution)/shard_map/ppermute | solution.py:36
  36.6 3.0 %step.3 = (f32[16,1024]{1,0:T(8,128)S(1)}, f32[160,128]{1,0:T(8,128)S(1)}, bf16[1024,1024]{1,0:T(8,128)(2,1)S(1)}, bf16[1024,1024]{1,0:T(8,128)(2,1)S(1)}) custom-call(f32[16,1024]{1,0:T(8,128)S(1)} %get-tuple-element.79.mixture.one.refs_2_, f32[16,1024]{1,0:T(8,128)S(1)} %get-tuple-element.73.alleles.zero.refs_1_, f32[160,128]{1,0:T(8,128)S(1)} %add.62.refs_0_, ...), custom_call_target="tpu_custom_call" | custom-call | tf_op jit(solution)/shard_map/step/pallas_call | solution.py:330
  52.1 2.7 %collective-permute-start.23 = (f32[16,128]{1,0:T(8,128)S(1)}, f32[16,128]{1,0:T(8,128)S(1)}, u32[]{:S(2)}, u32[]{:S(2)}) collective-permute-start(f32[16,128]{1,0:T(8,128)S(1)} %get-tuple-element.93.refs_8_), channel_id=1, source_target_pairs={{0,3},{1,2},{2,1},{3,0},{4,7},{5,6},{6,5},{7,4},{8,11},{9,10},{10,... | collective-permute-start | bytes 24584 | tf_op jit(solution)/shard_map/ppermute | solution.py:36
  58.6 3.4 %leap.2 = (f32[16,1024]{1,0:T(8,128)S(1)}, f32[16,1024]{1,0:T(8,128)S(1)}, f32[160,128]{1,0:T(8,128)S(1)}, bf16[1024,1024]{1,0:T(8,128)(2,1)S(1)}, bf16[1024,1024]{1,0:T(8,128)(2,1)S(1)}) custom-call(f32[16,1024]{1,0:T(8,128)S(1)} %get-tuple-element.72.mixture.zero.refs_0_, f32[16,1024]{1,0:T(8,128)S(1)} %get-tuple-element.73.alleles.zero.refs_1_, ...), custom_call_target="tpu_custom_call" | custom-call | tf_op jit(solution)/shard_map/leap/pallas_call | solution.py:330
  64.5 2.0 %collective-permute-start.28 = (f32[80,128]{1,0:T(8,128)S(1)}, f32[80,128]{1,0:T(8,128)S(1)}, u32[]{:S(2)}, u32[]{:S(2)}) collective-permute-start(f32[80,128]{1,0:T(8,128)S(1)} %sample_sums.8.refs_1_), channel_id=1, source_target_pairs={{0,2},{1,3},{2,0},{3,1},{4,6},{5,7},{6,4},{7,5},{8,10},{9,11},{10,... | collective-permute-start | bytes 122888 | tf_op jit(solution)/shard_map/ppermute | solution.py:36
  70.4 2.0 %collective-permute-done.27.refs_3_ = f32[80,128]{1,0:T(8,128)S(1)} collective-permute-done((f32[80,128]{1,0:T(8,128)S(1)}, f32[80,128]{1,0:T(8,128)S(1)}, u32[]{:S(2)}, u32[]{:S(2)}) %collective-permute-start.27) | collective-permute-done | bytes 40992 | tf_op jit(solution)/shard_map/ppermute | solution.py:36
  72.8 3.0 %step.4 = (f32[16,1024]{1,0:T(8,128)S(1)}, f32[160,128]{1,0:T(8,128)S(1)}, bf16[1024,1024]{1,0:T(8,128)(2,1)S(1)}, bf16[1024,1024]{1,0:T(8,128)(2,1)S(1)}) custom-call(f32[16,1024]{1,0:T(8,128)S(1)} %mixture.7.zero.refs_0_, f32[16,1024]{1,0:T(8,128)S(1)} %get-tuple-element.95.alleles, f32[160,128]{1,0:T(8,128)S(1)} %add.68.refs_0_, ...), custom_call_target="tpu_custom_call" | custom-call | tf_op jit(solution)/shard_map/step/pallas_call | solution.py:330
  80.4 2.7 %collective-permute-start.33 = (f32[80,128]{1,0:T(8,128)S(1)}, f32[80,128]{1,0:T(8,128)S(1)}, u32[]{:S(2)}, u32[]{:S(2)}) collective-permute-start(f32[80,128]{1,0:T(8,128)S(1)} %sample_sums.9.refs_1_), channel_id=1, source_target_pairs={{0,3},{1,2},{2,1},{3,0},{4,7},{5,6},{6,5},{7,4},{8,11},{9,10},{10,... | collective-permute-start | bytes 122888 | tf_op jit(solution)/shard_map/ppermute | solution.py:36
  83.1 1.8 %collective-permute-start.36 = (f32[160,128]{1,0:T(8,128)S(1)}, f32[160,128]{1,0:T(8,128)S(1)}, u32[]{:S(2)}, u32[]{:S(2)}) collective-permute-start(f32[160,128]{1,0:T(8,128)S(1)} %add.70.refs_0_), channel_id=1, source_target_pairs={{0,16},{4,20},{8,24},{12,28},{16,0},{20,4},{24,8},{28,12},{1,17},{... | collective-permute-start | bytes 245768 | tf_op jit(solution)/shard_map/ppermute | solution.py:36
  87.6 3.0 %step.5 = (f32[16,1024]{1,0:T(8,128)S(1)}, f32[160,128]{1,0:T(8,128)S(1)}, bf16[1024,1024]{1,0:T(8,128)(2,1)S(1)}, bf16[1024,1024]{1,0:T(8,128)(2,1)S(1)}) custom-call(f32[16,1024]{1,0:T(8,128)S(1)} %mixture.8.one.refs_2_, f32[16,1024]{1,0:T(8,128)S(1)} %get-tuple-element.101.alleles.zero.refs_1_, f32[160,128]{1,0:T(8,128)S(1)} %add.70.refs_0_, ...), custom_call_target="tpu_custom_call" | custom-call | tf_op jit(solution)/shard_map/step/pallas_call | solution.py:330
  92.5 2.8 %collective-permute-start.40 = (f32[80,128]{1,0:T(8,128)S(1)}, f32[80,128]{1,0:T(8,128)S(1)}, u32[]{:S(2)}, u32[]{:S(2)}) collective-permute-start(f32[80,128]{1,0:T(8,128)S(1)} %sample_sums.10.refs_0_), channel_id=1, source_target_pairs={{0,2},{1,3},{2,0},{3,1},{4,6},{5,7},{6,4},{7,5},{8,10},{9,11},{10,... | collective-permute-start | bytes 122888 | tf_op jit(solution)/shard_map/ppermute | solution.py:36
  96.9 1.8 %collective-permute-start.42 = (f32[160,128]{1,0:T(8,128)S(1)}, f32[160,128]{1,0:T(8,128)S(1)}, u32[]{:S(2)}, u32[]{:S(2)}) collective-permute-start(f32[160,128]{1,0:T(8,128)S(1)} %add.72.refs_0_), channel_id=1, source_target_pairs={{0,16},{4,20},{8,24},{12,28},{16,0},{20,4},{24,8},{28,12},{1,17},{... | collective-permute-start | bytes 245768 | tf_op jit(solution)/shard_map/ppermute | solution.py:36
  98.7 2.5 %collective-permute-done.39.refs_2_ = f32[80,128]{1,0:T(8,128)S(1)} collective-permute-done((f32[80,128]{1,0:T(8,128)S(1)}, f32[80,128]{1,0:T(8,128)S(1)}, u32[]{:S(2)}, u32[]{:S(2)}) %collective-permute-start.39) | collective-permute-done | bytes 40992 | tf_op jit(solution)/shard_map/ppermute | solution.py:36
  104.8 2.7 %collective-permute-start.47 = (f32[16,128]{1,0:T(8,128)S(1)}, f32[16,128]{1,0:T(8,128)S(1)}, u32[]{:S(2)}, u32[]{:S(2)}) collective-permute-start(f32[16,128]{1,0:T(8,128)S(1)} %get-tuple-element.118.refs_8_), channel_id=1, source_target_pairs={{0,3},{1,2},{2,1},{3,0},{4,7},{5,6},{6,5},{7,4},{8,11},{9,10},{10,... | collective-permute-start | bytes 24584 | tf_op jit(solution)/shard_map/ppermute | solution.py:36
  107.5 1.8 %collective-permute-start.45 = (f32[16,128]{1,0:T(8,128)S(1)}, f32[16,128]{1,0:T(8,128)S(1)}, u32[]{:S(2)}, u32[]{:S(2)}) collective-permute-start(f32[16,128]{1,0:T(8,128)S(1)} %add.74.refs_6_), channel_id=1, source_target_pairs={{0,16},{4,20},{8,24},{12,28},{16,0},{20,4},{24,8},{28,12},{1,17},{... | collective-permute-start | bytes 24584 | tf_op jit(solution)/shard_map/ppermute | solution.py:36
  111.2 3.2 %leap.3 = (f32[16,1024]{1,0:T(8,128)S(1)}, f32[16,1024]{1,0:T(8,128)S(1)}, f32[160,128]{1,0:T(8,128)S(1)}, bf16[1024,1024]{1,0:T(8,128)(2,1)S(1)}, bf16[1024,1024]{1,0:T(8,128)(2,1)S(1)}) custom-call(f32[16,1024]{1,0:T(8,128)S(1)} %mixture.7.zero.refs_0_, f32[16,1024]{1,0:T(8,128)S(1)} %get-tuple-element.101.alleles.zero.refs_1_, ...), custom_call_target="tpu_custom_call" | custom-call | tf_op jit(solution)/shard_map/leap/pallas_call | solution.py:330
  116.6 2.5 %collective-permute-start.52 = (f32[80,128]{1,0:T(8,128)S(1)}, f32[80,128]{1,0:T(8,128)S(1)}, u32[]{:S(2)}, u32[]{:S(2)}) collective-permute-start(f32[80,128]{1,0:T(8,128)S(1)} %sample_sums.11.refs_1_), channel_id=1, source_target_pairs={{0,2},{1,3},{2,0},{3,1},{4,6},{5,7},{6,4},{7,5},{8,10},{9,11},{10,... | collective-permute-start | bytes 122888 | tf_op jit(solution)/shard_map/ppermute | solution.py:36
  120.7 1.8 %collective-permute-start.54 = (f32[160,128]{1,0:T(8,128)S(1)}, f32[160,128]{1,0:T(8,128)S(1)}, u32[]{:S(2)}, u32[]{:S(2)}) collective-permute-start(f32[160,128]{1,0:T(8,128)S(1)} %add.76.refs_0_), channel_id=1, source_target_pairs={{0,16},{4,20},{8,24},{12,28},{16,0},{20,4},{24,8},{28,12},{1,17},{... | collective-permute-start | bytes 245768 | tf_op jit(solution)/shard_map/ppermute | solution.py:36
  122.8 2.2 %collective-permute-done.51.refs_3_ = f32[80,128]{1,0:T(8,128)S(1)} collective-permute-done((f32[80,128]{1,0:T(8,128)S(1)}, f32[80,128]{1,0:T(8,128)S(1)}, u32[]{:S(2)}, u32[]{:S(2)}) %collective-permute-start.51) | collective-permute-done | bytes 40992 | tf_op jit(solution)/shard_map/ppermute | solution.py:36
  (131 shorter events, 61.0 us)
Async XLA Ops:
  0.6 7.2 %collective-permute-start.1 = (f32[10,128]{1,0:T(8,128)}, f32[10,128]{1,0:T(8,128)S(1)}, u32[]{:S(2)}, u32[]{:S(2)}) collective-permute-start(f32[10,128]{1,0:T(8,128)} %param.7), channel_id=1, source_target_pairs={{2,0},{6,4},{11,9},{15,13},{16,18},{20,22},{25,27},{29,31}} | collective-permute-start | bytes 15368 | tf_op jit(solution)/shard_map/ppermute | solution.py:80
  1.9 7.6 %collective-permute-start = (f32[10,128]{1,0:T(8,128)}, f32[10,128]{1,0:T(8,128)S(1)}, u32[]{:S(2)}, u32[]{:S(2)}) collective-permute-start(f32[10,128]{1,0:T(8,128)} %param.7), channel_id=1, source_target_pairs={{3,0},{7,4},{10,9},{14,13},{17,18},{21,22},{24,27},{28,31}} | collective-permute-start | bytes 15368 | tf_op jit(solution)/shard_map/ppermute | solution.py:80
  3.2 6.3 %collective-permute-start.2 = (f32[10,128]{1,0:T(8,128)}, f32[10,128]{1,0:T(8,128)S(1)}, u32[]{:S(2)}, u32[]{:S(2)}) collective-permute-start(f32[10,128]{1,0:T(8,128)} %param.7), channel_id=1, source_target_pairs={{1,0},{5,4},{8,9},{12,13},{19,18},{23,22},{26,27},{30,31}} | collective-permute-start | bytes 15368 | tf_op jit(solution)/shard_map/ppermute | solution.py:80
  11.5 11.2 %collective-permute-start.6 = (f32[10,1024]{1,0:T(8,128)S(1)}, f32[10,1024]{1,0:T(8,128)S(1)}, u32[]{:S(2)}, u32[]{:S(2)}) collective-permute-start(f32[10,1024]{1,0:T(8,128)S(1)} %maximum_select_fusion), channel_id=1, source_target_pairs={{0,24},{4,28},{9,17},{13,21},{18,10},{22,14},{27,3},{31,7}} | collective-permute-start | bytes 122888 | tf_op jit(solution)/shard_map/ppermute | solution.py:98
  16.3 6.4 %collective-permute-start.5 = (f32[10,1024]{1,0:T(8,128)S(1)}, f32[10,1024]{1,0:T(8,128)S(1)}, u32[]{:S(2)}, u32[]{:S(2)}) collective-permute-start(f32[10,1024]{1,0:T(8,128)S(1)} %maximum_select_fusion), channel_id=1, source_target_pairs={{0,16},{4,20},{9,25},{13,29},{18,2},{22,6},{27,11},{31,15}} | collective-permute-start | bytes 122888 | tf_op jit(solution)/shard_map/ppermute | solution.py:98
  17.6 5.1 %collective-permute-start.4 = (f32[10,1024]{1,0:T(8,128)S(1)}, f32[10,1024]{1,0:T(8,128)S(1)}, u32[]{:S(2)}, u32[]{:S(2)}) collective-permute-start(f32[10,1024]{1,0:T(8,128)S(1)} %maximum_select_fusion), channel_id=1, source_target_pairs={{0,8},{4,12},{9,1},{13,5},{18,26},{22,30},{27,19},{31,23}} | collective-permute-start | bytes 122888 | tf_op jit(solution)/shard_map/ppermute | solution.py:98
  27.6 6.7 %collective-permute-start.10 = (f32[88,128]{1,0:T(8,128)S(1)}, f32[88,128]{1,0:T(8,128)S(1)}, u32[]{:S(2)}, u32[]{:S(2)}) collective-permute-start(f32[88,128]{1,0:T(8,128)S(1)} %sample_sums.6.refs_0_), channel_id=1, source_target_pairs={{0,2},{1,3},{2,0},{3,1},{4,6},{5,7},{6,4},{7,5},{8,10},{9,11},{10,... | collective-permute-start | bytes 135176 | tf_op jit(solution)/shard_map/ppermute | solution.py:36
  27.6 6.7 %collective-permute-start.9 = (f32[88,128]{1,0:T(8,128)S(1)}, f32[88,128]{1,0:T(8,128)S(1)}, u32[]{:S(2)}, u32[]{:S(2)}) collective-permute-start(f32[88,128]{1,0:T(8,128)S(1)} %sample_sums.6.refs_0_), channel_id=1, source_target_pairs={{0,3},{1,2},{2,1},{3,0},{4,7},{5,6},{6,5},{7,4},{8,11},{9,10},{10,... | collective-permute-start | bytes 135176 | tf_op jit(solution)/shard_map/ppermute | solution.py:36
  41.7 5.9 %collective-permute-start.16 = (f32[80,128]{1,0:T(8,128)S(1)}, f32[80,128]{1,0:T(8,128)S(1)}, u32[]{:S(2)}, u32[]{:S(2)}) collective-permute-start(f32[80,128]{1,0:T(8,128)S(1)} %sample_sums.7.refs_0_), channel_id=1, source_target_pairs={{0,2},{1,3},{2,0},{3,1},{4,6},{5,7},{6,4},{7,5},{8,10},{9,11},{10,... | collective-permute-start | bytes 122888 | tf_op jit(solution)/shard_map/ppermute | solution.py:36
  42.6 5.9 %collective-permute-start.15 = (f32[80,128]{1,0:T(8,128)S(1)}, f32[80,128]{1,0:T(8,128)S(1)}, u32[]{:S(2)}, u32[]{:S(2)}) collective-permute-start(f32[80,128]{1,0:T(8,128)S(1)} %sample_sums.7.refs_0_), channel_id=1, source_target_pairs={{0,3},{1,2},{2,1},{3,0},{4,7},{5,6},{6,5},{7,4},{8,11},{9,10},{10,... | collective-permute-start | bytes 122888 | tf_op jit(solution)/shard_map/ppermute | solution.py:36
  51.5 5.1 %collective-permute-start.24 = (f32[16,128]{1,0:T(8,128)S(1)}, f32[16,128]{1,0:T(8,128)S(1)}, u32[]{:S(2)}, u32[]{:S(2)}) collective-permute-start(f32[16,128]{1,0:T(8,128)S(1)} %get-tuple-element.93.refs_8_), channel_id=1, source_target_pairs={{0,2},{1,3},{2,0},{3,1},{4,6},{5,7},{6,4},{7,5},{8,10},{9,11},{10,... | collective-permute-start | bytes 24584 | tf_op jit(solution)/shard_map/ppermute | solution.py:36
  52.1 5.4 %collective-permute-start.23 = (f32[16,128]{1,0:T(8,128)S(1)}, f32[16,128]{1,0:T(8,128)S(1)}, u32[]{:S(2)}, u32[]{:S(2)}) collective-permute-start(f32[16,128]{1,0:T(8,128)S(1)} %get-tuple-element.93.refs_8_), channel_id=1, source_target_pairs={{0,3},{1,2},{2,1},{3,0},{4,7},{5,6},{6,5},{7,4},{8,11},{9,10},{10,... | collective-permute-start | bytes 24584 | tf_op jit(solution)/shard_map/ppermute | solution.py:36
  64.5 5.9 %collective-permute-start.28 = (f32[80,128]{1,0:T(8,128)S(1)}, f32[80,128]{1,0:T(8,128)S(1)}, u32[]{:S(2)}, u32[]{:S(2)}) collective-permute-start(f32[80,128]{1,0:T(8,128)S(1)} %sample_sums.8.refs_1_), channel_id=1, source_target_pairs={{0,2},{1,3},{2,0},{3,1},{4,6},{5,7},{6,4},{7,5},{8,10},{9,11},{10,... | collective-permute-start | bytes 122888 | tf_op jit(solution)/shard_map/ppermute | solution.py:36
  66.5 5.9 %collective-permute-start.27 = (f32[80,128]{1,0:T(8,128)S(1)}, f32[80,128]{1,0:T(8,128)S(1)}, u32[]{:S(2)}, u32[]{:S(2)}) collective-permute-start(f32[80,128]{1,0:T(8,128)S(1)} %sample_sums.8.refs_1_), channel_id=1, source_target_pairs={{0,3},{1,2},{2,1},{3,0},{4,7},{5,6},{6,5},{7,4},{8,11},{9,10},{10,... | collective-permute-start | bytes 122888 | tf_op jit(solution)/shard_map/ppermute | solution.py:36
  77.2 5.9 %collective-permute-start.35 = (f32[160,128]{1,0:T(8,128)S(1)}, f32[160,128]{1,0:T(8,128)S(1)}, u32[]{:S(2)}, u32[]{:S(2)}) collective-permute-start(f32[160,128]{1,0:T(8,128)S(1)} %add.69), channel_id=1, source_target_pairs={{0,8},{4,12},{8,0},{12,4},{16,24},{20,28},{24,16},{28,20},{1,9},{5... | collective-permute-start | bytes 245768 | tf_op jit(solution)/shard_map/ppermute | solution.py:36
  78.7 6.2 %collective-permute-start.34 = (f32[80,128]{1,0:T(8,128)S(1)}, f32[80,128]{1,0:T(8,128)S(1)}, u32[]{:S(2)}, u32[]{:S(2)}) collective-permute-start(f32[80,128]{1,0:T(8,128)S(1)} %sample_sums.9.refs_1_), channel_id=1, source_target_pairs={{0,2},{1,3},{2,0},{3,1},{4,6},{5,7},{6,4},{7,5},{8,10},{9,11},{10,... | collective-permute-start | bytes 122888 | tf_op jit(solution)/shard_map/ppermute | solution.py:36
  80.4 6.0 %collective-permute-start.33 = (f32[80,128]{1,0:T(8,128)S(1)}, f32[80,128]{1,0:T(8,128)S(1)}, u32[]{:S(2)}, u32[]{:S(2)}) collective-permute-start(f32[80,128]{1,0:T(8,128)S(1)} %sample_sums.9.refs_1_), channel_id=1, source_target_pairs={{0,3},{1,2},{2,1},{3,0},{4,7},{5,6},{6,5},{7,4},{8,11},{9,10},{10,... | collective-permute-start | bytes 122888 | tf_op jit(solution)/shard_map/ppermute | solution.py:36
  92.5 6.2 %collective-permute-start.40 = (f32[80,128]{1,0:T(8,128)S(1)}, f32[80,128]{1,0:T(8,128)S(1)}, u32[]{:S(2)}, u32[]{:S(2)}) collective-permute-start(f32[80,128]{1,0:T(8,128)S(1)} %sample_sums.10.refs_0_), channel_id=1, source_target_pairs={{0,2},{1,3},{2,0},{3,1},{4,6},{5,7},{6,4},{7,5},{8,10},{9,11},{10,... | collective-permute-start | bytes 122888 | tf_op jit(solution)/shard_map/ppermute | solution.py:36
  95.3 5.9 %collective-permute-start.39 = (f32[80,128]{1,0:T(8,128)S(1)}, f32[80,128]{1,0:T(8,128)S(1)}, u32[]{:S(2)}, u32[]{:S(2)}) collective-permute-start(f32[80,128]{1,0:T(8,128)S(1)} %sample_sums.10.refs_0_), channel_id=1, source_target_pairs={{0,3},{1,2},{2,1},{3,0},{4,7},{5,6},{6,5},{7,4},{8,11},{9,10},{10,... | collective-permute-start | bytes 122888 | tf_op jit(solution)/shard_map/ppermute | solution.py:36
  96.9 5.7 %collective-permute-start.42 = (f32[160,128]{1,0:T(8,128)S(1)}, f32[160,128]{1,0:T(8,128)S(1)}, u32[]{:S(2)}, u32[]{:S(2)}) collective-permute-start(f32[160,128]{1,0:T(8,128)S(1)} %add.72.refs_0_), channel_id=1, source_target_pairs={{0,16},{4,20},{8,24},{12,28},{16,0},{20,4},{24,8},{28,12},{1,17},{... | collective-permute-start | bytes 245768 | tf_op jit(solution)/shard_map/ppermute | solution.py:36
  103.9 5.4 %collective-permute-start.48 = (f32[16,128]{1,0:T(8,128)S(1)}, f32[16,128]{1,0:T(8,128)S(1)}, u32[]{:S(2)}, u32[]{:S(2)}) collective-permute-start(f32[16,128]{1,0:T(8,128)S(1)} %get-tuple-element.118.refs_8_), channel_id=1, source_target_pairs={{0,2},{1,3},{2,0},{3,1},{4,6},{5,7},{6,4},{7,5},{8,10},{9,11},{10,... | collective-permute-start | bytes 24584 | tf_op jit(solution)/shard_map/ppermute | solution.py:36
  104.8 5.4 %collective-permute-start.47 = (f32[16,128]{1,0:T(8,128)S(1)}, f32[16,128]{1,0:T(8,128)S(1)}, u32[]{:S(2)}, u32[]{:S(2)}) collective-permute-start(f32[16,128]{1,0:T(8,128)S(1)} %get-tuple-element.118.refs_8_), channel_id=1, source_target_pairs={{0,3},{1,2},{2,1},{3,0},{4,7},{5,6},{6,5},{7,4},{8,11},{9,10},{10,... | collective-permute-start | bytes 24584 | tf_op jit(solution)/shard_map/ppermute | solution.py:36
  116.6 6.2 %collective-permute-start.52 = (f32[80,128]{1,0:T(8,128)S(1)}, f32[80,128]{1,0:T(8,128)S(1)}, u32[]{:S(2)}, u32[]{:S(2)}) collective-permute-start(f32[80,128]{1,0:T(8,128)S(1)} %sample_sums.11.refs_1_), channel_id=1, source_target_pairs={{0,2},{1,3},{2,0},{3,1},{4,6},{5,7},{6,4},{7,5},{8,10},{9,11},{10,... | collective-permute-start | bytes 122888 | tf_op jit(solution)/shard_map/ppermute | solution.py:36
  119.0 5.9 %collective-permute-start.51 = (f32[80,128]{1,0:T(8,128)S(1)}, f32[80,128]{1,0:T(8,128)S(1)}, u32[]{:S(2)}, u32[]{:S(2)}) collective-permute-start(f32[80,128]{1,0:T(8,128)S(1)} %sample_sums.11.refs_1_), channel_id=1, source_target_pairs={{0,3},{1,2},{2,1},{3,0},{4,7},{5,6},{6,5},{7,4},{8,11},{9,10},{10,... | collective-permute-start | bytes 122888 | tf_op jit(solution)/shard_map/ppermute | solution.py:36
  (32 other events, 120.4 us)

commit v7 on v6

--- a/solution.py
+++ b/solution.py
@@ -15,7 +15,7 @@
 SUBLANES = 8
 LANES = 128
 VMEM_BYTES = 32 * 2**20
-TALL, WIDE = 512, 1024
+TALL, WIDE = 1024, 1024
 MIXTURE_COST = 5 * 10**9
 ALLELES_COST = 5 * 10**9
 

time: 126 us -> 127 us (level)
  no operation moved by 1% of the time
where the time goes in v7:
time: 127 us
  starting transfers between devices  60.9 us (48%)
  Pallas kernels  32.6 us (26%)
  waiting for transfers between devices  31.6 us (25%)
    ppermute x49, starting transfers between devices, swap(): return lax.ppermute(value, axis, [(i, i ^ mask) for i in range(size)])  49.7 us
    pallas_call x21, Pallas kernels, call(): pl.pallas_call(kernel, out_shape=tuple((jax.ShapeDtypeStruct(*out) for ou...  28.8 us
    ppermute x49, waiting for transfers between devices, swap(): return lax.ppermute(value, axis, [(i, i ^ mask) for i in range(size)])  26.7 us
    ppermute x3, starting transfers between devices, gather_frequencies(): total = total + lax.ppermute(held, both, pairs)  7.35 us
    ppermute x3, waiting for transfers between devices, gather_frequencies(): arrived.append(lax.ppermute(frequencies, both, pairs))  4.93 us
    ppermute x3, starting transfers between devices, gather_frequencies(): arrived.append(lax.ppermute(frequencies, both, pairs))  3.88 us
    pallas_call x1, Pallas kernels, local(): pl.pallas_call(prepare_kernel, out_shape=(pltpu.VMEM((samples, variants),...  3.79 us
  transfers between devices with their start and end apart: 55, of which 35 were waited for; matrix products, arithmetic and copies ran while one was open for 0% of the time, Pallas kernels for 9%

profile of v7, /device:TPU:0, one launch (start us, length us, event | category | flops | bytes accessed | tf_op | source)
XLA Modules:
  0.0 127.0 jit_solution(10589972440804507728)
XLA Ops:
  4.5 3.2 %collective-permute-done.1 = f32[10,128]{1,0:T(8,128)S(1)} collective-permute-done((f32[10,128]{1,0:T(8,128)}, f32[10,128]{1,0:T(8,128)S(1)}, u32[]{:S(2)}, u32[]{:S(2)}) %collective-permute-start.1) | collective-permute-done | bytes 5152 | tf_op jit(solution)/shard_map/ppermute | solution.py:80
  11.5 4.8 %collective-permute-start.6 = (f32[10,1024]{1,0:T(8,128)S(1)}, f32[10,1024]{1,0:T(8,128)S(1)}, u32[]{:S(2)}, u32[]{:S(2)}) collective-permute-start(f32[10,1024]{1,0:T(8,128)S(1)} %maximum_select_fusion), channel_id=1, source_target_pairs={{0,24},{4,28},{9,17},{13,21},{18,10},{22,14},{27,3},{31,7}} | collective-permute-start | bytes 122888 | tf_op jit(solution)/shard_map/ppermute | solution.py:98
  18.9 3.8 %prepare.1 = (f32[1024,1024]{1,0:T(8,128)S(1)}, f32[1024,1024]{1,0:T(8,128)S(1)}, f32[1,1024]{1,0:T(1,128)S(1)}) custom-call(s32[1024,1024]{1,0:T(8,128)} %genotypes, s32[1024,1024]{1,0:T(8,128)} %observed), custom_call_target="tpu_custom_call" | custom-call | tf_op jit(solution)/shard_map/prepare/pallas_call | solution.py:359
  22.8 3.2 %first.1 = (f32[16,1024]{1,0:T(8,128)S(1)}, f32[16,1024]{1,0:T(8,128)S(1)}, f32[160,128]{1,0:T(8,128)S(1)}, bf16[1024,1024]{1,0:T(8,128)(2,1)S(1)}, bf16[1024,1024]{1,0:T(8,128)(2,1)S(1)}) custom-call(f32[10,1024]{1,0:T(8,128)S(1)} %copy-done, f32[10,1024]{1,0:T(8,128)S(1)} %add_add_fusion.alleles, f32[1024,1024]{1,0:T(8,128)S(1)} %get-tuple-element.70.alt.refs_2_.refs_12_, ...), custom_call_target="tpu_custom_call" | custom-call | tf_op jit(solution)/shard_map/first/pallas_call | solution.py:330
  27.8 2.8 %collective-permute-start.9 = (f32[88,128]{1,0:T(8,128)S(1)}, f32[88,128]{1,0:T(8,128)S(1)}, u32[]{:S(2)}, u32[]{:S(2)}) collective-permute-start(f32[88,128]{1,0:T(8,128)S(1)} %sample_sums.6.refs_0_), channel_id=1, source_target_pairs={{0,3},{1,2},{2,1},{3,0},{4,7},{5,6},{6,5},{7,4},{8,11},{9,10},{10,... | collective-permute-start | bytes 135176 | tf_op jit(solution)/shard_map/ppermute | solution.py:36
  36.7 3.2 %step.3 = (f32[16,1024]{1,0:T(8,128)S(1)}, f32[160,128]{1,0:T(8,128)S(1)}, bf16[1024,1024]{1,0:T(8,128)(2,1)S(1)}, bf16[1024,1024]{1,0:T(8,128)(2,1)S(1)}) custom-call(f32[16,1024]{1,0:T(8,128)S(1)} %get-tuple-element.79.mixture.one.refs_2_, f32[16,1024]{1,0:T(8,128)S(1)} %get-tuple-element.73.alleles.zero.refs_1_, f32[160,128]{1,0:T(8,128)S(1)} %add.62.refs_0_, ...), custom_call_target="tpu_custom_call" | custom-call | tf_op jit(solution)/shard_map/step/pallas_call | solution.py:330
  52.4 2.7 %collective-permute-start.23 = (f32[16,128]{1,0:T(8,128)S(1)}, f32[16,128]{1,0:T(8,128)S(1)}, u32[]{:S(2)}, u32[]{:S(2)}) collective-permute-start(f32[16,128]{1,0:T(8,128)S(1)} %get-tuple-element.93.refs_8_), channel_id=1, source_target_pairs={{0,3},{1,2},{2,1},{3,0},{4,7},{5,6},{6,5},{7,4},{8,11},{9,10},{10,... | collective-permute-start | bytes 24584 | tf_op jit(solution)/shard_map/ppermute | solution.py:36
  58.9 3.5 %leap.2 = (f32[16,1024]{1,0:T(8,128)S(1)}, f32[16,1024]{1,0:T(8,128)S(1)}, f32[160,128]{1,0:T(8,128)S(1)}, bf16[1024,1024]{1,0:T(8,128)(2,1)S(1)}, bf16[1024,1024]{1,0:T(8,128)(2,1)S(1)}) custom-call(f32[16,1024]{1,0:T(8,128)S(1)} %get-tuple-element.72.mixture.zero.refs_0_, f32[16,1024]{1,0:T(8,128)S(1)} %get-tuple-element.73.alleles.zero.refs_1_, ...), custom_call_target="tpu_custom_call" | custom-call | tf_op jit(solution)/shard_map/leap/pallas_call | solution.py:330
  65.0 2.0 %collective-permute-start.28 = (f32[80,128]{1,0:T(8,128)S(1)}, f32[80,128]{1,0:T(8,128)S(1)}, u32[]{:S(2)}, u32[]{:S(2)}) collective-permute-start(f32[80,128]{1,0:T(8,128)S(1)} %sample_sums.8.refs_1_), channel_id=1, source_target_pairs={{0,2},{1,3},{2,0},{3,1},{4,6},{5,7},{6,4},{7,5},{8,10},{9,11},{10,... | collective-permute-start | bytes 122888 | tf_op jit(solution)/shard_map/ppermute | solution.py:36
  70.9 2.0 %collective-permute-done.27.refs_3_ = f32[80,128]{1,0:T(8,128)S(1)} collective-permute-done((f32[80,128]{1,0:T(8,128)S(1)}, f32[80,128]{1,0:T(8,128)S(1)}, u32[]{:S(2)}, u32[]{:S(2)}) %collective-permute-start.27) | collective-permute-done | bytes 40992 | tf_op jit(solution)/shard_map/ppermute | solution.py:36
  73.3 3.2 %step.4 = (f32[16,1024]{1,0:T(8,128)S(1)}, f32[160,128]{1,0:T(8,128)S(1)}, bf16[1024,1024]{1,0:T(8,128)(2,1)S(1)}, bf16[1024,1024]{1,0:T(8,128)(2,1)S(1)}) custom-call(f32[16,1024]{1,0:T(8,128)S(1)} %mixture.7.zero.refs_0_, f32[16,1024]{1,0:T(8,128)S(1)} %get-tuple-element.95.alleles, f32[160,128]{1,0:T(8,128)S(1)} %add.68.refs_0_, ...), custom_call_target="tpu_custom_call" | custom-call | tf_op jit(solution)/shard_map/step/pallas_call | solution.py:330
  79.3 1.7 %collective-permute-start.34 = (f32[80,128]{1,0:T(8,128)S(1)}, f32[80,128]{1,0:T(8,128)S(1)}, u32[]{:S(2)}, u32[]{:S(2)}) collective-permute-start(f32[80,128]{1,0:T(8,128)S(1)} %sample_sums.9.refs_1_), channel_id=1, source_target_pairs={{0,2},{1,3},{2,0},{3,1},{4,6},{5,7},{6,4},{7,5},{8,10},{9,11},{10,... | collective-permute-start | bytes 122888 | tf_op jit(solution)/shard_map/ppermute | solution.py:36
  81.0 2.7 %collective-permute-start.33 = (f32[80,128]{1,0:T(8,128)S(1)}, f32[80,128]{1,0:T(8,128)S(1)}, u32[]{:S(2)}, u32[]{:S(2)}) collective-permute-start(f32[80,128]{1,0:T(8,128)S(1)} %sample_sums.9.refs_1_), channel_id=1, source_target_pairs={{0,3},{1,2},{2,1},{3,0},{4,7},{5,6},{6,5},{7,4},{8,11},{9,10},{10,... | collective-permute-start | bytes 122888 | tf_op jit(solution)/shard_map/ppermute | solution.py:36
  83.7 1.8 %collective-permute-start.36 = (f32[160,128]{1,0:T(8,128)S(1)}, f32[160,128]{1,0:T(8,128)S(1)}, u32[]{:S(2)}, u32[]{:S(2)}) collective-permute-start(f32[160,128]{1,0:T(8,128)S(1)} %add.70.refs_0_), channel_id=1, source_target_pairs={{0,16},{4,20},{8,24},{12,28},{16,0},{20,4},{24,8},{28,12},{1,17},{... | collective-permute-start | bytes 245768 | tf_op jit(solution)/shard_map/ppermute | solution.py:36
  88.2 3.2 %step.5 = (f32[16,1024]{1,0:T(8,128)S(1)}, f32[160,128]{1,0:T(8,128)S(1)}, bf16[1024,1024]{1,0:T(8,128)(2,1)S(1)}, bf16[1024,1024]{1,0:T(8,128)(2,1)S(1)}) custom-call(f32[16,1024]{1,0:T(8,128)S(1)} %mixture.8.one.refs_2_, f32[16,1024]{1,0:T(8,128)S(1)} %get-tuple-element.101.alleles.zero.refs_1_, f32[160,128]{1,0:T(8,128)S(1)} %add.70.refs_0_, ...), custom_call_target="tpu_custom_call" | custom-call | tf_op jit(solution)/shard_map/step/pallas_call | solution.py:330
  93.3 2.8 %collective-permute-start.40 = (f32[80,128]{1,0:T(8,128)S(1)}, f32[80,128]{1,0:T(8,128)S(1)}, u32[]{:S(2)}, u32[]{:S(2)}) collective-permute-start(f32[80,128]{1,0:T(8,128)S(1)} %sample_sums.10.refs_0_), channel_id=1, source_target_pairs={{0,2},{1,3},{2,0},{3,1},{4,6},{5,7},{6,4},{7,5},{8,10},{9,11},{10,... | collective-permute-start | bytes 122888 | tf_op jit(solution)/shard_map/ppermute | solution.py:36
  97.7 1.8 %collective-permute-start.42 = (f32[160,128]{1,0:T(8,128)S(1)}, f32[160,128]{1,0:T(8,128)S(1)}, u32[]{:S(2)}, u32[]{:S(2)}) collective-permute-start(f32[160,128]{1,0:T(8,128)S(1)} %add.72.refs_0_), channel_id=1, source_target_pairs={{0,16},{4,20},{8,24},{12,28},{16,0},{20,4},{24,8},{28,12},{1,17},{... | collective-permute-start | bytes 245768 | tf_op jit(solution)/shard_map/ppermute | solution.py:36
  99.4 2.5 %collective-permute-done.39.refs_2_ = f32[80,128]{1,0:T(8,128)S(1)} collective-permute-done((f32[80,128]{1,0:T(8,128)S(1)}, f32[80,128]{1,0:T(8,128)S(1)}, u32[]{:S(2)}, u32[]{:S(2)}) %collective-permute-start.39) | collective-permute-done | bytes 40992 | tf_op jit(solution)/shard_map/ppermute | solution.py:36
  105.6 2.7 %collective-permute-start.47 = (f32[16,128]{1,0:T(8,128)S(1)}, f32[16,128]{1,0:T(8,128)S(1)}, u32[]{:S(2)}, u32[]{:S(2)}) collective-permute-start(f32[16,128]{1,0:T(8,128)S(1)} %get-tuple-element.118.refs_8_), channel_id=1, source_target_pairs={{0,3},{1,2},{2,1},{3,0},{4,7},{5,6},{6,5},{7,4},{8,11},{9,10},{10,... | collective-permute-start | bytes 24584 | tf_op jit(solution)/shard_map/ppermute | solution.py:36
  108.2 1.8 %collective-permute-start.45 = (f32[16,128]{1,0:T(8,128)S(1)}, f32[16,128]{1,0:T(8,128)S(1)}, u32[]{:S(2)}, u32[]{:S(2)}) collective-permute-start(f32[16,128]{1,0:T(8,128)S(1)} %add.74.refs_6_), channel_id=1, source_target_pairs={{0,16},{4,20},{8,24},{12,28},{16,0},{20,4},{24,8},{28,12},{1,17},{... | collective-permute-start | bytes 24584 | tf_op jit(solution)/shard_map/ppermute | solution.py:36
  112.0 3.6 %leap.3 = (f32[16,1024]{1,0:T(8,128)S(1)}, f32[16,1024]{1,0:T(8,128)S(1)}, f32[160,128]{1,0:T(8,128)S(1)}, bf16[1024,1024]{1,0:T(8,128)(2,1)S(1)}, bf16[1024,1024]{1,0:T(8,128)(2,1)S(1)}) custom-call(f32[16,1024]{1,0:T(8,128)S(1)} %mixture.7.zero.refs_0_, f32[16,1024]{1,0:T(8,128)S(1)} %get-tuple-element.101.alleles.zero.refs_1_, ...), custom_call_target="tpu_custom_call" | custom-call | tf_op jit(solution)/shard_map/leap/pallas_call | solution.py:330
  117.7 2.5 %collective-permute-start.52 = (f32[80,128]{1,0:T(8,128)S(1)}, f32[80,128]{1,0:T(8,128)S(1)}, u32[]{:S(2)}, u32[]{:S(2)}) collective-permute-start(f32[80,128]{1,0:T(8,128)S(1)} %sample_sums.11.refs_1_), channel_id=1, source_target_pairs={{0,2},{1,3},{2,0},{3,1},{4,6},{5,7},{6,4},{7,5},{8,10},{9,11},{10,... | collective-permute-start | bytes 122888 | tf_op jit(solution)/shard_map/ppermute | solution.py:36
  121.9 1.8 %collective-permute-start.54 = (f32[160,128]{1,0:T(8,128)S(1)}, f32[160,128]{1,0:T(8,128)S(1)}, u32[]{:S(2)}, u32[]{:S(2)}) collective-permute-start(f32[160,128]{1,0:T(8,128)S(1)} %add.76.refs_0_), channel_id=1, source_target_pairs={{0,16},{4,20},{8,24},{12,28},{16,0},{20,4},{24,8},{28,12},{1,17},{... | collective-permute-start | bytes 245768 | tf_op jit(solution)/shard_map/ppermute | solution.py:36
  123.9 2.2 %collective-permute-done.51.refs_3_ = f32[80,128]{1,0:T(8,128)S(1)} collective-permute-done((f32[80,128]{1,0:T(8,128)S(1)}, f32[80,128]{1,0:T(8,128)S(1)}, u32[]{:S(2)}, u32[]{:S(2)}) %collective-permute-start.51) | collective-permute-done | bytes 40992 | tf_op jit(solution)/shard_map/ppermute | solution.py:36
  (131 shorter events, 61.0 us)
Async XLA Ops:
  0.6 7.2 %collective-permute-start.1 = (f32[10,128]{1,0:T(8,128)}, f32[10,128]{1,0:T(8,128)S(1)}, u32[]{:S(2)}, u32[]{:S(2)}) collective-permute-start(f32[10,128]{1,0:T(8,128)} %param.7), channel_id=1, source_target_pairs={{2,0},{6,4},{11,9},{15,13},{16,18},{20,22},{25,27},{29,31}} | collective-permute-start | bytes 15368 | tf_op jit(solution)/shard_map/ppermute | solution.py:80
  1.9 7.6 %collective-permute-start = (f32[10,128]{1,0:T(8,128)}, f32[10,128]{1,0:T(8,128)S(1)}, u32[]{:S(2)}, u32[]{:S(2)}) collective-permute-start(f32[10,128]{1,0:T(8,128)} %param.7), channel_id=1, source_target_pairs={{3,0},{7,4},{10,9},{14,13},{17,18},{21,22},{24,27},{28,31}} | collective-permute-start | bytes 15368 | tf_op jit(solution)/shard_map/ppermute | solution.py:80
  3.2 6.3 %collective-permute-start.2 = (f32[10,128]{1,0:T(8,128)}, f32[10,128]{1,0:T(8,128)S(1)}, u32[]{:S(2)}, u32[]{:S(2)}) collective-permute-start(f32[10,128]{1,0:T(8,128)} %param.7), channel_id=1, source_target_pairs={{1,0},{5,4},{8,9},{12,13},{19,18},{23,22},{26,27},{30,31}} | collective-permute-start | bytes 15368 | tf_op jit(solution)/shard_map/ppermute | solution.py:80
  11.5 11.2 %collective-permute-start.6 = (f32[10,1024]{1,0:T(8,128)S(1)}, f32[10,1024]{1,0:T(8,128)S(1)}, u32[]{:S(2)}, u32[]{:S(2)}) collective-permute-start(f32[10,1024]{1,0:T(8,128)S(1)} %maximum_select_fusion), channel_id=1, source_target_pairs={{0,24},{4,28},{9,17},{13,21},{18,10},{22,14},{27,3},{31,7}} | collective-permute-start | bytes 122888 | tf_op jit(solution)/shard_map/ppermute | solution.py:98
  16.3 6.4 %collective-permute-start.5 = (f32[10,1024]{1,0:T(8,128)S(1)}, f32[10,1024]{1,0:T(8,128)S(1)}, u32[]{:S(2)}, u32[]{:S(2)}) collective-permute-start(f32[10,1024]{1,0:T(8,128)S(1)} %maximum_select_fusion), channel_id=1, source_target_pairs={{0,16},{4,20},{9,25},{13,29},{18,2},{22,6},{27,11},{31,15}} | collective-permute-start | bytes 122888 | tf_op jit(solution)/shard_map/ppermute | solution.py:98
  17.6 5.1 %collective-permute-start.4 = (f32[10,1024]{1,0:T(8,128)S(1)}, f32[10,1024]{1,0:T(8,128)S(1)}, u32[]{:S(2)}, u32[]{:S(2)}) collective-permute-start(f32[10,1024]{1,0:T(8,128)S(1)} %maximum_select_fusion), channel_id=1, source_target_pairs={{0,8},{4,12},{9,1},{13,5},{18,26},{22,30},{27,19},{31,23}} | collective-permute-start | bytes 122888 | tf_op jit(solution)/shard_map/ppermute | solution.py:98
  27.8 6.7 %collective-permute-start.10 = (f32[88,128]{1,0:T(8,128)S(1)}, f32[88,128]{1,0:T(8,128)S(1)}, u32[]{:S(2)}, u32[]{:S(2)}) collective-permute-start(f32[88,128]{1,0:T(8,128)S(1)} %sample_sums.6.refs_0_), channel_id=1, source_target_pairs={{0,2},{1,3},{2,0},{3,1},{4,6},{5,7},{6,4},{7,5},{8,10},{9,11},{10,... | collective-permute-start | bytes 135176 | tf_op jit(solution)/shard_map/ppermute | solution.py:36
  27.8 6.7 %collective-permute-start.9 = (f32[88,128]{1,0:T(8,128)S(1)}, f32[88,128]{1,0:T(8,128)S(1)}, u32[]{:S(2)}, u32[]{:S(2)}) collective-permute-start(f32[88,128]{1,0:T(8,128)S(1)} %sample_sums.6.refs_0_), channel_id=1, source_target_pairs={{0,3},{1,2},{2,1},{3,0},{4,7},{5,6},{6,5},{7,4},{8,11},{9,10},{10,... | collective-permute-start | bytes 135176 | tf_op jit(solution)/shard_map/ppermute | solution.py:36
  42.0 5.9 %collective-permute-start.16 = (f32[80,128]{1,0:T(8,128)S(1)}, f32[80,128]{1,0:T(8,128)S(1)}, u32[]{:S(2)}, u32[]{:S(2)}) collective-permute-start(f32[80,128]{1,0:T(8,128)S(1)} %sample_sums.7.refs_0_), channel_id=1, source_target_pairs={{0,2},{1,3},{2,0},{3,1},{4,6},{5,7},{6,4},{7,5},{8,10},{9,11},{10,... | collective-permute-start | bytes 122888 | tf_op jit(solution)/shard_map/ppermute | solution.py:36
  42.9 5.9 %collective-permute-start.15 = (f32[80,128]{1,0:T(8,128)S(1)}, f32[80,128]{1,0:T(8,128)S(1)}, u32[]{:S(2)}, u32[]{:S(2)}) collective-permute-start(f32[80,128]{1,0:T(8,128)S(1)} %sample_sums.7.refs_0_), channel_id=1, source_target_pairs={{0,3},{1,2},{2,1},{3,0},{4,7},{5,6},{6,5},{7,4},{8,11},{9,10},{10,... | collective-permute-start | bytes 122888 | tf_op jit(solution)/shard_map/ppermute | solution.py:36
  51.8 5.1 %collective-permute-start.24 = (f32[16,128]{1,0:T(8,128)S(1)}, f32[16,128]{1,0:T(8,128)S(1)}, u32[]{:S(2)}, u32[]{:S(2)}) collective-permute-start(f32[16,128]{1,0:T(8,128)S(1)} %get-tuple-element.93.refs_8_), channel_id=1, source_target_pairs={{0,2},{1,3},{2,0},{3,1},{4,6},{5,7},{6,4},{7,5},{8,10},{9,11},{10,... | collective-permute-start | bytes 24584 | tf_op jit(solution)/shard_map/ppermute | solution.py:36
  52.4 5.4 %collective-permute-start.23 = (f32[16,128]{1,0:T(8,128)S(1)}, f32[16,128]{1,0:T(8,128)S(1)}, u32[]{:S(2)}, u32[]{:S(2)}) collective-permute-start(f32[16,128]{1,0:T(8,128)S(1)} %get-tuple-element.93.refs_8_), channel_id=1, source_target_pairs={{0,3},{1,2},{2,1},{3,0},{4,7},{5,6},{6,5},{7,4},{8,11},{9,10},{10,... | collective-permute-start | bytes 24584 | tf_op jit(solution)/shard_map/ppermute | solution.py:36
  65.0 5.9 %collective-permute-start.28 = (f32[80,128]{1,0:T(8,128)S(1)}, f32[80,128]{1,0:T(8,128)S(1)}, u32[]{:S(2)}, u32[]{:S(2)}) collective-permute-start(f32[80,128]{1,0:T(8,128)S(1)} %sample_sums.8.refs_1_), channel_id=1, source_target_pairs={{0,2},{1,3},{2,0},{3,1},{4,6},{5,7},{6,4},{7,5},{8,10},{9,11},{10,... | collective-permute-start | bytes 122888 | tf_op jit(solution)/shard_map/ppermute | solution.py:36
  67.0 5.9 %collective-permute-start.27 = (f32[80,128]{1,0:T(8,128)S(1)}, f32[80,128]{1,0:T(8,128)S(1)}, u32[]{:S(2)}, u32[]{:S(2)}) collective-permute-start(f32[80,128]{1,0:T(8,128)S(1)} %sample_sums.8.refs_1_), channel_id=1, source_target_pairs={{0,3},{1,2},{2,1},{3,0},{4,7},{5,6},{6,5},{7,4},{8,11},{9,10},{10,... | collective-permute-start | bytes 122888 | tf_op jit(solution)/shard_map/ppermute | solution.py:36
  77.8 5.8 %collective-permute-start.35 = (f32[160,128]{1,0:T(8,128)S(1)}, f32[160,128]{1,0:T(8,128)S(1)}, u32[]{:S(2)}, u32[]{:S(2)}) collective-permute-start(f32[160,128]{1,0:T(8,128)S(1)} %add.69), channel_id=1, source_target_pairs={{0,8},{4,12},{8,0},{12,4},{16,24},{20,28},{24,16},{28,20},{1,9},{5... | collective-permute-start | bytes 245768 | tf_op jit(solution)/shard_map/ppermute | solution.py:36
  79.3 6.2 %collective-permute-start.34 = (f32[80,128]{1,0:T(8,128)S(1)}, f32[80,128]{1,0:T(8,128)S(1)}, u32[]{:S(2)}, u32[]{:S(2)}) collective-permute-start(f32[80,128]{1,0:T(8,128)S(1)} %sample_sums.9.refs_1_), channel_id=1, source_target_pairs={{0,2},{1,3},{2,0},{3,1},{4,6},{5,7},{6,4},{7,5},{8,10},{9,11},{10,... | collective-permute-start | bytes 122888 | tf_op jit(solution)/shard_map/ppermute | solution.py:36
  81.0 6.0 %collective-permute-start.33 = (f32[80,128]{1,0:T(8,128)S(1)}, f32[80,128]{1,0:T(8,128)S(1)}, u32[]{:S(2)}, u32[]{:S(2)}) collective-permute-start(f32[80,128]{1,0:T(8,128)S(1)} %sample_sums.9.refs_1_), channel_id=1, source_target_pairs={{0,3},{1,2},{2,1},{3,0},{4,7},{5,6},{6,5},{7,4},{8,11},{9,10},{10,... | collective-permute-start | bytes 122888 | tf_op jit(solution)/shard_map/ppermute | solution.py:36
  93.3 6.2 %collective-permute-start.40 = (f32[80,128]{1,0:T(8,128)S(1)}, f32[80,128]{1,0:T(8,128)S(1)}, u32[]{:S(2)}, u32[]{:S(2)}) collective-permute-start(f32[80,128]{1,0:T(8,128)S(1)} %sample_sums.10.refs_0_), channel_id=1, source_target_pairs={{0,2},{1,3},{2,0},{3,1},{4,6},{5,7},{6,4},{7,5},{8,10},{9,11},{10,... | collective-permute-start | bytes 122888 | tf_op jit(solution)/shard_map/ppermute | solution.py:36
  96.0 5.9 %collective-permute-start.39 = (f32[80,128]{1,0:T(8,128)S(1)}, f32[80,128]{1,0:T(8,128)S(1)}, u32[]{:S(2)}, u32[]{:S(2)}) collective-permute-start(f32[80,128]{1,0:T(8,128)S(1)} %sample_sums.10.refs_0_), channel_id=1, source_target_pairs={{0,3},{1,2},{2,1},{3,0},{4,7},{5,6},{6,5},{7,4},{8,11},{9,10},{10,... | collective-permute-start | bytes 122888 | tf_op jit(solution)/shard_map/ppermute | solution.py:36
  97.7 5.7 %collective-permute-start.42 = (f32[160,128]{1,0:T(8,128)S(1)}, f32[160,128]{1,0:T(8,128)S(1)}, u32[]{:S(2)}, u32[]{:S(2)}) collective-permute-start(f32[160,128]{1,0:T(8,128)S(1)} %add.72.refs_0_), channel_id=1, source_target_pairs={{0,16},{4,20},{8,24},{12,28},{16,0},{20,4},{24,8},{28,12},{1,17},{... | collective-permute-start | bytes 245768 | tf_op jit(solution)/shard_map/ppermute | solution.py:36
  104.6 5.4 %collective-permute-start.48 = (f32[16,128]{1,0:T(8,128)S(1)}, f32[16,128]{1,0:T(8,128)S(1)}, u32[]{:S(2)}, u32[]{:S(2)}) collective-permute-start(f32[16,128]{1,0:T(8,128)S(1)} %get-tuple-element.118.refs_8_), channel_id=1, source_target_pairs={{0,2},{1,3},{2,0},{3,1},{4,6},{5,7},{6,4},{7,5},{8,10},{9,11},{10,... | collective-permute-start | bytes 24584 | tf_op jit(solution)/shard_map/ppermute | solution.py:36
  105.6 5.4 %collective-permute-start.47 = (f32[16,128]{1,0:T(8,128)S(1)}, f32[16,128]{1,0:T(8,128)S(1)}, u32[]{:S(2)}, u32[]{:S(2)}) collective-permute-start(f32[16,128]{1,0:T(8,128)S(1)} %get-tuple-element.118.refs_8_), channel_id=1, source_target_pairs={{0,3},{1,2},{2,1},{3,0},{4,7},{5,6},{6,5},{7,4},{8,11},{9,10},{10,... | collective-permute-start | bytes 24584 | tf_op jit(solution)/shard_map/ppermute | solution.py:36
  117.7 6.2 %collective-permute-start.52 = (f32[80,128]{1,0:T(8,128)S(1)}, f32[80,128]{1,0:T(8,128)S(1)}, u32[]{:S(2)}, u32[]{:S(2)}) collective-permute-start(f32[80,128]{1,0:T(8,128)S(1)} %sample_sums.11.refs_1_), channel_id=1, source_target_pairs={{0,2},{1,3},{2,0},{3,1},{4,6},{5,7},{6,4},{7,5},{8,10},{9,11},{10,... | collective-permute-start | bytes 122888 | tf_op jit(solution)/shard_map/ppermute | solution.py:36
  120.2 5.9 %collective-permute-start.51 = (f32[80,128]{1,0:T(8,128)S(1)}, f32[80,128]{1,0:T(8,128)S(1)}, u32[]{:S(2)}, u32[]{:S(2)}) collective-permute-start(f32[80,128]{1,0:T(8,128)S(1)} %sample_sums.11.refs_1_), channel_id=1, source_target_pairs={{0,3},{1,2},{2,1},{3,0},{4,7},{5,6},{6,5},{7,4},{8,11},{9,10},{10,... | collective-permute-start | bytes 122888 | tf_op jit(solution)/shard_map/ppermute | solution.py:36
  (32 other events, 120.4 us)
